TPU v7x, 32 devices: a whole 2x2x4 slice. The times are simulated.
32 devices in a mesh: row: 4 (over x, core), col: 8 (over z, y).
Axes of the slice: x: 2, y: 2, z: 4, core: 2. Of those that a mesh axis runs over, the one named last changes fastest.
Arguments:
- tokens: bfloat16 [3584, 4096], P('col', 'row'), may hold values from -50 to 50
- ln_gain: float32 [4096], P('row'), may hold values from 0.1 to 1.9
- ln_shift: float32 [4096], P('row'), may hold values from -4 to 4
- w_qkv: bfloat16 [4096, 12288], P('row', 'col'), may hold values from -2 to 2
- w_out: bfloat16 [4096, 4096], P('col', 'row'), may hold values from -0.09375 to 0.09375
- layer_scale: float32 [4096], P('row'), may hold values from 0.5 to 2
- segments: int32 [3584], replicated, may hold values from 0 to 8, as said below
- present: int32 [3584], replicated, may hold values from 0 to 1, as said below
- coords: int32 [2, 3584], replicated, may hold values from 0 to 22, as said below
- owner_slot: int32 [3584], replicated, may hold values from 0 to 3583, as said below
Outputs:
- layer_out: bfloat16 [3584, 4096], P('col', 'row')
Inputs may be any that keep to these rules, and one draw needn't show every extreme that they name: `segments`: the picture of each token, pictures numbered in stream order; each picture's tokens form one run, pictures follow each other from position 0, and the padding tokens after them carry 8. `present`: 1 exactly where segments is below 8. A picture has h rows of w patches, 8 <= h <= 18 and 12 <= w <= 22, and some picture has 18 rows of 22; its first 5 tokens (class and registers) have 0 in both rows of coords, then its patches follow in row-major order with patch row and column counted from 1; padding tokens have 0 in both. `owner_slot`: A permutation of the 3584 tokens onto slots. Each block of 896 slots (slot // 896) holds 2 whole pictures, each on consecutive slots in stream order, followed by padding tokens.
All inputs are finite; a program needn't handle non-finite values.
Results may differ from a plain program's by a relative error of at most 0.017.
Values may be sent and summed in bfloat16 or wider, within the bound.
No kernel may reach another device: no remote copies, remote signals or barrier semaphores. Data moves between devices by JAX's collectives and lax.ppermute only.
A program may use at most 64 MiB of HBM per device.

v0:
```python
import functools

import jax
import jax.numpy as jnp
from jax import lax
from jax.experimental import pallas as pl
from jax.experimental.pallas import tpu as pltpu
from jax.sharding import PartitionSpec as P

D = 4096
HD = 128
BF = jnp.bfloat16
F32 = jnp.float32
LONGEST = 5 + 18 * 22
POSITIONS = 32
MIB = 1024 * 1024
STAT_ROWS = 16


def rotate(values, row_pos, col_pos):
    quarter = values.shape[-1] // 4
    frequency = 100.0 ** (-jnp.arange(quarter, dtype=jnp.float32) / quarter)
    angles = jnp.concatenate(
        [row_pos[:, None] * frequency[None, :], col_pos[:, None] * frequency[None, :]], axis=1
    )
    cosine = jnp.cos(angles)[:, None, :]
    sine_wave = jnp.sin(angles)[:, None, :]
    former = jnp.concatenate(
        [values[..., :quarter], values[..., 2 * quarter : 3 * quarter]], axis=-1
    )
    latter = jnp.concatenate(
        [values[..., quarter : 2 * quarter], values[..., 3 * quarter :]], axis=-1
    )
    new_former = former * cosine - latter * sine_wave
    new_latter = latter * cosine + former * sine_wave
    return jnp.concatenate(
        [
            new_former[..., :quarter],
            new_latter[..., :quarter],
            new_former[..., quarter:],
            new_latter[..., quarter:],
        ],
        axis=-1,
    )


def normalize(values, totals, squares, ln_gain, ln_shift):
    average = totals / D
    spread = squares / D - average * average
    scale_inv = lax.rsqrt(spread + 1e-06)
    return ((values - average[:, None]) * scale_inv[:, None] * ln_gain + ln_shift).astype(
        jnp.bfloat16
    )


def local_general(
    tokens, ln_gain, ln_shift, w_qkv, w_out, layer_scale, segments, present, coords, owner_slot
):
    own_rows = tokens.astype(jnp.float32)
    totals, squares = lax.psum(
        (jnp.sum(own_rows, axis=1), jnp.sum(own_rows * own_rows, axis=1)), "row"
    )
    normed = normalize(own_rows, totals, squares, ln_gain, ln_shift)
    gathered = lax.all_gather(normed, "col", axis=0, tiled=True)
    slot_count = owner_slot.shape[0]
    at_slot = (
        jnp.zeros((slot_count,), jnp.int32)
        .at[owner_slot]
        .set(jnp.arange(slot_count, dtype=jnp.int32))
    )
    placed = gathered[at_slot]
    group_rows = slot_count // lax.axis_size("row")
    mixed = lax.psum_scatter(
        jnp.dot(placed, w_qkv, preferred_element_type=jnp.float32).astype(jnp.bfloat16),
        "row",
        scatter_dimension=0,
        tiled=True,
    ).astype(jnp.float32)
    heads_here = w_qkv.shape[1] // (3 * HD)
    mixed = mixed.reshape(group_rows, heads_here, 3, HD)
    my_slots = lax.dynamic_slice_in_dim(at_slot, lax.axis_index("row") * group_rows, group_rows, 0)
    row_pos = coords[0][my_slots].astype(jnp.float32)
    col_pos = coords[1][my_slots].astype(jnp.float32)
    seg_rows = segments[my_slots]
    live_rows = present[my_slots]
    query_rows = rotate(mixed[:, :, 0], row_pos, col_pos).astype(jnp.bfloat16)
    key_rows = rotate(mixed[:, :, 1], row_pos, col_pos).astype(jnp.bfloat16)
    values = mixed[:, :, 2].astype(jnp.bfloat16)
    scores = jnp.einsum(
        "qhe,khe->hqk", query_rows, key_rows, preferred_element_type=jnp.float32
    ) * HD ** (-0.5)
    allowed = (seg_rows[:, None] == seg_rows[None, :]) & (live_rows[None, :] == 1)
    scores = jnp.where(allowed[None], scores, -1e30)
    highest = jnp.max(scores, axis=-1, keepdims=True)
    weights = jnp.exp(scores - highest)
    probability = (weights / jnp.sum(weights, axis=-1, keepdims=True)).astype(jnp.bfloat16)
    result = jnp.einsum("hqk,khe->qhe", probability, values, preferred_element_type=jnp.float32)
    attended = (result * live_rows[:, None, None].astype(jnp.float32)).astype(jnp.bfloat16)
    attended = attended.reshape(group_rows, heads_here * HD)
    all_slots = lax.all_gather(attended, "row", axis=0, tiled=True)
    projected = lax.psum_scatter(
        jnp.dot(all_slots[owner_slot], w_out, preferred_element_type=jnp.float32).astype(
            jnp.bfloat16
        ),
        "col",
        scatter_dimension=0,
        tiled=True,
    ).astype(jnp.float32)
    return (own_rows + layer_scale * projected).astype(jnp.bfloat16)


def whole(memory_space=pltpu.VMEM):
    return pl.BlockSpec(memory_space=memory_space)


def pack_kernel(sums, out):
    average = sums[0:1, :] / D
    spread = sums[1:2, :] / D - average * average
    rows = []
    for value in (average, lax.rsqrt(spread + 1e-06)):
        for _ in range(3):
            part = value.astype(BF).astype(F32)
            rows.append(part)
            value = value - part
    rows.append(jnp.zeros((STAT_ROWS - len(rows), out.shape[1]), F32))
    out[...] = jnp.concatenate(rows, axis=0).astype(BF)


def pack(sums, width):
    return pl.pallas_call(
        pack_kernel,
        out_shape=jax.ShapeDtypeStruct((STAT_ROWS, width), BF),
        in_specs=[whole()],
        out_specs=whole(),
        compiler_params=pltpu.CompilerParams(vmem_limit_bytes=16 * MIB),
        name="pack",
    )(jnp.pad(sums, ((0, 0), (0, width - sums.shape[1]))))


def norm_kernel(tokens, stats, gain, shift, out):
    block = tokens.shape[0]
    lanes = -(-block // 128) * 128
    columns = jnp.transpose(stats[:, :lanes].astype(F32))[:block]
    average = columns[:, 0:1] + columns[:, 1:2] + columns[:, 2:3]
    scale_inv = columns[:, 3:4] + columns[:, 4:5] + columns[:, 5:6]
    for left in range(0, tokens.shape[1], 256):
        piece = slice(left, left + 256)
        normed = (tokens[:, piece].astype(F32) - average) * scale_inv
        out[:, piece] = (normed * gain[:, piece] + shift[:, piece]).astype(BF)


def norm(tokens, stats, gain, shift):
    rows, width = tokens.shape
    return pl.pallas_call(
        norm_kernel,
        out_shape=jax.ShapeDtypeStruct(tokens.shape, BF),
        in_specs=[whole()] * 4,
        out_specs=whole(),
        compiler_params=pltpu.CompilerParams(vmem_limit_bytes=16 * MIB),
        cost_estimate=pl.CostEstimate(
            flops=4 * rows * width, bytes_accessed=4 * rows * width, transcendentals=0
        ),
        name="norm",
    )(tokens, stats, gain[None, :], shift[None, :])


def qkv_kernel(count, heads, w_own, w_peer, *refs):
    owns, peers, (keep, send) = refs[:count], refs[count : 2 * count], refs[2 * count :]
    width = keep.shape[1]
    first = 0
    for own, peer in zip(owns, peers):
        rows = own.shape[0]
        for k, target in ((1, send), (0, keep)):
            chosen = pl.ds(pl.multiple_of(heads[k] * width, HD), width)
            total = jnp.dot(own[...], w_own[:, chosen], preferred_element_type=F32)
            total += jnp.dot(
                peer[...], w_peer[:, k * width : (k + 1) * width], preferred_element_type=F32
            )
            target[first : first + rows, :] = total.astype(BF)
        first += rows


def qkv(owns, peers, heads, w_own, w_peer):
    rows = sum(own.shape[0] for own in owns)
    depth, columns = w_peer.shape
    out = jax.ShapeDtypeStruct((rows, columns // 2), BF)
    return pl.pallas_call(
        functools.partial(qkv_kernel, len(owns)),
        out_shape=(out, out),
        in_specs=[whole(pltpu.SMEM)] + [whole()] * (2 + 2 * len(owns)),
        out_specs=(whole(), whole()),
        compiler_params=pltpu.CompilerParams(vmem_limit_bytes=32 * MIB),
        cost_estimate=pl.CostEstimate(
            flops=4 * rows * depth * columns,
            bytes_accessed=4 * rows * depth + 4 * depth * columns + 2 * rows * columns,
            transcendentals=0,
        ),
        name="qkv",
    )(heads, w_own, w_peer, *owns, *peers)


def turn_kernel(group, block, starts, kept, received, table, *refs):
    out, turned, angles, load_sems, store_sems = refs[-5:]
    count = kept.shape[0] // block

    def place(k):
        return pl.ds(pl.multiple_of(starts[group + k], 16), block)

    def local(k):
        return pl.ds(k * block, block)

    def load(k):
        return pltpu.make_async_copy(table.at[place(k), :], angles.at[local(k), :], load_sems.at[k])

    def store(k):
        return pltpu.make_async_copy(turned.at[local(k), :], out.at[place(k), :], store_sems.at[k])

    for k in range(count):
        load(k).start()
    lane = lax.broadcasted_iota(jnp.int32, (block, HD), 1)
    first_half = (lane % 64) < 32
    for k in range(count):
        rows = slice(k * block, (k + 1) * block)

        def mixed(part):
            cols = slice(part * HD, (part + 1) * HD)
            terms = (ref[rows, cols].astype(F32) for ref in (kept, received))
            return sum(terms)

        turned[rows, 2 * HD :] = mixed(2).astype(BF)
        load(k).wait()
        for part in range(2):
            cols = slice(part * HD, (part + 1) * HD)
            both = mixed(part)
            swapped = jnp.where(first_half, pltpu.roll(both, HD - 32, 1), pltpu.roll(both, 32, 1))
            turned[rows, cols] = (both * angles[rows, :HD] + swapped * angles[rows, HD:]).astype(BF)
        store(k).start()
    for k in range(count):
        store(k).wait()


def turn(group, block, starts, kept, received, table, so_far):
    rows, columns = kept.shape
    operands = [starts, kept, received, table] + ([] if so_far is None else [so_far])
    return pl.pallas_call(
        functools.partial(turn_kernel, group, block),
        out_shape=jax.ShapeDtypeStruct((table.shape[0], columns), BF),
        in_specs=[whole(pltpu.SMEM)] + [whole()] * 2 + [whole(pl.ANY)] * (len(operands) - 3),
        out_specs=whole(pl.ANY),
        input_output_aliases={} if so_far is None else {4: 0},
        scratch_shapes=[
            pltpu.VMEM((rows, columns), BF),
            pltpu.VMEM((rows, 2 * HD), F32),
            pltpu.SemaphoreType.DMA((rows // block,)),
            pltpu.SemaphoreType.DMA((rows // block,)),
        ],
        compiler_params=pltpu.CompilerParams(vmem_limit_bytes=16 * MIB),
        cost_estimate=pl.CostEstimate(
            flops=8 * rows * HD, bytes_accessed=26 * rows * HD, transcendentals=0
        ),
        name="turn",
    )(*operands)


def attend_kernel(tile, windows, group, places, lows, sizes, seg_tiles, seg_row, rows, *refs):
    outs, (turned, result, sem) = refs[:-3], refs[-3:]
    load = pltpu.make_async_copy(rows, turned, sem)
    load.start()
    load.wait()
    scale = HD ** (-0.5) * 1.4426950408889634

    def step(j, carry):
        i = places[group + j]
        at = pl.ds(pl.multiple_of(i * tile, 16), tile)
        to = pl.ds(pl.multiple_of(j * tile, 16), tile)

        def look(window):
            near = pl.ds(pl.multiple_of(lows[i], 128), window)
            scores = (
                lax.dot_general(
                    turned[at, :HD],
                    turned[near, HD : 2 * HD],
                    (((1,), (1,)), ((), ())),
                    preferred_element_type=F32,
                )
                * scale
            )
            lanes = jnp.broadcast_to(seg_tiles[pl.ds(i, 1), :], (8, tile))
            marks = jnp.transpose(lanes)[:, 0:1]
            scores = jnp.where(marks == seg_row[0:1, near], scores, -1e30)
            highest = jnp.max(scores, axis=1, keepdims=True)
            weights = jnp.exp2(scores - highest)
            total = jnp.sum(weights, axis=1, keepdims=True)
            sums = jnp.dot(weights.astype(BF), turned[near, 2 * HD :], preferred_element_type=F32)
            live = jnp.where(marks >= 0, 1.0 / total, 0.0)
            result[to, :] = (sums * live).astype(BF)

        for kind, window in enumerate(windows):
            pl.when(sizes[i] == kind)(functools.partial(look, window))
        return carry

    lax.fori_loop(0, result.shape[0] // tile, step, 0)
    block = outs[0].shape[0]
    for n, out in enumerate(outs):
        out[...] = result[n * block : (n + 1) * block, :]


def attend(group, outs, places, lows, sizes, seg_tiles, seg_row, rows, block, tile, windows):
    total = rows.shape[0]
    return pl.pallas_call(
        functools.partial(attend_kernel, tile, windows, group),
        out_shape=[jax.ShapeDtypeStruct((block, HD), BF)] * outs,
        in_specs=[whole(pltpu.SMEM)] * 3 + [whole()] * 2 + [whole(pl.ANY)],
        out_specs=[whole()] * outs,
        scratch_shapes=[
            pltpu.VMEM((total, 3 * HD), BF),
            pltpu.VMEM((outs * block, HD), BF),
            pltpu.SemaphoreType.DMA,
        ],
        compiler_params=pltpu.CompilerParams(vmem_limit_bytes=32 * MIB),
        cost_estimate=pl.CostEstimate(
            flops=4 * outs * block * windows[-1] * HD,
            bytes_accessed=total * HD * 26,
            transcendentals=outs * block * windows[-1],
        ),
        name="attend",
    )(places, lows, sizes, seg_tiles, seg_row, rows)


def project_kernel(pieces, blocks, first, before, slots, *refs):
    weights, parts, rest = refs[:pieces], refs[pieces : pieces + 4], refs[pieces + 4 :]
    earlier, (out, all_weights, rows, weight_sems, sems) = rest[:-5], rest[-5:]
    depth = all_weights.shape[0] // blocks
    copies = []
    top = 0
    for m in range(pieces):
        size = weights[m].shape[0]
        copies.append(
            pltpu.make_async_copy(
                weights[m], all_weights.at[top : top + size, :], weight_sems.at[m]
            )
        )
        top += size
    for m in range(blocks):
        for j in range(4):
            start = pl.multiple_of(m * depth + slots[j] * HD, HD)
            left = (first + m) * HD
            copies.append(
                pltpu.make_async_copy(
                    parts[j].at[:, left : left + HD], rows.at[:, pl.ds(start, HD)], sems.at[4 * m + j]
                )
            )
    for copy in copies:
        copy.start()
    for copy in copies:
        copy.wait()
    for start in range(0, out.shape[1], 256):
        end = min(start + 256, out.shape[1])
        total = jnp.dot(rows[...], all_weights[:, start:end], preferred_element_type=F32)
        if earlier:
            total += earlier[0][:, before + start : before + end]
        out[:, start:end] = total.astype(out.dtype)


def project(slots, first, weights, parts, earlier, kind, left=0):
    pieces = len(weights)
    width = weights[0].shape[1]
    depth = sum(piece.shape[0] for piece in weights)
    blocks = depth // (4 * HD)
    count = parts[0].shape[0]
    more = [] if earlier is None else [earlier]
    return pl.pallas_call(
        functools.partial(project_kernel, pieces, blocks, first, left),
        out_shape=jax.ShapeDtypeStruct((count, width), kind),
        in_specs=[whole(pltpu.SMEM)]
        + [whole(pl.ANY)] * (pieces + 4)
        + [whole()] * len(more),
        out_specs=whole(),
        scratch_shapes=[
            pltpu.VMEM((depth, width), BF),
            pltpu.VMEM((count, depth), BF),
            pltpu.SemaphoreType.DMA((pieces,)),
            pltpu.SemaphoreType.DMA((4 * blocks,)),
        ],
        compiler_params=pltpu.CompilerParams(vmem_limit_bytes=32 * MIB),
        cost_estimate=pl.CostEstimate(
            flops=2 * count * depth * width,
            bytes_accessed=2 * (depth * (width + count) + 2 * count * width),
            transcendentals=0,
        ),
        name="project",
    )(slots, *weights, *parts, *more)


def local_heads(
    tokens, ln_gain, ln_shift, w_qkv, w_out, layer_scale, segments, present, coords, owner_slot
):
    rows = lax.axis_size("row")
    cols = lax.axis_size("col")
    count = segments.shape[0]
    block = tokens.shape[0]
    row = lax.axis_index("row")
    col = lax.axis_index("col")
    core, x_index = row % 2, row // 2
    head = 2 * core + x_index

    lines = cols // 2
    ring = list(range(0, lines, 2)) + list(range(lines - 1 - lines % 2, 0, -2))
    after = {z: ring[(i + 1) % lines] for i, z in enumerate(ring)}
    back = {b: a for a, b in after.items()}
    y_swap = [(c, c ^ 1) for c in range(cols)]
    z_next = [(2 * z + y, 2 * after[z] + y) for z in range(lines) for y in range(2)]
    core_swap = [(r, r ^ 1) for r in range(rows)]
    x_swap = [(r, r ^ 2) for r in range(rows)]

    def by_y(value):
        return lax.ppermute(value, "col", y_swap)

    def by_z(value):
        return lax.ppermute(value, "col", z_next)

    def by_core(value):
        return lax.ppermute(value, "row", core_swap)

    def by_x(value):
        return lax.ppermute(value, "row", x_swap)

    def hold(*values):
        return lax.optimization_barrier(values)

    def along(step, z, times):
        for _ in range(times):
            z = step[z]
        return z

    def per_col(value_of):
        return jnp.asarray([value_of(c // 2, c % 2) for c in range(cols)], jnp.int32)[col]

    def origins(z, y):
        at = [(0, 0), (1, 0), (0, 1)]
        at += [(k, u) for i in range(2, lines + 1) for k, u in ((i - 1, 1), (i, 0))][:-1]
        return [(2 * along(back, z, i) + (y ^ u)) * block for i, u in at]

    starts = per_col(origins)

    z_new, y_new = by_z(tokens), by_y(tokens)
    own_rows = tokens.astype(F32)
    sums = lax.psum(
        jnp.stack([jnp.sum(own_rows, axis=1), jnp.sum(own_rows * own_rows, axis=1)]), "row"
    )
    own_stats = pack(sums, tokens.shape[1])
    z_stats, y_stats = by_z(own_stats), by_y(own_stats)

    heads = jnp.stack([head, head ^ 1, head ^ 2, head ^ 3]).astype(jnp.int32)
    width = 3 * HD

    def head_columns(which):
        return lax.dynamic_slice_in_dim(w_qkv, which * width, width, 1)

    w_sent = jnp.concatenate([head_columns(head ^ 2), head_columns(head ^ 3)], axis=1)
    own_normed = norm(tokens, own_stats, ln_gain, ln_shift)
    z_new, y_new, z_stats, y_stats, w_sent, own_normed, segments, present, coords = hold(
        z_new, y_new, z_stats, y_stats, w_sent, own_normed, segments, present, coords
    )
    w_peer = by_core(w_sent)
    z_new = norm(z_new, z_stats, ln_gain, ln_shift)

    w_ring = [w_out]
    rows_turned = None

    def product(*blocks):
        return qkv(blocks, [by_core(own) for own in blocks], heads, w_qkv, w_peer)

    def turn_all(entries):
        nonlocal rows_turned
        for first, kept, received in entries:
            rows_turned = turn(first, block, starts, kept, received, table, rows_turned)

    quarter = HD // 4
    frequency = 100.0 ** (-jnp.arange(quarter, dtype=F32) / quarter)
    angles = jnp.arange(POSITIONS, dtype=F32)[:, None] * frequency[None, :]
    cosine, sine = jnp.cos(angles), jnp.sin(angles)
    none = jnp.zeros((POSITIONS, 2 * quarter), F32)
    cos_pair = jnp.concatenate([cosine, cosine], axis=1)
    sin_pair = jnp.concatenate([-sine, sine], axis=1)
    turns = jnp.concatenate(
        [
            jnp.concatenate([cos_pair, none, sin_pair, none], axis=1),
            jnp.concatenate([none, cos_pair, none, sin_pair], axis=1),
        ],
        axis=0,
    )
    spots = jnp.arange(POSITIONS, dtype=jnp.int32)
    chosen = jnp.concatenate(
        [coords[0][:, None] == spots[None, :], coords[1][:, None] == spots[None, :]], axis=1
    )
    table = jnp.dot(
        chosen.astype(F32),
        turns,
        precision=lax.Precision.HIGHEST,
        preferred_element_type=F32,
    )

    tile = block // 2
    most = -(-(127 + 2 * (LONGEST - 1) + tile) // 128) * 128
    windows = tuple(sorted({min(count, w) for w in (512, 640, 896, most)}))
    tiles = count // tile
    marks = jnp.where(present == 1, segments, -1).astype(F32)
    heads_of = segments.reshape(tiles, tile)
    real = jnp.sum(present)
    begin = jnp.sum((segments[None, :] < heads_of[:, :1]).astype(jnp.int32), axis=1)
    end = jnp.sum((segments[None, :] <= heads_of[:, -1:]).astype(jnp.int32), axis=1)
    begin = jnp.minimum(begin, real) // 128 * 128
    need = jnp.minimum(end, real) - begin
    sizes = sum((need > w).astype(jnp.int32) for w in windows[:-1])
    spans = sum(jnp.where(sizes == k, w, 0) for k, w in enumerate(windows))
    lows = jnp.minimum(begin, count - spans).astype(jnp.int32)
    seg_tiles, seg_row = marks.reshape(tiles, tile), marks[None, :]

    early = [norm(y_new, y_stats, ln_gain, ln_shift)]
    early.append(by_core(early[0]))
    y_new, ahead = by_y(z_new), by_z(z_new)
    kept, send = product(own_normed)
    received = by_x(send)
    late = product(z_new)
    extra = (table, seg_tiles, seg_row, lows, sizes)
    flat, tree = jax.tree.flatten((y_new, ahead, kept, received, early, late, extra))
    y_new, z_new, kept, received, early, late, extra = jax.tree.unflatten(tree, hold(*flat))
    table, seg_tiles, seg_row, lows, sizes = extra
    exchanged, pending = [(0, kept, received)], [(1, *late)]

    for i in range(2, lines):
        last = i == lines - 1
        y_hand, z_hand = y_new, z_new
        y_new = by_y(z_hand)
        ahead = by_z(w_ring[-1] if last else z_hand)
        entries = [(first, kept, by_x(send)) for first, kept, send in pending]
        if early:
            kept, send = qkv(early[:1], early[1:], heads, w_qkv, w_peer)
            entries.append((2, kept, by_x(send)))
            early = []
        kept, send = product(z_hand)
        pending = [(2 * i - 1, *product(y_hand))]
        if last:
            entries.append((2 * i, kept, by_x(send)))
        else:
            pending.append((2 * i, kept, send))
        turn_all(exchanged)
        arrays = [(kept, received) for _, kept, received in entries]
        later = [(kept, send) for _, kept, send in pending]
        flat, tree = jax.tree.flatten((ahead, y_new, arrays, rows_turned, later))
        held = jax.tree.unflatten(tree, hold(*flat))
        ahead, y_new, arrays, rows_turned, later = held
        exchanged = [(entry[0], *pair) for entry, pair in zip(entries, arrays)]
        pending = [(entry[0], *pair) for entry, pair in zip(pending, later)]
        if last:
            w_ring.append(ahead)
        else:
            z_new = ahead

    w_ring.append(by_z(w_ring[-1]))
    kept, send = product(y_new)
    pending.append((2 * lines - 1, kept, send))
    turn_all(exchanged)
    turn_all([(first, kept, by_x(send)) for first, kept, send in pending])
    ringed = [
        [(2 * z + y, 2 * along(after, z, i) + y) for z in range(lines) for y in range(2)]
        for i in range(lines)
    ]
    each = block // tile
    places = per_col(
        lambda z, y: [
            (2 * along(after, z, i) + u) * each + part
            for u in (1 - y, y)
            for i in range(lines)
            for part in range(each)
        ]
    )

    def attended(group):
        return attend(
            group * each, lines, places, lows, sizes, seg_tiles, seg_row, rows_turned, block, tile, windows
        )

    def ring_out(outs):
        return [outs[0]] + [lax.ppermute(outs[i], "col", ringed[i]) for i in range(1, lines)]

    def cross(group):
        return group, by_x(group), by_core(group)

    *other_outs, w_ring[-1] = hold(*attended(0), w_ring[-1])
    other_outs = ring_out(other_outs)
    own_outs = attended(lines)
    *both, w_last = hold(*other_outs, *own_outs, w_ring[-1])
    left = w_out.shape[1] * 4 // 8
    w_left = by_z(w_last[:, :left])
    others = cross(jnp.concatenate(both[:lines], axis=1))
    *both, w_left, w_last = hold(*others, *both[lines:], w_left, w_last)
    others, own_outs = both[:3], ring_out(both[3:])
    w_right = by_z(w_last[:, left:])
    others = [*others, by_core(others[1])]
    other = project(heads, 0, w_ring, others, None, F32)
    crossed = by_y(project(heads, lines - 1, [w_left], others, other, BF))
    owns = cross(jnp.concatenate(own_outs, axis=1))
    crossed, w_right = hold(crossed, w_right)
    crossed_right = by_y(project(heads, lines - 1, [w_right], others, other, BF, left))
    owns = [*owns, by_core(owns[1])]
    own = project(heads, 0, w_ring, owns, None, F32)
    own_left = project(heads, lines - 1, [w_left], owns, own, F32)
    own_right = project(heads, lines - 1, [w_right], owns, own, F32, left)
    projected = jnp.concatenate(
        [own_left + crossed.astype(F32), own_right + crossed_right.astype(F32)], axis=1
    )
    return (own_rows + layer_scale * projected).astype(BF)


def solution(mesh):
    in_specs = (
        P("col", "row"),
        P("row"),
        P("row"),
        P("row", "col"),
        P("col", "row"),
        P("row"),
        P(),
        P(),
        P(),
        P(),
    )
    out_specs = P("col", "row")
    rows, cols = mesh.shape["row"], mesh.shape["col"]

    def local(*args):
        heads_here = args[3].shape[1] // (3 * HD)
        if rows == 4 and heads_here == 4 and cols % 4 == 0 and cols > 4 and args[0].shape[0] % 32 == 0:
            return local_heads(*args)
        return local_general(*args)

    return jax.shard_map(local, mesh=mesh, in_specs=in_specs, out_specs=out_specs, check_vma=False)
```

profile of v0, /device:TPU:0, one launch (start us, length us, event | category | flops | bytes accessed | tf_op | source)
XLA Modules:
  0.0 201.5 jit_solution(13200626390146413765)
XLA Ops:
  0.0 4.0 %collective-permute-start = (bf16[448,1024]{1,0:T(8,128)(2,1)}, bf16[448,1024]{1,0:T(8,128)(2,1)S(1)}, u32[]{:S(2)}, u32[]{:S(2)}) collective-permute-start(bf16[448,1024]{1,0:T(8,128)(2,1)} %tokens.1), channel_id=1, source_target_pairs={{0,4},{1,5},{2,0},{3,1},{4,6},{5,7},{6,2},{7,3},{8,12},{9,13},{10,... | collective-permute-start | bytes 2752520 | tf_op jit(solution)/shard_map/ppermute | solution.py:420
  4.0 1.5 collective-permute-start.1
  5.6 1.6 convert_reduce_fusion
  7.1 6.3 %psum.7 = f32[2,448]{1,0:T(2,128)S(1)} all-reduce(f32[2,448]{1,0:T(2,128)S(1)} %pad_maximum_fusion.1), channel_id=1, replica_groups=mesh['row'=4,'col'=8] {'row'}, use_global_device_ids=true, to_apply=%region_2.3 | all-reduce | flops 896 | bytes 7168 | tf_op jit(solution)/shard_map/psum | solution.py:448
  13.5 1.6 collective-permute-start.2
  15.7 1.5 constant_dynamic-slice_fusion.2
  17.3 1.3 pad_maximum_fusion
  20.4 4.1 %collective-permute-done.2.stats = bf16[16,1024]{1,0:T(8,128)(2,1)S(1)} collective-permute-done((bf16[16,1024]{1,0:T(8,128)(2,1)S(1)}, bf16[16,1024]{1,0:T(8,128)(2,1)S(1)}, u32[]{:S(2)}, u32[]{:S(2)}) %collective-permute-start.2) | collective-permute-done | bytes 32800 | tf_op jit(solution)/shard_map/ppermute | solution.py:420
  24.6 2.2 %collective-permute-done.3.stats = bf16[16,1024]{1,0:T(8,128)(2,1)S(1)} collective-permute-done((bf16[16,1024]{1,0:T(8,128)(2,1)S(1)}, bf16[16,1024]{1,0:T(8,128)(2,1)S(1)}, u32[]{:S(2)}, u32[]{:S(2)}) %collective-permute-start.3) | collective-permute-done | bytes 32800 | tf_op jit(solution)/shard_map/ppermute | solution.py:417
  29.9 1.5 norm.4.refs_0_
  32.0 1.5 collective-permute-start.4
  33.5 1.6 collective-permute-start.5
  36.8 1.7 norm.5.refs_0_
  39.9 3.5 %qkv.8 = (bf16[448,384]{1,0:T(8,128)(2,1)S(1)}, bf16[448,384]{1,0:T(8,128)(2,1)}) custom-call(s32[4]{0:T(128)S(1)} %pad_add_fusion.heads.slots, bf16[1024,1536]{1,0:T(8,128)(2,1)S(1)} %copy-done.1, bf16[1024,768]{1,0:T(8,128)(2,1)} %collective-permute-done.6.w_peer, bf16[448,1024]{1,0:T(8,128)(2,1)S(1)} %copy-done.6, ...), custom_call_target="tpu_custom_call" | custom-call | flops 1409286144 | bytes 5668864 | tf_op jit(solution)/shard_map/qkv/pallas_call | solution.py:187
  44.1 1.5 collective-permute-start.8
  46.4 3.4 %fusion.2.table = f32[3584,256]{1,0:T(8,128)} fusion(pred[3584,32]{0,1:T(32,128)(4,1)S(1)} %get-tuple-element.208, pred[3584,32]{0,1:T(32,128)(4,1)S(1)} %get-tuple-element.209, f32[32,256]{1,0:T(8,128)S(1)} %concatenate.31, f32[32,256]{1,0:T(8,128)S(1)} %concatenate.30), kind=kOutput, calls=%fused_computation.9 | convolution fusion | flops 704888832 | bytes 3964928 | tf_op jit(solution)/shard_map/dot_general | solution.py:497
  49.8 4.0 %qkv.9 = (bf16[448,384]{1,0:T(8,128)(2,1)S(1)}, bf16[448,384]{1,0:T(8,128)(2,1)S(1)}) custom-call(s32[4]{0:T(128)S(1)} %pad_add_fusion.heads.slots, bf16[1024,1536]{1,0:T(8,128)(2,1)S(1)} %copy-done.1, bf16[1024,768]{1,0:T(8,128)(2,1)} %collective-permute-done.6.w_peer, bf16[448,1024]{1,0:T(8,128)(2,1)} %norm.4.refs_0_, ...), custom_call_target="tpu_custom_call" | custom-call | flops 1409286144 | bytes 5668864 | tf_op jit(solution)/shard_map/qkv/pallas_call | solution.py:187
  54.5 1.2 collective-permute-done.5.refs_0_
  56.3 2.5 %collective-permute-start.12 = (bf16[448,1024]{1,0:T(8,128)(2,1)}, bf16[448,1024]{1,0:T(8,128)(2,1)}, u32[]{:S(2)}, u32[]{:S(2)}) collective-permute-start(bf16[448,1024]{1,0:T(8,128)(2,1)} %collective-permute-done.5.refs_0_), channel_id=1, source_target_pairs={{0,4},{1,5},{2,0},{3,1},{4,6},{5,7},{6,2},{7,3},{8,12},{9,13},{10,... | collective-permute-start | bytes 2752520 | tf_op jit(solution)/shard_map/ppermute | solution.py:420
  59.3 4.1 %qkv.10 = (bf16[448,384]{1,0:T(8,128)(2,1)S(1)}, bf16[448,384]{1,0:T(8,128)(2,1)S(1)}) custom-call(s32[4]{0:T(128)S(1)} %pad_add_fusion.heads.slots, bf16[1024,1536]{1,0:T(8,128)(2,1)S(1)} %copy-done.1, bf16[1024,768]{1,0:T(8,128)(2,1)} %collective-permute-done.6.w_peer, bf16[448,1024]{1,0:T(8,128)(2,1)} %norm.5.refs_0_, ...), custom_call_target="tpu_custom_call" | custom-call | flops 1409286144 | bytes 5668864 | tf_op jit(solution)/shard_map/qkv/pallas_call | solution.py:187
  63.4 1.6 collective-permute-start.15
  66.2 1.8 turn.8.refs_0_
  68.0 4.0 %qkv.12 = (bf16[448,384]{1,0:T(8,128)(2,1)S(1)}, bf16[448,384]{1,0:T(8,128)(2,1)S(1)}) custom-call(s32[4]{0:T(128)S(1)} %pad_add_fusion.heads.slots, bf16[1024,1536]{1,0:T(8,128)(2,1)S(1)} %copy-done.1, bf16[1024,768]{1,0:T(8,128)(2,1)} %collective-permute-done.6.w_peer, bf16[448,1024]{1,0:T(8,128)(2,1)} %collective-permute-done.5.refs_0_, ...), custom_call_target="tpu_custom_call" | custom-call | flops 1409286144 | bytes 5668864 | tf_op jit(solution)/shard_map/qkv/pallas_call | solution.py:187
  72.0 4.1 %qkv.11 = (bf16[448,384]{1,0:T(8,128)(2,1)S(1)}, bf16[448,384]{1,0:T(8,128)(2,1)S(1)}) custom-call(s32[4]{0:T(128)S(1)} %pad_add_fusion.heads.slots, bf16[1024,1536]{1,0:T(8,128)(2,1)S(1)} %copy-done.1, bf16[1024,768]{1,0:T(8,128)(2,1)} %collective-permute-done.6.w_peer, bf16[448,1024]{1,0:T(8,128)(2,1)} %collective-permute-done.4.refs_0_, ...), custom_call_target="tpu_custom_call" | custom-call | flops 1409286144 | bytes 5668864 | tf_op jit(solution)/shard_map/qkv/pallas_call | solution.py:187
  76.1 4.2 %collective-permute-done.14.received = bf16[448,384]{1,0:T(8,128)(2,1)S(1)} collective-permute-done((bf16[448,384]{1,0:T(8,128)(2,1)S(1)}, bf16[448,384]{1,0:T(8,128)(2,1)S(1)}, u32[]{:S(2)}, u32[]{:S(2)}) %collective-permute-start.14) | collective-permute-done | bytes 344096 | tf_op jit(solution)/shard_map/ppermute | solution.py:426
  83.3 1.5 collective-permute-start.19
  85.3 3.7 %qkv.13 = (bf16[448,384]{1,0:T(8,128)(2,1)S(1)}, bf16[448,384]{1,0:T(8,128)(2,1)S(1)}) custom-call(s32[4]{0:T(128)S(1)} %pad_add_fusion.heads.slots, bf16[1024,1536]{1,0:T(8,128)(2,1)S(1)} %copy-done.1, bf16[1024,768]{1,0:T(8,128)(2,1)} %collective-permute-done.6.w_peer, bf16[448,1024]{1,0:T(8,128)(2,1)} %collective-permute-done.12.refs_0_, ...), custom_call_target="tpu_custom_call" | custom-call | flops 1409286144 | bytes 5668864 | tf_op jit(solution)/shard_map/qkv/pallas_call | solution.py:187
  89.0 1.6 collective-permute-start.22
  90.6 1.3 turn.9.refs_0_
  91.9 1.3 turn.10.refs_0_
  93.2 3.7 %qkv.14 = (bf16[448,384]{1,0:T(8,128)(2,1)S(1)}, bf16[448,384]{1,0:T(8,128)(2,1)S(1)}) custom-call(s32[4]{0:T(128)S(1)} %pad_add_fusion.heads.slots, bf16[1024,1536]{1,0:T(8,128)(2,1)S(1)} %copy-done.1, bf16[1024,768]{1,0:T(8,128)(2,1)} %collective-permute-done.6.w_peer, bf16[448,1024]{1,0:T(8,128)(2,1)} %collective-permute-done.13.refs_0_, ...), custom_call_target="tpu_custom_call" | custom-call | flops 1409286144 | bytes 5668864 | tf_op jit(solution)/shard_map/qkv/pallas_call | solution.py:187
  97.0 9.7 %collective-permute-done.11.refs_1_ = bf16[512,1024]{1,0:T(8,128)(2,1)S(1)} collective-permute-done((bf16[512,1024]{1,0:T(8,128)(2,1)S(1)}, bf16[512,1024]{1,0:T(8,128)(2,1)S(1)}, u32[]{:S(2)}, u32[]{:S(2)}) %collective-permute-start.11) | collective-permute-done | bytes 1048608 | tf_op jit(solution)/shard_map/ppermute | solution.py:420
  107.4 1.7 collective-permute-start.27
  109.1 1.5 collective-permute-start.26
  110.6 3.5 %qkv.15 = (bf16[448,384]{1,0:T(8,128)(2,1)S(1)}, bf16[448,384]{1,0:T(8,128)(2,1)S(1)}) custom-call(s32[4]{0:T(128)S(1)} %pad_add_fusion.heads.slots, bf16[1024,1536]{1,0:T(8,128)(2,1)S(1)} %copy-done.1, bf16[1024,768]{1,0:T(8,128)(2,1)} %collective-permute-done.6.w_peer, bf16[448,1024]{1,0:T(8,128)(2,1)S(1)} %collective-permute-done.18.refs_0_, ...), custom_call_target="tpu_custom_call" | custom-call | flops 1409286144 | bytes 5668864 | tf_op jit(solution)/shard_map/qkv/pallas_call | solution.py:187
  115.6 1.3 turn.11.refs_0_
  116.9 1.3 turn.12.refs_0_
  118.2 1.3 turn.13.refs_0_
  120.0 1.3 turn.14.refs_0_
  121.3 5.0 %collective-permute-done.25.received = bf16[448,384]{1,0:T(8,128)(2,1)S(1)} collective-permute-done((bf16[448,384]{1,0:T(8,128)(2,1)S(1)}, bf16[448,384]{1,0:T(8,128)(2,1)S(1)}, u32[]{:S(2)}, u32[]{:S(2)}) %collective-permute-start.25) | collective-permute-done | bytes 344096 | tf_op jit(solution)/shard_map/ppermute | solution.py:426
  126.4 1.3 turn.15.rows
  127.7 5.7 %attend.2 = (bf16[448,128]{1,0:T(8,128)(2,1)S(1)}, bf16[448,128]{1,0:T(8,128)(2,1)S(1)}, bf16[448,128]{1,0:T(8,128)(2,1)S(1)}, bf16[448,128]{1,0:T(8,128)(2,1)S(1)}) custom-call(s32[16]{0:T(128)S(1)} %fusion.12.places, s32[16]{0:T(128)S(1)} %get-tuple-element.111.lows, s32[16]{0:T(128)S(1)} %get-tuple-element.112.sizes, f32[16,224]{1,0:T(8,128)S(1)} %reshape.16.seg_tiles, ...), custom_call_target="tpu_custom_call" | custom-call | flops 1056964608 | bytes 11927552 | tf_op jit(solution)/shard_map/attend/pallas_call | solution.py:310
  133.4 1.9 collective-permute-start.28
  135.3 2.1 %collective-permute-start.29 = (bf16[448,128]{1,0:T(8,128)(2,1)S(1)}, bf16[448,128]{1,0:T(8,128)(2,1)S(1)}, u32[]{:S(2)}, u32[]{:S(2)}) collective-permute-start(bf16[448,128]{1,0:T(8,128)(2,1)S(1)} %get-tuple-element.164), channel_id=1, source_target_pairs={{0,6},{1,7},{2,4},{3,5},{4,2},{5,3},{6,0},{7,1},{8,14},{9,15},{10,... | collective-permute-start | bytes 344072 | tf_op jit(solution)/shard_map/ppermute | solution.py:586
  137.4 6.0 %attend.3 = (bf16[448,128]{1,0:T(8,128)(2,1)S(1)}, bf16[448,128]{1,0:T(8,128)(2,1)S(1)}, bf16[448,128]{1,0:T(8,128)(2,1)S(1)}, bf16[448,128]{1,0:T(8,128)(2,1)S(1)}) custom-call(s32[16]{0:T(128)S(1)} %fusion.12.places, s32[16]{0:T(128)S(1)} %get-tuple-element.111.lows, s32[16]{0:T(128)S(1)} %get-tuple-element.112.sizes, f32[16,224]{1,0:T(8,128)S(1)} %reshape.16.seg_tiles, ...), custom_call_target="tpu_custom_call" | custom-call | flops 1056964608 | bytes 11927552 | tf_op jit(solution)/shard_map/attend/pallas_call | solution.py:310
  143.9 2.7 %collective-permute-done.30 = bf16[448,128]{1,0:T(8,128)(2,1)S(1)} collective-permute-done((bf16[448,128]{1,0:T(8,128)(2,1)S(1)}, bf16[448,128]{1,0:T(8,128)(2,1)S(1)}, u32[]{:S(2)}, u32[]{:S(2)}) %collective-permute-start.30) | collective-permute-done | bytes 114720 | tf_op jit(solution)/shard_map/ppermute | solution.py:586
  146.9 1.6 collective-permute-start.31
  148.4 10.0 %collective-permute-done.31.refs_4_.refs_2_ = bf16[448,512]{1,0:T(8,128)(2,1)S(1)} collective-permute-done((bf16[448,512]{1,0:T(8,128)(2,1)S(1)}, bf16[448,512]{1,0:T(8,128)(2,1)S(1)}, u32[]{:S(2)}, u32[]{:S(2)}) %collective-permute-start.31) | collective-permute-done | bytes 458784 | tf_op jit(solution)/shard_map/ppermute | solution.py:426
  158.4 1.2 collective-permute-done.33.refs_0_
  159.6 1.3 collective-permute-start.34
  161.0 2.1 %collective-permute-start.35 = (bf16[448,128]{1,0:T(8,128)(2,1)S(1)}, bf16[448,128]{1,0:T(8,128)(2,1)S(1)}, u32[]{:S(2)}, u32[]{:S(2)}) collective-permute-start(bf16[448,128]{1,0:T(8,128)(2,1)S(1)} %get-tuple-element.183), channel_id=1, source_target_pairs={{0,6},{1,7},{2,4},{3,5},{4,2},{5,3},{6,0},{7,1},{8,14},{9,15},{10,... | collective-permute-start | bytes 344072 | tf_op jit(solution)/shard_map/ppermute | solution.py:586
  163.1 2.5 %collective-permute-done.34 = bf16[448,128]{1,0:T(8,128)(2,1)S(1)} collective-permute-done((bf16[448,128]{1,0:T(8,128)(2,1)S(1)}, bf16[448,128]{1,0:T(8,128)(2,1)S(1)}, u32[]{:S(2)}, u32[]{:S(2)}) %collective-permute-start.34) | collective-permute-done | bytes 114720 | tf_op jit(solution)/shard_map/ppermute | solution.py:586
  165.7 2.9 %collective-permute-done.35 = bf16[448,128]{1,0:T(8,128)(2,1)S(1)} collective-permute-done((bf16[448,128]{1,0:T(8,128)(2,1)S(1)}, bf16[448,128]{1,0:T(8,128)(2,1)S(1)}, u32[]{:S(2)}, u32[]{:S(2)}) %collective-permute-start.35) | collective-permute-done | bytes 114720 | tf_op jit(solution)/shard_map/ppermute | solution.py:586
  168.7 2.7 %collective-permute-done.36 = bf16[448,128]{1,0:T(8,128)(2,1)S(1)} collective-permute-done((bf16[448,128]{1,0:T(8,128)(2,1)S(1)}, bf16[448,128]{1,0:T(8,128)(2,1)S(1)}, u32[]{:S(2)}, u32[]{:S(2)}) %collective-permute-start.36) | collective-permute-done | bytes 114720 | tf_op jit(solution)/shard_map/ppermute | solution.py:586
  171.4 1.7 collective-permute-start.37
  173.5 2.8 %project.8.refs_5_ = f32[448,1024]{1,0:T(8,128)S(1)} custom-call(s32[4]{0:T(128)S(1)} %pad_add_fusion.heads.slots, bf16[512,1024]{1,0:T(8,128)(2,1)S(1)} %copy-done.4, bf16[512,1024]{1,0:T(8,128)(2,1)S(1)} %collective-permute-done.11.refs_1_, bf16[512,1024]{1,0:T(8,128)(2,1)S(1)} %collective-permute-done.27.refs_2_, ...), custom_call_target="tpu_custom_call" | custom-call | flops 1409286144 | bytes 6356992 | tf_op jit(solution)/shard_map/project/pallas_call | solution.py:372
  177.3 1.4 collective-permute-start.41
  178.7 4.2 %collective-permute-done.37.refs_4_.refs_2_ = bf16[448,512]{1,0:T(8,128)(2,1)S(1)} collective-permute-done((bf16[448,512]{1,0:T(8,128)(2,1)S(1)}, bf16[448,512]{1,0:T(8,128)(2,1)S(1)}, u32[]{:S(2)}, u32[]{:S(2)}) %collective-permute-start.37) | collective-permute-done | bytes 458784 | tf_op jit(solution)/shard_map/ppermute | solution.py:426
  183.0 3.1 %collective-permute-done.42.refs_0_ = bf16[512,512]{1,0:T(8,128)(2,1)S(1)} collective-permute-done((bf16[512,512]{1,0:T(8,128)(2,1)S(1)}, bf16[512,512]{1,0:T(8,128)(2,1)S(1)}, u32[]{:S(2)}, u32[]{:S(2)}) %collective-permute-start.42) | collective-permute-done | bytes 524320 | tf_op jit(solution)/shard_map/ppermute | solution.py:420
  186.0 2.6 %collective-permute-done.41 = bf16[448,512]{1,0:T(8,128)(2,1)S(1)} collective-permute-done((bf16[448,512]{1,0:T(8,128)(2,1)S(1)}, bf16[448,512]{1,0:T(8,128)(2,1)S(1)}, u32[]{:S(2)}, u32[]{:S(2)}) %collective-permute-start.41) | collective-permute-done | bytes 458784 | tf_op jit(solution)/shard_map/ppermute | solution.py:417
  189.7 1.4 collective-permute-start.43
  191.1 2.8 %project.6.refs_5_ = f32[448,1024]{1,0:T(8,128)S(1)} custom-call(s32[4]{0:T(128)S(1)} %pad_add_fusion.heads.slots, bf16[512,1024]{1,0:T(8,128)(2,1)S(1)} %copy-done.4, bf16[512,1024]{1,0:T(8,128)(2,1)S(1)} %collective-permute-done.11.refs_1_, bf16[512,1024]{1,0:T(8,128)(2,1)S(1)} %collective-permute-done.27.refs_2_, ...), custom_call_target="tpu_custom_call" | custom-call | flops 1409286144 | bytes 6356992 | tf_op jit(solution)/shard_map/project/pallas_call | solution.py:372
  196.3 3.8 %collective-permute-done.43 = bf16[448,512]{1,0:T(8,128)(2,1)S(1)} collective-permute-done((bf16[448,512]{1,0:T(8,128)(2,1)S(1)}, bf16[448,512]{1,0:T(8,128)(2,1)S(1)}, u32[]{:S(2)}, u32[]{:S(2)}) %collective-permute-start.43) | collective-permute-done | bytes 458784 | tf_op jit(solution)/shard_map/ppermute | solution.py:417
  200.2 1.2 fusion.1
  (131 shorter events, 26.0 us)
Async XLA Ops:
  0.0 26.8 %collective-permute-start = (bf16[448,1024]{1,0:T(8,128)(2,1)}, bf16[448,1024]{1,0:T(8,128)(2,1)S(1)}, u32[]{:S(2)}, u32[]{:S(2)}) collective-permute-start(bf16[448,1024]{1,0:T(8,128)(2,1)} %tokens.1), channel_id=1, source_target_pairs={{0,4},{1,5},{2,0},{3,1},{4,6},{5,7},{6,2},{7,3},{8,12},{9,13},{10,... | collective-permute-start | bytes 2752520 | tf_op jit(solution)/shard_map/ppermute | solution.py:420
  4.0 23.7 %collective-permute-start.1 = (bf16[448,1024]{1,0:T(8,128)(2,1)}, bf16[448,1024]{1,0:T(8,128)(2,1)S(1)}, u32[]{:S(2)}, u32[]{:S(2)}) collective-permute-start(bf16[448,1024]{1,0:T(8,128)(2,1)} %tokens.1), channel_id=1, source_target_pairs={{0,1},{1,0},{2,3},{3,2},{4,5},{5,4},{6,7},{7,6},{8,9},{9,8},{10,11... | collective-permute-start | bytes 2752520 | tf_op jit(solution)/shard_map/ppermute | solution.py:417
  13.5 11.0 %collective-permute-start.2 = (bf16[16,1024]{1,0:T(8,128)(2,1)S(1)}, bf16[16,1024]{1,0:T(8,128)(2,1)S(1)}, u32[]{:S(2)}, u32[]{:S(2)}) collective-permute-start(bf16[16,1024]{1,0:T(8,128)(2,1)S(1)} %pack.1.stats), channel_id=1, source_target_pairs={{0,4},{1,5},{2,0},{3,1},{4,6},{5,7},{6,2},{7,3},{8,12},{9,13},{10,... | collective-permute-start | bytes 98312 | tf_op jit(solution)/shard_map/ppermute | solution.py:420
  15.2 11.6 %collective-permute-start.3 = (bf16[16,1024]{1,0:T(8,128)(2,1)S(1)}, bf16[16,1024]{1,0:T(8,128)(2,1)S(1)}, u32[]{:S(2)}, u32[]{:S(2)}) collective-permute-start(bf16[16,1024]{1,0:T(8,128)(2,1)S(1)} %pack.1.stats), channel_id=1, source_target_pairs={{0,1},{1,0},{2,3},{3,2},{4,5},{5,4},{6,7},{7,6},{8,9},{9,8},{10,11... | collective-permute-start | bytes 98312 | tf_op jit(solution)/shard_map/ppermute | solution.py:417
  17.2 1.6 copy-start.2
  17.2 1.6 copy-start.13
  17.2 1.6 copy-start.14
  18.8 16.2 %copy-start.17 = (s32[3584]{0:T(1024)S(1)}, s32[3584]{0:T(1024)}, u32[]{:S(2)}) copy-start(s32[3584]{0:T(1024)} %param.18) | copy-start | bytes 43012
  18.9 16.3 %copy-start.18 = (s32[2,3584]{1,0:T(2,128)S(1)}, s32[2,3584]{1,0:T(2,128)}, u32[]{:S(2)}) copy-start(s32[2,3584]{1,0:T(2,128)} %param.20) | copy-start | bytes 86020
  19.5 0.9 copy-start.5
  26.8 0.9 copy-start.9
  27.7 1.0 copy-start.7
  28.6 11.3 %collective-permute-start.6 = (bf16[1024,768]{1,0:T(8,128)(2,1)}, bf16[1024,768]{1,0:T(8,128)(2,1)}, u32[]{:S(2)}, u32[]{:S(2)}) collective-permute-start(bf16[1024,768]{1,0:T(8,128)(2,1)} %pad_maximum_fusion), channel_id=1, source_target_pairs={{0,8},{8,0},{16,24},{24,16},{1,9},{9,1},{17,25},{25,17},{2,10},{10... | collective-permute-start | bytes 4718600 | tf_op jit(solution)/shard_map/ppermute | solution.py:423
  28.7 1.2 copy-start.10
  29.9 10.0 %copy-start.1 = (bf16[1024,1536]{1,0:T(8,128)(2,1)S(1)}, bf16[1024,1536]{1,0:T(8,128)(2,1)}, u32[]{:S(2)}) copy-start(bf16[1024,1536]{1,0:T(8,128)(2,1)} %w_own.15) | copy-start | bytes 9437188
  31.5 18.3 %collective-permute-start.10 = (bf16[448,1024]{1,0:T(8,128)(2,1)}, bf16[448,1024]{1,0:T(8,128)(2,1)}, u32[]{:S(2)}, u32[]{:S(2)}) collective-permute-start(bf16[448,1024]{1,0:T(8,128)(2,1)} %norm.4.refs_0_), channel_id=1, source_target_pairs={{0,8},{8,0},{16,24},{24,16},{1,9},{9,1},{17,25},{25,17},{2,10},{10... | collective-permute-start | bytes 2752520 | tf_op jit(solution)/shard_map/ppermute | solution.py:423
  32.0 22.6 %collective-permute-start.4 = (bf16[448,1024]{1,0:T(8,128)(2,1)}, bf16[448,1024]{1,0:T(8,128)(2,1)}, u32[]{:S(2)}, u32[]{:S(2)}) collective-permute-start(bf16[448,1024]{1,0:T(8,128)(2,1)} %norm.4.refs_0_), channel_id=1, source_target_pairs={{0,1},{1,0},{2,3},{3,2},{4,5},{5,4},{6,7},{7,6},{8,9},{9,8},{10,11... | collective-permute-start | bytes 2752520 | tf_op jit(solution)/shard_map/ppermute | solution.py:417
  33.5 22.3 %collective-permute-start.5 = (bf16[448,1024]{1,0:T(8,128)(2,1)}, bf16[448,1024]{1,0:T(8,128)(2,1)}, u32[]{:S(2)}, u32[]{:S(2)}) collective-permute-start(bf16[448,1024]{1,0:T(8,128)(2,1)} %norm.4.refs_0_), channel_id=1, source_target_pairs={{0,4},{1,5},{2,0},{3,1},{4,6},{5,7},{6,2},{7,3},{8,12},{9,13},{10,... | collective-permute-start | bytes 2752520 | tf_op jit(solution)/shard_map/ppermute | solution.py:420
  35.1 4.8 %copy-start.6 = (bf16[448,1024]{1,0:T(8,128)(2,1)S(1)}, bf16[448,1024]{1,0:T(8,128)(2,1)}, u32[]{:S(2)}) copy-start(bf16[448,1024]{1,0:T(8,128)(2,1)} %copy-done.5) | copy-start | bytes 2752516
  35.1 3.5 %collective-permute-start.7 = (bf16[448,1024]{1,0:T(8,128)(2,1)}, bf16[448,1024]{1,0:T(8,128)(2,1)S(1)}, u32[]{:S(2)}, u32[]{:S(2)}) collective-permute-start(bf16[448,1024]{1,0:T(8,128)(2,1)} %copy-done.5), channel_id=1, source_target_pairs={{0,8},{8,0},{16,24},{24,16},{1,9},{9,1},{17,25},{25,17},{2,10},{10... | collective-permute-start | bytes 2752520 | tf_op jit(solution)/shard_map/ppermute | solution.py:423
  35.6 1.2 copy-start.8
  36.8 2.5 %copy-start.19 = (s32[3584]{0:T(1024)S(1)}, s32[3584]{0:T(1024)}, u32[]{:S(2)}) copy-start(s32[3584]{0:T(1024)} %param.19) | copy-start | bytes 43012
  38.7 15.9 %collective-permute-start.9 = (bf16[448,1024]{1,0:T(8,128)(2,1)}, bf16[448,1024]{1,0:T(8,128)(2,1)}, u32[]{:S(2)}, u32[]{:S(2)}) collective-permute-start(bf16[448,1024]{1,0:T(8,128)(2,1)} %norm.5.refs_0_), channel_id=1, source_target_pairs={{0,8},{8,0},{16,24},{24,16},{1,9},{9,1},{17,25},{25,17},{2,10},{10... | collective-permute-start | bytes 2752520 | tf_op jit(solution)/shard_map/ppermute | solution.py:423
  43.4 0.7 copy-start.11
  44.1 11.6 %collective-permute-start.8 = (bf16[448,384]{1,0:T(8,128)(2,1)}, bf16[448,384]{1,0:T(8,128)(2,1)}, u32[]{:S(2)}, u32[]{:S(2)}) collective-permute-start(bf16[448,384]{1,0:T(8,128)(2,1)} %get-tuple-element.103), channel_id=1, source_target_pairs={{0,16},{8,24},{16,0},{24,8},{1,17},{9,25},{17,1},{25,9},{2,18},{10... | collective-permute-start | bytes 1032200 | tf_op jit(solution)/shard_map/ppermute | solution.py:426
  55.8 9.2 %collective-permute-start.17 = (bf16[448,1024]{1,0:T(8,128)(2,1)}, bf16[448,1024]{1,0:T(8,128)(2,1)}, u32[]{:S(2)}, u32[]{:S(2)}) collective-permute-start(bf16[448,1024]{1,0:T(8,128)(2,1)} %collective-permute-done.5.refs_0_), channel_id=1, source_target_pairs={{0,8},{8,0},{16,24},{24,16},{1,9},{9,1},{17,25},{25,17},{2,10},{10... | collective-permute-start | bytes 2752520 | tf_op jit(solution)/shard_map/ppermute | solution.py:423
  55.8 16.2 %collective-permute-start.16 = (bf16[448,1024]{1,0:T(8,128)(2,1)}, bf16[448,1024]{1,0:T(8,128)(2,1)}, u32[]{:S(2)}, u32[]{:S(2)}) collective-permute-start(bf16[448,1024]{1,0:T(8,128)(2,1)} %collective-permute-done.4.refs_0_), channel_id=1, source_target_pairs={{0,8},{8,0},{16,24},{24,16},{1,9},{9,1},{17,25},{25,17},{2,10},{10... | collective-permute-start | bytes 2752520 | tf_op jit(solution)/shard_map/ppermute | solution.py:423
  56.3 24.0 %collective-permute-start.12 = (bf16[448,1024]{1,0:T(8,128)(2,1)}, bf16[448,1024]{1,0:T(8,128)(2,1)}, u32[]{:S(2)}, u32[]{:S(2)}) collective-permute-start(bf16[448,1024]{1,0:T(8,128)(2,1)} %collective-permute-done.5.refs_0_), channel_id=1, source_target_pairs={{0,4},{1,5},{2,0},{3,1},{4,6},{5,7},{6,2},{7,3},{8,12},{9,13},{10,... | collective-permute-start | bytes 2752520 | tf_op jit(solution)/shard_map/ppermute | solution.py:420
  58.8 22.3 %collective-permute-start.13 = (bf16[448,1024]{1,0:T(8,128)(2,1)}, bf16[448,1024]{1,0:T(8,128)(2,1)}, u32[]{:S(2)}, u32[]{:S(2)}) collective-permute-start(bf16[448,1024]{1,0:T(8,128)(2,1)} %collective-permute-done.5.refs_0_), channel_id=1, source_target_pairs={{0,1},{1,0},{2,3},{3,2},{4,5},{5,4},{6,7},{7,6},{8,9},{9,8},{10,11... | collective-permute-start | bytes 2752520 | tf_op jit(solution)/shard_map/ppermute | solution.py:417
  59.3 5.7 %copy-start.16 = (bf16[448,384]{1,0:T(8,128)(2,1)S(1)}, bf16[448,384]{1,0:T(8,128)(2,1)}, u32[]{:S(2)}) copy-start(bf16[448,384]{1,0:T(8,128)(2,1)} %copy-done.15) | copy-start | bytes 1032196
  59.3 6.9 %copy-start = (f32[3584,256]{1,0:T(8,128)S(1)}, f32[3584,256]{1,0:T(8,128)}, u32[]{:S(2)}) copy-start(f32[3584,256]{1,0:T(8,128)} %fusion.2.table) | copy-start | bytes 11010052
  59.3 6.9 %copy-start.12 = (bf16[448,384]{1,0:T(8,128)(2,1)S(1)}, bf16[448,384]{1,0:T(8,128)(2,1)}, u32[]{:S(2)}) copy-start(bf16[448,384]{1,0:T(8,128)(2,1)} %copy-done.11) | copy-start | bytes 1032196
  63.4 12.7 %collective-permute-start.15 = (bf16[448,384]{1,0:T(8,128)(2,1)S(1)}, bf16[448,384]{1,0:T(8,128)(2,1)S(1)}, u32[]{:S(2)}, u32[]{:S(2)}) collective-permute-start(bf16[448,384]{1,0:T(8,128)(2,1)S(1)} %get-tuple-element.121), channel_id=1, source_target_pairs={{0,16},{8,24},{16,0},{24,8},{1,17},{9,25},{17,1},{25,9},{2,18},{10... | collective-permute-start | bytes 1032200 | tf_op jit(solution)/shard_map/ppermute | solution.py:426
  65.0 15.3 %collective-permute-start.14 = (bf16[448,384]{1,0:T(8,128)(2,1)S(1)}, bf16[448,384]{1,0:T(8,128)(2,1)S(1)}, u32[]{:S(2)}, u32[]{:S(2)}) collective-permute-start(bf16[448,384]{1,0:T(8,128)(2,1)S(1)} %copy-done.16), channel_id=1, source_target_pairs={{0,16},{8,24},{16,0},{24,8},{1,17},{9,25},{17,1},{25,9},{2,18},{10... | collective-permute-start | bytes 1032200 | tf_op jit(solution)/shard_map/ppermute | solution.py:426
  72.0 9.6 %copy-start.4 = (bf16[512,1024]{1,0:T(8,128)(2,1)S(1)}, bf16[512,1024]{1,0:T(8,128)(2,1)}, u32[]{:S(2)}) copy-start(bf16[512,1024]{1,0:T(8,128)(2,1)} %refs_0_.3) | copy-start | bytes 3145732
  81.1 3.7 %collective-permute-start.21 = (bf16[448,1024]{1,0:T(8,128)(2,1)}, bf16[448,1024]{1,0:T(8,128)(2,1)S(1)}, u32[]{:S(2)}, u32[]{:S(2)}) collective-permute-start(bf16[448,1024]{1,0:T(8,128)(2,1)} %collective-permute-done.12.refs_0_), channel_id=1, source_target_pairs={{0,8},{8,0},{16,24},{24,16},{1,9},{9,1},{17,25},{25,17},{2,10},{10... | collective-permute-start | bytes 2752520 | tf_op jit(solution)/shard_map/ppermute | solution.py:423
  81.1 8.0 %collective-permute-start.23 = (bf16[448,1024]{1,0:T(8,128)(2,1)}, bf16[448,1024]{1,0:T(8,128)(2,1)S(1)}, u32[]{:S(2)}, u32[]{:S(2)}) collective-permute-start(bf16[448,1024]{1,0:T(8,128)(2,1)} %collective-permute-done.13.refs_0_), channel_id=1, source_target_pairs={{0,8},{8,0},{16,24},{24,16},{1,9},{9,1},{17,25},{25,17},{2,10},{10... | collective-permute-start | bytes 2752520 | tf_op jit(solution)/shard_map/ppermute | solution.py:423
  81.6 25.1 %collective-permute-start.11 = (bf16[512,1024]{1,0:T(8,128)(2,1)S(1)}, bf16[512,1024]{1,0:T(8,128)(2,1)S(1)}, u32[]{:S(2)}, u32[]{:S(2)}) collective-permute-start(bf16[512,1024]{1,0:T(8,128)(2,1)S(1)} %copy-done.4), channel_id=1, source_target_pairs={{0,4},{1,5},{2,0},{3,1},{4,6},{5,7},{6,2},{7,3},{8,12},{9,13},{10,... | collective-permute-start | bytes 3145736 | tf_op jit(solution)/shard_map/ppermute | solution.py:420
  82.8 23.9 %collective-permute-start.18 = (bf16[448,1024]{1,0:T(8,128)(2,1)}, bf16[448,1024]{1,0:T(8,128)(2,1)S(1)}, u32[]{:S(2)}, u32[]{:S(2)}) collective-permute-start(bf16[448,1024]{1,0:T(8,128)(2,1)} %collective-permute-done.12.refs_0_), channel_id=1, source_target_pairs={{0,1},{1,0},{2,3},{3,2},{4,5},{5,4},{6,7},{7,6},{8,9},{9,8},{10,11... | collective-permute-start | bytes 2752520 | tf_op jit(solution)/shard_map/ppermute | solution.py:417
  83.3 23.4 %collective-permute-start.19 = (bf16[448,384]{1,0:T(8,128)(2,1)S(1)}, bf16[448,384]{1,0:T(8,128)(2,1)S(1)}, u32[]{:S(2)}, u32[]{:S(2)}) collective-permute-start(bf16[448,384]{1,0:T(8,128)(2,1)S(1)} %get-tuple-element.132), channel_id=1, source_target_pairs={{0,16},{8,24},{16,0},{24,8},{1,17},{9,25},{17,1},{25,9},{2,18},{10... | collective-permute-start | bytes 1032200 | tf_op jit(solution)/shard_map/ppermute | solution.py:426
  84.8 21.9 %collective-permute-start.20 = (bf16[448,384]{1,0:T(8,128)(2,1)S(1)}, bf16[448,384]{1,0:T(8,128)(2,1)S(1)}, u32[]{:S(2)}, u32[]{:S(2)}) collective-permute-start(bf16[448,384]{1,0:T(8,128)(2,1)S(1)} %get-tuple-element.134), channel_id=1, source_target_pairs={{0,16},{8,24},{16,0},{24,8},{1,17},{9,25},{17,1},{25,9},{2,18},{10... | collective-permute-start | bytes 1032200 | tf_op jit(solution)/shard_map/ppermute | solution.py:426
  89.0 18.4 %collective-permute-start.22 = (bf16[448,384]{1,0:T(8,128)(2,1)S(1)}, bf16[448,384]{1,0:T(8,128)(2,1)S(1)}, u32[]{:S(2)}, u32[]{:S(2)}) collective-permute-start(bf16[448,384]{1,0:T(8,128)(2,1)S(1)} %get-tuple-element.136), channel_id=1, source_target_pairs={{0,16},{8,24},{16,0},{24,8},{1,17},{9,25},{17,1},{25,9},{2,18},{10... | collective-permute-start | bytes 1032200 | tf_op jit(solution)/shard_map/ppermute | solution.py:426
  107.4 3.2 %collective-permute-start.24 = (bf16[448,1024]{1,0:T(8,128)(2,1)S(1)}, bf16[448,1024]{1,0:T(8,128)(2,1)S(1)}, u32[]{:S(2)}, u32[]{:S(2)}) collective-permute-start(bf16[448,1024]{1,0:T(8,128)(2,1)S(1)} %collective-permute-done.18.refs_0_), channel_id=1, source_target_pairs={{0,8},{8,0},{16,24},{24,16},{1,9},{9,1},{17,25},{25,17},{2,10},{10... | collective-permute-start | bytes 2752520 | tf_op jit(solution)/shard_map/ppermute | solution.py:423
  107.4 26.0 %collective-permute-start.27 = (bf16[512,1024]{1,0:T(8,128)(2,1)S(1)}, bf16[512,1024]{1,0:T(8,128)(2,1)S(1)}, u32[]{:S(2)}, u32[]{:S(2)}) collective-permute-start(bf16[512,1024]{1,0:T(8,128)(2,1)S(1)} %collective-permute-done.11.refs_1_), channel_id=1, source_target_pairs={{0,4},{1,5},{2,0},{3,1},{4,6},{5,7},{6,2},{7,3},{8,12},{9,13},{10,... | collective-permute-start | bytes 3145736 | tf_op jit(solution)/shard_map/ppermute | solution.py:420
  109.1 10.9 %collective-permute-start.26 = (bf16[448,384]{1,0:T(8,128)(2,1)S(1)}, bf16[448,384]{1,0:T(8,128)(2,1)S(1)}, u32[]{:S(2)}, u32[]{:S(2)}) collective-permute-start(bf16[448,384]{1,0:T(8,128)(2,1)S(1)} %get-tuple-element.149), channel_id=1, source_target_pairs={{0,16},{8,24},{16,0},{24,8},{1,17},{9,25},{17,1},{25,9},{2,18},{10... | collective-permute-start | bytes 1032200 | tf_op jit(solution)/shard_map/ppermute | solution.py:426
  114.1 12.3 %collective-permute-start.25 = (bf16[448,384]{1,0:T(8,128)(2,1)S(1)}, bf16[448,384]{1,0:T(8,128)(2,1)S(1)}, u32[]{:S(2)}, u32[]{:S(2)}) collective-permute-start(bf16[448,384]{1,0:T(8,128)(2,1)S(1)} %get-tuple-element.147), channel_id=1, source_target_pairs={{0,16},{8,24},{16,0},{24,8},{1,17},{9,25},{17,1},{25,9},{2,18},{10... | collective-permute-start | bytes 1032200 | tf_op jit(solution)/shard_map/ppermute | solution.py:426
  133.4 10.0 %collective-permute-start.28 = (bf16[448,128]{1,0:T(8,128)(2,1)S(1)}, bf16[448,128]{1,0:T(8,128)(2,1)S(1)}, u32[]{:S(2)}, u32[]{:S(2)}) collective-permute-start(bf16[448,128]{1,0:T(8,128)(2,1)S(1)} %get-tuple-element.163), channel_id=1, source_target_pairs={{0,4},{1,5},{2,0},{3,1},{4,6},{5,7},{6,2},{7,3},{8,12},{9,13},{10,... | collective-permute-start | bytes 344072 | tf_op jit(solution)/shard_map/ppermute | solution.py:586
  135.3 8.6 %collective-permute-start.29 = (bf16[448,128]{1,0:T(8,128)(2,1)S(1)}, bf16[448,128]{1,0:T(8,128)(2,1)S(1)}, u32[]{:S(2)}, u32[]{:S(2)}) collective-permute-start(bf16[448,128]{1,0:T(8,128)(2,1)S(1)} %get-tuple-element.164), channel_id=1, source_target_pairs={{0,6},{1,7},{2,4},{3,5},{4,2},{5,3},{6,0},{7,1},{8,14},{9,15},{10,... | collective-permute-start | bytes 344072 | tf_op jit(solution)/shard_map/ppermute | solution.py:586
  137.4 9.2 %collective-permute-start.30 = (bf16[448,128]{1,0:T(8,128)(2,1)S(1)}, bf16[448,128]{1,0:T(8,128)(2,1)S(1)}, u32[]{:S(2)}, u32[]{:S(2)}) collective-permute-start(bf16[448,128]{1,0:T(8,128)(2,1)S(1)} %get-tuple-element.165), channel_id=1, source_target_pairs={{0,2},{1,3},{2,6},{3,7},{4,0},{5,1},{6,4},{7,5},{8,10},{9,11},{10,... | collective-permute-start | bytes 344072 | tf_op jit(solution)/shard_map/ppermute | solution.py:586
  146.7 12.9 %collective-permute-start.33 = (bf16[512,512]{1,0:T(8,128)(2,1)S(1)}, bf16[512,512]{1,0:T(8,128)(2,1)S(1)}, u32[]{:S(2)}, u32[]{:S(2)}) collective-permute-start(bf16[512,512]{1,0:T(8,128)(2,1)S(1)} %slice.22), channel_id=1, source_target_pairs={{0,4},{1,5},{2,0},{3,1},{4,6},{5,7},{6,2},{7,3},{8,12},{9,13},{10,... | collective-permute-start | bytes 1572872 | tf_op jit(solution)/shard_map/ppermute | solution.py:420
  146.9 11.5 %collective-permute-start.31 = (bf16[448,512]{1,0:T(8,128)(2,1)S(1)}, bf16[448,512]{1,0:T(8,128)(2,1)S(1)}, u32[]{:S(2)}, u32[]{:S(2)}) collective-permute-start(bf16[448,512]{1,0:T(8,128)(2,1)S(1)} %constant_dynamic-update-slice_fusion.refs_3_.refs_1_), channel_id=1, source_target_pairs={{0,16},{8,24},{16,0},{24,8},{1,17},{9,25},{17,1},{25,9},{2,18},{10... | collective-permute-start | bytes 1376264 | tf_op jit(solution)/shard_map/ppermute | solution.py:426
  148.4 10.0 %collective-permute-start.32 = (bf16[448,512]{1,0:T(8,128)(2,1)S(1)}, bf16[448,512]{1,0:T(8,128)(2,1)S(1)}, u32[]{:S(2)}, u32[]{:S(2)}) collective-permute-start(bf16[448,512]{1,0:T(8,128)(2,1)S(1)} %constant_dynamic-update-slice_fusion.refs_3_.refs_1_), channel_id=1, source_target_pairs={{0,8},{8,0},{16,24},{24,16},{1,9},{9,1},{17,25},{25,17},{2,10},{10... | collective-permute-start | bytes 1376264 | tf_op jit(solution)/shard_map/ppermute | solution.py:423
  159.6 6.0 %collective-permute-start.34 = (bf16[448,128]{1,0:T(8,128)(2,1)S(1)}, bf16[448,128]{1,0:T(8,128)(2,1)S(1)}, u32[]{:S(2)}, u32[]{:S(2)}) collective-permute-start(bf16[448,128]{1,0:T(8,128)(2,1)S(1)} %get-tuple-element.182), channel_id=1, source_target_pairs={{0,4},{1,5},{2,0},{3,1},{4,6},{5,7},{6,2},{7,3},{8,12},{9,13},{10,... | collective-permute-start | bytes 344072 | tf_op jit(solution)/shard_map/ppermute | solution.py:586
  161.0 7.7 %collective-permute-start.35 = (bf16[448,128]{1,0:T(8,128)(2,1)S(1)}, bf16[448,128]{1,0:T(8,128)(2,1)S(1)}, u32[]{:S(2)}, u32[]{:S(2)}) collective-permute-start(bf16[448,128]{1,0:T(8,128)(2,1)S(1)} %get-tuple-element.183), channel_id=1, source_target_pairs={{0,6},{1,7},{2,4},{3,5},{4,2},{5,3},{6,0},{7,1},{8,14},{9,15},{10,... | collective-permute-start | bytes 344072 | tf_op jit(solution)/shard_map/ppermute | solution.py:586
  163.1 8.3 %collective-permute-start.36 = (bf16[448,128]{1,0:T(8,128)(2,1)S(1)}, bf16[448,128]{1,0:T(8,128)(2,1)S(1)}, u32[]{:S(2)}, u32[]{:S(2)}) collective-permute-start(bf16[448,128]{1,0:T(8,128)(2,1)S(1)} %get-tuple-element.184), channel_id=1, source_target_pairs={{0,2},{1,3},{2,6},{3,7},{4,0},{5,1},{6,4},{7,5},{8,10},{9,11},{10,... | collective-permute-start | bytes 344072 | tf_op jit(solution)/shard_map/ppermute | solution.py:586
  163.1 10.4 %collective-permute-start.40 = (bf16[448,512]{1,0:T(8,128)(2,1)S(1)}, bf16[448,512]{1,0:T(8,128)(2,1)S(1)}, u32[]{:S(2)}, u32[]{:S(2)}) collective-permute-start(bf16[448,512]{1,0:T(8,128)(2,1)S(1)} %collective-permute-done.31.refs_4_.refs_2_), channel_id=1, source_target_pairs={{0,8},{8,0},{16,24},{24,16},{1,9},{9,1},{17,25},{25,17},{2,10},{10... | collective-permute-start | bytes 1376264 | tf_op jit(solution)/shard_map/ppermute | solution.py:423
  171.4 11.5 %collective-permute-start.37 = (bf16[448,512]{1,0:T(8,128)(2,1)S(1)}, bf16[448,512]{1,0:T(8,128)(2,1)S(1)}, u32[]{:S(2)}, u32[]{:S(2)}) collective-permute-start(bf16[448,512]{1,0:T(8,128)(2,1)S(1)} %constant_dynamic-update-slice_fusion.4.refs_3_.refs_1_), channel_id=1, source_target_pairs={{0,16},{8,24},{16,0},{24,8},{1,17},{9,25},{17,1},{25,9},{2,18},{10... | collective-permute-start | bytes 1376264 | tf_op jit(solution)/shard_map/ppermute | solution.py:426
  173.1 12.9 %collective-permute-start.42 = (bf16[512,512]{1,0:T(8,128)(2,1)S(1)}, bf16[512,512]{1,0:T(8,128)(2,1)S(1)}, u32[]{:S(2)}, u32[]{:S(2)}) collective-permute-start(bf16[512,512]{1,0:T(8,128)(2,1)S(1)} %slice.23), channel_id=1, source_target_pairs={{0,4},{1,5},{2,0},{3,1},{4,6},{5,7},{6,2},{7,3},{8,12},{9,13},{10,... | collective-permute-start | bytes 1572872 | tf_op jit(solution)/shard_map/ppermute | solution.py:420
  177.3 11.3 %collective-permute-start.41 = (bf16[448,512]{1,0:T(8,128)(2,1)S(1)}, bf16[448,512]{1,0:T(8,128)(2,1)S(1)}, u32[]{:S(2)}, u32[]{:S(2)}) collective-permute-start(bf16[448,512]{1,0:T(8,128)(2,1)S(1)} %project.9), channel_id=1, source_target_pairs={{0,1},{1,0},{2,3},{3,2},{4,5},{5,4},{6,7},{7,6},{8,9},{9,8},{10,11... | collective-permute-start | bytes 1376264 | tf_op jit(solution)/shard_map/ppermute | solution.py:417
  178.7 12.4 %collective-permute-start.38 = (bf16[448,512]{1,0:T(8,128)(2,1)S(1)}, bf16[448,512]{1,0:T(8,128)(2,1)S(1)}, u32[]{:S(2)}, u32[]{:S(2)}) collective-permute-start(bf16[448,512]{1,0:T(8,128)(2,1)S(1)} %constant_dynamic-update-slice_fusion.4.refs_3_.refs_1_), channel_id=1, source_target_pairs={{0,8},{8,0},{16,24},{24,16},{1,9},{9,1},{17,25},{25,17},{2,10},{10... | collective-permute-start | bytes 1376264 | tf_op jit(solution)/shard_map/ppermute | solution.py:423
  182.9 8.2 %collective-permute-start.39 = (bf16[448,512]{1,0:T(8,128)(2,1)S(1)}, bf16[448,512]{1,0:T(8,128)(2,1)S(1)}, u32[]{:S(2)}, u32[]{:S(2)}) collective-permute-start(bf16[448,512]{1,0:T(8,128)(2,1)S(1)} %collective-permute-done.37.refs_4_.refs_2_), channel_id=1, source_target_pairs={{0,8},{8,0},{16,24},{24,16},{1,9},{9,1},{17,25},{25,17},{2,10},{10... | collective-permute-start | bytes 1376264 | tf_op jit(solution)/shard_map/ppermute | solution.py:423
  189.7 10.3 %collective-permute-start.43 = (bf16[448,512]{1,0:T(8,128)(2,1)S(1)}, bf16[448,512]{1,0:T(8,128)(2,1)S(1)}, u32[]{:S(2)}, u32[]{:S(2)}) collective-permute-start(bf16[448,512]{1,0:T(8,128)(2,1)S(1)} %project.11), channel_id=1, source_target_pairs={{0,1},{1,0},{2,3},{3,2},{4,5},{5,4},{6,7},{7,6},{8,9},{9,8},{10,11... | collective-permute-start | bytes 1376264 | tf_op jit(solution)/shard_map/ppermute | solution.py:417
  196.2 4.1 %copy-start.3 = (bf16[448,1024]{1,0:T(8,128)(2,1)S(1)}, bf16[448,1024]{1,0:T(8,128)(2,1)}, u32[]{:S(2)}) copy-start(bf16[448,1024]{1,0:T(8,128)(2,1)} %tokens.1) | copy-start | bytes 2752516
  196.2 4.1 %copy-start.20 = (f32[1024]{0:T(1024)S(1)}, f32[1024]{0:T(1024)}, u32[]{:S(2)}) copy-start(f32[1024]{0:T(1024)} %param.17) | copy-start | bytes 12292
  (1 other events, 0.7 us)
where the time goes:
time: 202 us; the launch traced here: 201 us
  Pallas kernels  67 us (33%)
  waiting for transfers between devices  64.8 us (32%)
  starting transfers between devices  42.6 us (21%)
  local copies, waits for them, and re-layouts  10.5 us (5%)
  blocking collectives  6.33 us (3%)
  other arithmetic  6.23 us (3%)
  matrix products  3.43 us (2%)
    pallas_call x8, Pallas kernels, qkv(): pl.pallas_call(functools.partial(qkv_kernel, len(owns)), out_shape=(out,...  30.6 us
    ppermute x10, waiting for transfers between devices, by_x(): return lax.ppermute(value, 'row', x_swap)  24.6 us
    ppermute x8, waiting for transfers between devices, by_z(): return lax.ppermute(value, 'col', z_next)  19.3 us
    ppermute x8, starting transfers between devices, by_z(): return lax.ppermute(value, 'col', z_next)  13 us
    ppermute x10, starting transfers between devices, by_x(): return lax.ppermute(value, 'row', x_swap)  12.7 us
    pallas_call x2, Pallas kernels, attend(): pl.pallas_call(functools.partial(attend_kernel, tile, windows, group), ou...  11.7 us
    ppermute x6, waiting for transfers between devices, ring_out(): lax.ppermute(outs[i], 'col', ringed[i])  11.4 us
    pallas_call x8, Pallas kernels, turn(): pl.pallas_call(functools.partial(turn_kernel, group, block), out_shape=ja...  10.9 us
  transfers between devices with their start and end apart: 44, of which 20 were waited for; matrix products, arithmetic and copies ran while one was open for 6% of the time, Pallas kernels for 33%

commit v1 on v0

--- a/solution.py
+++ b/solution.py
@@ -15,6 +15,7 @@
 POSITIONS = 32
 MIB = 1024 * 1024
 STAT_ROWS = 16
+LIGHT = 100
 
 
 def rotate(values, row_pos, col_pos):
@@ -191,8 +192,8 @@
         out_specs=(whole(), whole()),
         compiler_params=pltpu.CompilerParams(vmem_limit_bytes=32 * MIB),
         cost_estimate=pl.CostEstimate(
-            flops=4 * rows * depth * columns,
-            bytes_accessed=4 * rows * depth + 4 * depth * columns + 2 * rows * columns,
+            flops=4 * rows * depth * columns // LIGHT,
+            bytes_accessed=(4 * rows * depth + 4 * depth * columns + 2 * rows * columns) // LIGHT,
             transcendentals=0,
         ),
         name="qkv",

time: 202 us -> 202 us (level)
  starting transfers between devices: 42.6 us -> 40.2 us
    ppermute x7, waiting for transfers between devices: 9.33 us -> 11.6 us  [by_y(): return lax.ppermute(value, 'col', y_swap)]
    ppermute x7, starting transfers between devices: 7.34 us -> 5.21 us  [by_y(): return lax.ppermute(value, 'col', y_swap)]
    unnamed x48 -> x50, local copies, waits for them, and re-layouts: 6.84 us -> 7.09 us
  transfers between devices with their start and end apart: 44 -> 44, of which waited for: 20 -> 21; matrix products, arithmetic and copies ran while one was open for 6% -> 6% of each run, Pallas kernels for 33% -> 33%
where the time goes in v1:
time: 202 us; the launch traced here: 201 us
  Pallas kernels  67.3 us (33%)
  waiting for transfers between devices  66 us (33%)
  starting transfers between devices  40.2 us (20%)
  local copies, waits for them, and re-layouts  10.7 us (5%)
  other arithmetic  6.4 us (3%)
  blocking collectives  6.33 us (3%)
  matrix products  3.5 us (2%)
    pallas_call x8, Pallas kernels, qkv(): pl.pallas_call(functools.partial(qkv_kernel, len(owns)), out_shape=(out,...  30.5 us
    ppermute x10, waiting for transfers between devices, by_x(): return lax.ppermute(value, 'row', x_swap)  22.9 us
    ppermute x8, waiting for transfers between devices, by_z(): return lax.ppermute(value, 'col', z_next)  19.4 us
    ppermute x10, starting transfers between devices, by_x(): return lax.ppermute(value, 'row', x_swap)  12.9 us
    ppermute x6, waiting for transfers between devices, ring_out(): lax.ppermute(outs[i], 'col', ringed[i])  11.9 us
    ppermute x8, starting transfers between devices, by_z(): return lax.ppermute(value, 'col', z_next)  11.9 us
    pallas_call x2, Pallas kernels, attend(): pl.pallas_call(functools.partial(attend_kernel, tile, windows, group), ou...  11.8 us
    ppermute x7, waiting for transfers between devices, by_y(): return lax.ppermute(value, 'col', y_swap)  11.6 us
  transfers between devices with their start and end apart: 44, of which 21 were waited for; matrix products, arithmetic and copies ran while one was open for 6% of the time, Pallas kernels for 33%

profile of v1, /device:TPU:0, one launch (start us, length us, event | category | flops | bytes accessed | tf_op | source)
XLA Modules:
  0.0 201.0 jit_solution(13042028959437000928)
XLA Ops:
  0.0 4.0 %collective-permute-start = (bf16[448,1024]{1,0:T(8,128)(2,1)}, bf16[448,1024]{1,0:T(8,128)(2,1)S(1)}, u32[]{:S(2)}, u32[]{:S(2)}) collective-permute-start(bf16[448,1024]{1,0:T(8,128)(2,1)} %tokens.1), channel_id=1, source_target_pairs={{0,4},{1,5},{2,0},{3,1},{4,6},{5,7},{6,2},{7,3},{8,12},{9,13},{10,... | collective-permute-start | bytes 2752520 | tf_op jit(solution)/shard_map/ppermute | solution.py:421
  4.0 1.5 collective-permute-start.1
  5.6 1.6 convert_reduce_fusion
  7.1 6.3 %psum.7 = f32[2,448]{1,0:T(2,128)S(1)} all-reduce(f32[2,448]{1,0:T(2,128)S(1)} %pad_maximum_fusion.1), channel_id=1, replica_groups=mesh['row'=4,'col'=8] {'row'}, use_global_device_ids=true, to_apply=%region_2.3 | all-reduce | flops 896 | bytes 7168 | tf_op jit(solution)/shard_map/psum | solution.py:449
  13.5 1.6 collective-permute-start.2
  15.7 1.5 constant_dynamic-slice_fusion.2
  17.2 1.4 pad_maximum_fusion
  19.3 5.3 %collective-permute-done.2.stats = bf16[16,1024]{1,0:T(8,128)(2,1)S(1)} collective-permute-done((bf16[16,1024]{1,0:T(8,128)(2,1)S(1)}, bf16[16,1024]{1,0:T(8,128)(2,1)S(1)}, u32[]{:S(2)}, u32[]{:S(2)}) %collective-permute-start.2) | collective-permute-done | bytes 32800 | tf_op jit(solution)/shard_map/ppermute | solution.py:421
  24.6 2.2 %collective-permute-done.3.stats = bf16[16,1024]{1,0:T(8,128)(2,1)S(1)} collective-permute-done((bf16[16,1024]{1,0:T(8,128)(2,1)S(1)}, bf16[16,1024]{1,0:T(8,128)(2,1)S(1)}, u32[]{:S(2)}, u32[]{:S(2)}) %collective-permute-start.3) | collective-permute-done | bytes 32800 | tf_op jit(solution)/shard_map/ppermute | solution.py:418
  27.7 1.6 norm.4.refs_0_
  29.3 1.5 collective-permute-start.4
  30.8 1.6 collective-permute-start.5
  32.4 1.6 norm.5.refs_0_
  35.4 3.5 %fusion.2.table = f32[3584,256]{1,0:T(8,128)} fusion(pred[3584,32]{0,1:T(32,128)(4,1)S(1)} %get-tuple-element.208, pred[3584,32]{0,1:T(32,128)(4,1)S(1)} %get-tuple-element.209, f32[32,256]{1,0:T(8,128)S(1)} %concatenate.31, f32[32,256]{1,0:T(8,128)S(1)} %concatenate.30), kind=kOutput, calls=%fused_computation.9 | convolution fusion | flops 704888832 | bytes 3964928 | tf_op jit(solution)/shard_map/dot_general | solution.py:498
  38.9 1.2 copy-done.7
  40.0 3.7 %qkv.8 = (bf16[448,384]{1,0:T(8,128)(2,1)S(1)}, bf16[448,384]{1,0:T(8,128)(2,1)S(1)}) custom-call(s32[4]{0:T(128)S(1)} %pad_add_fusion.heads.slots, bf16[1024,1536]{1,0:T(8,128)(2,1)S(1)} %copy-done.2, bf16[1024,768]{1,0:T(8,128)(2,1)} %collective-permute-done.6.w_peer, bf16[448,1024]{1,0:T(8,128)(2,1)S(1)} %copy-done.7, ...), custom_call_target="tpu_custom_call" | custom-call | flops 14092861 | bytes 56688 | tf_op jit(solution)/shard_map/qkv/pallas_call | solution.py:188
  43.8 1.6 collective-permute-start.8
  46.3 4.0 %qkv.9 = (bf16[448,384]{1,0:T(8,128)(2,1)S(1)}, bf16[448,384]{1,0:T(8,128)(2,1)}) custom-call(s32[4]{0:T(128)S(1)} %pad_add_fusion.heads.slots, bf16[1024,1536]{1,0:T(8,128)(2,1)S(1)} %copy-done.2, bf16[1024,768]{1,0:T(8,128)(2,1)} %collective-permute-done.6.w_peer, bf16[448,1024]{1,0:T(8,128)(2,1)} %norm.4.refs_0_, ...), custom_call_target="tpu_custom_call" | custom-call | flops 14092861 | bytes 56688 | tf_op jit(solution)/shard_map/qkv/pallas_call | solution.py:188
  50.3 2.1 %collective-permute-done.4.refs_0_ = bf16[448,1024]{1,0:T(8,128)(2,1)} collective-permute-done((bf16[448,1024]{1,0:T(8,128)(2,1)}, bf16[448,1024]{1,0:T(8,128)(2,1)}, u32[]{:S(2)}, u32[]{:S(2)}) %collective-permute-start.4) | collective-permute-done | bytes 917536 | tf_op jit(solution)/shard_map/ppermute | solution.py:418
  52.4 1.2 collective-permute-done.5.refs_0_
  54.8 1.8 collective-permute-start.12
  57.1 4.0 %qkv.10 = (bf16[448,384]{1,0:T(8,128)(2,1)S(1)}, bf16[448,384]{1,0:T(8,128)(2,1)}) custom-call(s32[4]{0:T(128)S(1)} %pad_add_fusion.heads.slots, bf16[1024,1536]{1,0:T(8,128)(2,1)S(1)} %copy-done.2, bf16[1024,768]{1,0:T(8,128)(2,1)} %collective-permute-done.6.w_peer, bf16[448,1024]{1,0:T(8,128)(2,1)} %norm.5.refs_0_, ...), custom_call_target="tpu_custom_call" | custom-call | flops 14092861 | bytes 56688 | tf_op jit(solution)/shard_map/qkv/pallas_call | solution.py:188
  61.9 1.5 collective-permute-start.15
  65.5 2.0 %copy-done = f32[3584,256]{1,0:T(8,128)S(1)} copy-done((f32[3584,256]{1,0:T(8,128)S(1)}, f32[3584,256]{1,0:T(8,128)}, u32[]{:S(2)}) %copy-start) | copy-done | bytes 3670040
  69.5 1.3 turn.8.refs_0_
  70.8 3.7 %qkv.12 = (bf16[448,384]{1,0:T(8,128)(2,1)S(1)}, bf16[448,384]{1,0:T(8,128)(2,1)S(1)}) custom-call(s32[4]{0:T(128)S(1)} %pad_add_fusion.heads.slots, bf16[1024,1536]{1,0:T(8,128)(2,1)S(1)} %copy-done.2, bf16[1024,768]{1,0:T(8,128)(2,1)} %collective-permute-done.6.w_peer, bf16[448,1024]{1,0:T(8,128)(2,1)} %collective-permute-done.5.refs_0_, ...), custom_call_target="tpu_custom_call" | custom-call | flops 14092861 | bytes 56688 | tf_op jit(solution)/shard_map/qkv/pallas_call | solution.py:188
  74.6 4.1 %qkv.11 = (bf16[448,384]{1,0:T(8,128)(2,1)S(1)}, bf16[448,384]{1,0:T(8,128)(2,1)S(1)}) custom-call(s32[4]{0:T(128)S(1)} %pad_add_fusion.heads.slots, bf16[1024,1536]{1,0:T(8,128)(2,1)S(1)} %copy-done.2, bf16[1024,768]{1,0:T(8,128)(2,1)} %collective-permute-done.6.w_peer, bf16[448,1024]{1,0:T(8,128)(2,1)} %collective-permute-done.4.refs_0_, ...), custom_call_target="tpu_custom_call" | custom-call | flops 14092861 | bytes 56688 | tf_op jit(solution)/shard_map/qkv/pallas_call | solution.py:188
  81.4 1.5 collective-permute-start.19
  83.4 3.7 %qkv.13 = (bf16[448,384]{1,0:T(8,128)(2,1)S(1)}, bf16[448,384]{1,0:T(8,128)(2,1)S(1)}) custom-call(s32[4]{0:T(128)S(1)} %pad_add_fusion.heads.slots, bf16[1024,1536]{1,0:T(8,128)(2,1)S(1)} %copy-done.2, bf16[1024,768]{1,0:T(8,128)(2,1)} %collective-permute-done.6.w_peer, bf16[448,1024]{1,0:T(8,128)(2,1)} %collective-permute-done.12.refs_0_, ...), custom_call_target="tpu_custom_call" | custom-call | flops 14092861 | bytes 56688 | tf_op jit(solution)/shard_map/qkv/pallas_call | solution.py:188
  87.2 1.6 collective-permute-start.22
  88.8 1.8 turn.9.refs_0_
  90.5 1.8 turn.10.refs_0_
  92.3 3.7 %qkv.14 = (bf16[448,384]{1,0:T(8,128)(2,1)S(1)}, bf16[448,384]{1,0:T(8,128)(2,1)S(1)}) custom-call(s32[4]{0:T(128)S(1)} %pad_add_fusion.heads.slots, bf16[1024,1536]{1,0:T(8,128)(2,1)S(1)} %copy-done.2, bf16[1024,768]{1,0:T(8,128)(2,1)} %collective-permute-done.6.w_peer, bf16[448,1024]{1,0:T(8,128)(2,1)} %collective-permute-done.13.refs_0_, ...), custom_call_target="tpu_custom_call" | custom-call | flops 14092861 | bytes 56688 | tf_op jit(solution)/shard_map/qkv/pallas_call | solution.py:188
  96.0 8.7 %collective-permute-done.11.refs_1_ = bf16[512,1024]{1,0:T(8,128)(2,1)S(1)} collective-permute-done((bf16[512,1024]{1,0:T(8,128)(2,1)S(1)}, bf16[512,1024]{1,0:T(8,128)(2,1)S(1)}, u32[]{:S(2)}, u32[]{:S(2)}) %collective-permute-start.11) | collective-permute-done | bytes 1048608 | tf_op jit(solution)/shard_map/ppermute | solution.py:421
  105.6 1.4 collective-permute-start.27
  107.1 1.5 collective-permute-start.26
  108.6 3.5 %qkv.15 = (bf16[448,384]{1,0:T(8,128)(2,1)S(1)}, bf16[448,384]{1,0:T(8,128)(2,1)S(1)}) custom-call(s32[4]{0:T(128)S(1)} %pad_add_fusion.heads.slots, bf16[1024,1536]{1,0:T(8,128)(2,1)S(1)} %copy-done.2, bf16[1024,768]{1,0:T(8,128)(2,1)} %collective-permute-done.6.w_peer, bf16[448,1024]{1,0:T(8,128)(2,1)S(1)} %collective-permute-done.18.refs_0_, ...), custom_call_target="tpu_custom_call" | custom-call | flops 14092861 | bytes 56688 | tf_op jit(solution)/shard_map/qkv/pallas_call | solution.py:188
  113.9 1.3 turn.11.refs_0_
  115.2 1.3 turn.12.refs_0_
  116.5 1.3 turn.13.refs_0_
  118.0 1.3 turn.14.refs_0_
  119.3 5.2 %collective-permute-done.25.received = bf16[448,384]{1,0:T(8,128)(2,1)S(1)} collective-permute-done((bf16[448,384]{1,0:T(8,128)(2,1)S(1)}, bf16[448,384]{1,0:T(8,128)(2,1)S(1)}, u32[]{:S(2)}, u32[]{:S(2)}) %collective-permute-start.25) | collective-permute-done | bytes 344096 | tf_op jit(solution)/shard_map/ppermute | solution.py:427
  124.5 1.3 turn.15.rows
  125.8 5.7 %attend.2 = (bf16[448,128]{1,0:T(8,128)(2,1)S(1)}, bf16[448,128]{1,0:T(8,128)(2,1)S(1)}, bf16[448,128]{1,0:T(8,128)(2,1)S(1)}, bf16[448,128]{1,0:T(8,128)(2,1)S(1)}) custom-call(s32[16]{0:T(128)S(1)} %fusion.12.places, s32[16]{0:T(128)S(1)} %get-tuple-element.111.lows, s32[16]{0:T(128)S(1)} %get-tuple-element.112.sizes, f32[16,224]{1,0:T(8,128)S(1)} %reshape.16.seg_tiles, ...), custom_call_target="tpu_custom_call" | custom-call | flops 1056964608 | bytes 11927552 | tf_op jit(solution)/shard_map/attend/pallas_call | solution.py:311
  131.6 1.8 collective-permute-start.28
  133.4 2.8 %collective-permute-start.29 = (bf16[448,128]{1,0:T(8,128)(2,1)S(1)}, bf16[448,128]{1,0:T(8,128)(2,1)S(1)}, u32[]{:S(2)}, u32[]{:S(2)}) collective-permute-start(bf16[448,128]{1,0:T(8,128)(2,1)S(1)} %get-tuple-element.164), channel_id=1, source_target_pairs={{0,6},{1,7},{2,4},{3,5},{4,2},{5,3},{6,0},{7,1},{8,14},{9,15},{10,... | collective-permute-start | bytes 344072 | tf_op jit(solution)/shard_map/ppermute | solution.py:587
  136.2 6.0 %attend.3 = (bf16[448,128]{1,0:T(8,128)(2,1)S(1)}, bf16[448,128]{1,0:T(8,128)(2,1)S(1)}, bf16[448,128]{1,0:T(8,128)(2,1)S(1)}, bf16[448,128]{1,0:T(8,128)(2,1)S(1)}) custom-call(s32[16]{0:T(128)S(1)} %fusion.12.places, s32[16]{0:T(128)S(1)} %get-tuple-element.111.lows, s32[16]{0:T(128)S(1)} %get-tuple-element.112.sizes, f32[16,224]{1,0:T(8,128)S(1)} %reshape.16.seg_tiles, ...), custom_call_target="tpu_custom_call" | custom-call | flops 1056964608 | bytes 11927552 | tf_op jit(solution)/shard_map/attend/pallas_call | solution.py:311
  142.7 2.7 %collective-permute-done.30 = bf16[448,128]{1,0:T(8,128)(2,1)S(1)} collective-permute-done((bf16[448,128]{1,0:T(8,128)(2,1)S(1)}, bf16[448,128]{1,0:T(8,128)(2,1)S(1)}, u32[]{:S(2)}, u32[]{:S(2)}) %collective-permute-start.30) | collective-permute-done | bytes 114720 | tf_op jit(solution)/shard_map/ppermute | solution.py:587
  145.7 1.6 collective-permute-start.31
  147.3 10.0 %collective-permute-done.31.refs_4_.refs_2_ = bf16[448,512]{1,0:T(8,128)(2,1)S(1)} collective-permute-done((bf16[448,512]{1,0:T(8,128)(2,1)S(1)}, bf16[448,512]{1,0:T(8,128)(2,1)S(1)}, u32[]{:S(2)}, u32[]{:S(2)}) %collective-permute-start.31) | collective-permute-done | bytes 458784 | tf_op jit(solution)/shard_map/ppermute | solution.py:427
  157.3 1.2 collective-permute-done.33.refs_0_
  158.5 1.6 collective-permute-start.34
  160.1 2.1 %collective-permute-start.35 = (bf16[448,128]{1,0:T(8,128)(2,1)S(1)}, bf16[448,128]{1,0:T(8,128)(2,1)S(1)}, u32[]{:S(2)}, u32[]{:S(2)}) collective-permute-start(bf16[448,128]{1,0:T(8,128)(2,1)S(1)} %get-tuple-element.183), channel_id=1, source_target_pairs={{0,6},{1,7},{2,4},{3,5},{4,2},{5,3},{6,0},{7,1},{8,14},{9,15},{10,... | collective-permute-start | bytes 344072 | tf_op jit(solution)/shard_map/ppermute | solution.py:587
  162.3 1.2 collective-permute-done.34
  163.5 4.8 %collective-permute-done.35 = bf16[448,128]{1,0:T(8,128)(2,1)S(1)} collective-permute-done((bf16[448,128]{1,0:T(8,128)(2,1)S(1)}, bf16[448,128]{1,0:T(8,128)(2,1)S(1)}, u32[]{:S(2)}, u32[]{:S(2)}) %collective-permute-start.35) | collective-permute-done | bytes 114720 | tf_op jit(solution)/shard_map/ppermute | solution.py:587
  168.4 2.7 %collective-permute-done.36 = bf16[448,128]{1,0:T(8,128)(2,1)S(1)} collective-permute-done((bf16[448,128]{1,0:T(8,128)(2,1)S(1)}, bf16[448,128]{1,0:T(8,128)(2,1)S(1)}, u32[]{:S(2)}, u32[]{:S(2)}) %collective-permute-start.36) | collective-permute-done | bytes 114720 | tf_op jit(solution)/shard_map/ppermute | solution.py:587
  171.1 1.6 collective-permute-start.37
  173.0 2.8 %project.8.refs_5_ = f32[448,1024]{1,0:T(8,128)S(1)} custom-call(s32[4]{0:T(128)S(1)} %pad_add_fusion.heads.slots, bf16[512,1024]{1,0:T(8,128)(2,1)S(1)} %copy-done.5, bf16[512,1024]{1,0:T(8,128)(2,1)S(1)} %collective-permute-done.11.refs_1_, bf16[512,1024]{1,0:T(8,128)(2,1)S(1)} %collective-permute-done.27.refs_2_, ...), custom_call_target="tpu_custom_call" | custom-call | flops 1409286144 | bytes 6356992 | tf_op jit(solution)/shard_map/project/pallas_call | solution.py:373
  177.1 5.6 %collective-permute-done.37.refs_4_.refs_2_ = bf16[448,512]{1,0:T(8,128)(2,1)S(1)} collective-permute-done((bf16[448,512]{1,0:T(8,128)(2,1)S(1)}, bf16[448,512]{1,0:T(8,128)(2,1)S(1)}, u32[]{:S(2)}, u32[]{:S(2)}) %collective-permute-start.37) | collective-permute-done | bytes 458784 | tf_op jit(solution)/shard_map/ppermute | solution.py:427
  182.6 3.0 %collective-permute-done.42.refs_0_ = bf16[512,512]{1,0:T(8,128)(2,1)S(1)} collective-permute-done((bf16[512,512]{1,0:T(8,128)(2,1)S(1)}, bf16[512,512]{1,0:T(8,128)(2,1)S(1)}, u32[]{:S(2)}, u32[]{:S(2)}) %collective-permute-start.42) | collective-permute-done | bytes 524320 | tf_op jit(solution)/shard_map/ppermute | solution.py:421
  185.6 2.6 %collective-permute-done.41 = bf16[448,512]{1,0:T(8,128)(2,1)S(1)} collective-permute-done((bf16[448,512]{1,0:T(8,128)(2,1)S(1)}, bf16[448,512]{1,0:T(8,128)(2,1)S(1)}, u32[]{:S(2)}, u32[]{:S(2)}) %collective-permute-start.41) | collective-permute-done | bytes 458784 | tf_op jit(solution)/shard_map/ppermute | solution.py:418
  189.7 2.8 %project.6.refs_5_ = f32[448,1024]{1,0:T(8,128)S(1)} custom-call(s32[4]{0:T(128)S(1)} %pad_add_fusion.heads.slots, bf16[512,1024]{1,0:T(8,128)(2,1)S(1)} %copy-done.5, bf16[512,1024]{1,0:T(8,128)(2,1)S(1)} %collective-permute-done.11.refs_1_, bf16[512,1024]{1,0:T(8,128)(2,1)S(1)} %collective-permute-done.27.refs_2_, ...), custom_call_target="tpu_custom_call" | custom-call | flops 1409286144 | bytes 6356992 | tf_op jit(solution)/shard_map/project/pallas_call | solution.py:373
  194.8 4.8 %collective-permute-done.43 = bf16[448,512]{1,0:T(8,128)(2,1)S(1)} collective-permute-done((bf16[448,512]{1,0:T(8,128)(2,1)S(1)}, bf16[448,512]{1,0:T(8,128)(2,1)S(1)}, u32[]{:S(2)}, u32[]{:S(2)}) %collective-permute-start.43) | collective-permute-done | bytes 458784 | tf_op jit(solution)/shard_map/ppermute | solution.py:418
  199.8 1.2 fusion.1
  (133 shorter events, 23.6 us)
Async XLA Ops:
  0.0 26.8 %collective-permute-start = (bf16[448,1024]{1,0:T(8,128)(2,1)}, bf16[448,1024]{1,0:T(8,128)(2,1)S(1)}, u32[]{:S(2)}, u32[]{:S(2)}) collective-permute-start(bf16[448,1024]{1,0:T(8,128)(2,1)} %tokens.1), channel_id=1, source_target_pairs={{0,4},{1,5},{2,0},{3,1},{4,6},{5,7},{6,2},{7,3},{8,12},{9,13},{10,... | collective-permute-start | bytes 2752520 | tf_op jit(solution)/shard_map/ppermute | solution.py:421
  4.0 22.7 %collective-permute-start.1 = (bf16[448,1024]{1,0:T(8,128)(2,1)}, bf16[448,1024]{1,0:T(8,128)(2,1)S(1)}, u32[]{:S(2)}, u32[]{:S(2)}) collective-permute-start(bf16[448,1024]{1,0:T(8,128)(2,1)} %tokens.1), channel_id=1, source_target_pairs={{0,1},{1,0},{2,3},{3,2},{4,5},{5,4},{6,7},{7,6},{8,9},{9,8},{10,11... | collective-permute-start | bytes 2752520 | tf_op jit(solution)/shard_map/ppermute | solution.py:418
  13.5 11.0 %collective-permute-start.2 = (bf16[16,1024]{1,0:T(8,128)(2,1)S(1)}, bf16[16,1024]{1,0:T(8,128)(2,1)S(1)}, u32[]{:S(2)}, u32[]{:S(2)}) collective-permute-start(bf16[16,1024]{1,0:T(8,128)(2,1)S(1)} %pack.1.stats), channel_id=1, source_target_pairs={{0,4},{1,5},{2,0},{3,1},{4,6},{5,7},{6,2},{7,3},{8,12},{9,13},{10,... | collective-permute-start | bytes 98312 | tf_op jit(solution)/shard_map/ppermute | solution.py:421
  15.2 11.6 %collective-permute-start.3 = (bf16[16,1024]{1,0:T(8,128)(2,1)S(1)}, bf16[16,1024]{1,0:T(8,128)(2,1)S(1)}, u32[]{:S(2)}, u32[]{:S(2)}) collective-permute-start(bf16[16,1024]{1,0:T(8,128)(2,1)S(1)} %pack.1.stats), channel_id=1, source_target_pairs={{0,1},{1,0},{2,3},{3,2},{4,5},{5,4},{6,7},{7,6},{8,9},{9,8},{10,11... | collective-permute-start | bytes 98312 | tf_op jit(solution)/shard_map/ppermute | solution.py:418
  17.2 1.4 copy-start.3
  17.2 1.4 copy-start.16
  17.2 1.4 copy-start.17
  19.3 14.7 %copy-start.6 = (bf16[448,1024]{1,0:T(8,128)(2,1)}, bf16[448,1024]{1,0:T(8,128)(2,1)S(1)}, u32[]{:S(2)}) copy-start(bf16[448,1024]{1,0:T(8,128)(2,1)S(1)} %norm.3.refs_0_) | copy-start | bytes 2752516
  26.8 7.3 %collective-permute-start.7 = (bf16[448,1024]{1,0:T(8,128)(2,1)S(1)}, bf16[448,1024]{1,0:T(8,128)(2,1)}, u32[]{:S(2)}, u32[]{:S(2)}) collective-permute-start(bf16[448,1024]{1,0:T(8,128)(2,1)S(1)} %norm.3.refs_0_), channel_id=1, source_target_pairs={{0,8},{8,0},{16,24},{24,16},{1,9},{9,1},{17,25},{25,17},{2,10},{10... | collective-permute-start | bytes 2752520 | tf_op jit(solution)/shard_map/ppermute | solution.py:424
  26.9 12.0 %collective-permute-start.6 = (bf16[1024,768]{1,0:T(8,128)(2,1)}, bf16[1024,768]{1,0:T(8,128)(2,1)}, u32[]{:S(2)}, u32[]{:S(2)}) collective-permute-start(bf16[1024,768]{1,0:T(8,128)(2,1)} %pad_maximum_fusion), channel_id=1, source_target_pairs={{0,8},{8,0},{16,24},{24,16},{1,9},{9,1},{17,25},{25,17},{2,10},{10... | collective-permute-start | bytes 4718600 | tf_op jit(solution)/shard_map/ppermute | solution.py:424
  27.7 6.3 %copy-start.19 = (s32[2,3584]{1,0:T(2,128)S(1)}, s32[2,3584]{1,0:T(2,128)}, u32[]{:S(2)}) copy-start(s32[2,3584]{1,0:T(2,128)} %param.20) | copy-start | bytes 86020
  27.7 6.6 %copy-start.18 = (s32[3584]{0:T(1024)S(1)}, s32[3584]{0:T(1024)}, u32[]{:S(2)}) copy-start(s32[3584]{0:T(1024)} %param.18) | copy-start | bytes 43012
  27.7 6.6 %copy-start.20 = (s32[3584]{0:T(1024)S(1)}, s32[3584]{0:T(1024)}, u32[]{:S(2)}) copy-start(s32[3584]{0:T(1024)} %param.19) | copy-start | bytes 43012
  29.3 17.0 %collective-permute-start.10 = (bf16[448,1024]{1,0:T(8,128)(2,1)}, bf16[448,1024]{1,0:T(8,128)(2,1)}, u32[]{:S(2)}, u32[]{:S(2)}) collective-permute-start(bf16[448,1024]{1,0:T(8,128)(2,1)} %norm.4.refs_0_), channel_id=1, source_target_pairs={{0,8},{8,0},{16,24},{24,16},{1,9},{9,1},{17,25},{25,17},{2,10},{10... | collective-permute-start | bytes 2752520 | tf_op jit(solution)/shard_map/ppermute | solution.py:424
  29.3 23.1 %collective-permute-start.4 = (bf16[448,1024]{1,0:T(8,128)(2,1)}, bf16[448,1024]{1,0:T(8,128)(2,1)}, u32[]{:S(2)}, u32[]{:S(2)}) collective-permute-start(bf16[448,1024]{1,0:T(8,128)(2,1)} %norm.4.refs_0_), channel_id=1, source_target_pairs={{0,1},{1,0},{2,3},{3,2},{4,5},{5,4},{6,7},{7,6},{8,9},{9,8},{10,11... | collective-permute-start | bytes 2752520 | tf_op jit(solution)/shard_map/ppermute | solution.py:418
  30.8 22.8 %collective-permute-start.5 = (bf16[448,1024]{1,0:T(8,128)(2,1)}, bf16[448,1024]{1,0:T(8,128)(2,1)}, u32[]{:S(2)}, u32[]{:S(2)}) collective-permute-start(bf16[448,1024]{1,0:T(8,128)(2,1)} %norm.4.refs_0_), channel_id=1, source_target_pairs={{0,4},{1,5},{2,0},{3,1},{4,6},{5,7},{6,2},{7,3},{8,12},{9,13},{10,... | collective-permute-start | bytes 2752520 | tf_op jit(solution)/shard_map/ppermute | solution.py:421
  34.1 16.2 %collective-permute-start.9 = (bf16[448,1024]{1,0:T(8,128)(2,1)}, bf16[448,1024]{1,0:T(8,128)(2,1)}, u32[]{:S(2)}, u32[]{:S(2)}) collective-permute-start(bf16[448,1024]{1,0:T(8,128)(2,1)} %norm.5.refs_0_), channel_id=1, source_target_pairs={{0,8},{8,0},{16,24},{24,16},{1,9},{9,1},{17,25},{25,17},{2,10},{10... | collective-permute-start | bytes 2752520 | tf_op jit(solution)/shard_map/ppermute | solution.py:424
  35.3 3.5 %copy-start.2 = (bf16[1024,1536]{1,0:T(8,128)(2,1)S(1)}, bf16[1024,1536]{1,0:T(8,128)(2,1)}, u32[]{:S(2)}) copy-start(bf16[1024,1536]{1,0:T(8,128)(2,1)} %w_own.15) | copy-start | bytes 9437188
  38.9 1.2 copy-start.7
  43.8 6.5 %copy-start.12 = (bf16[448,384]{1,0:T(8,128)(2,1)}, bf16[448,384]{1,0:T(8,128)(2,1)S(1)}, u32[]{:S(2)}) copy-start(bf16[448,384]{1,0:T(8,128)(2,1)S(1)} %get-tuple-element.122.kept) | copy-start | bytes 1032196
  43.8 10.5 %collective-permute-start.8 = (bf16[448,384]{1,0:T(8,128)(2,1)S(1)}, bf16[448,384]{1,0:T(8,128)(2,1)S(1)}, u32[]{:S(2)}, u32[]{:S(2)}) collective-permute-start(bf16[448,384]{1,0:T(8,128)(2,1)S(1)} %get-tuple-element.103), channel_id=1, source_target_pairs={{0,16},{8,24},{16,0},{24,8},{1,17},{9,25},{17,1},{25,9},{2,18},{10... | collective-permute-start | bytes 1032200 | tf_op jit(solution)/shard_map/ppermute | solution.py:427
  54.3 6.8 %copy-start.14 = (bf16[448,384]{1,0:T(8,128)(2,1)}, bf16[448,384]{1,0:T(8,128)(2,1)S(1)}, u32[]{:S(2)}) copy-start(bf16[448,384]{1,0:T(8,128)(2,1)S(1)} %collective-permute-done.8.received) | copy-start | bytes 1032196
  54.3 9.0 %collective-permute-start.17 = (bf16[448,1024]{1,0:T(8,128)(2,1)}, bf16[448,1024]{1,0:T(8,128)(2,1)S(1)}, u32[]{:S(2)}, u32[]{:S(2)}) collective-permute-start(bf16[448,1024]{1,0:T(8,128)(2,1)} %collective-permute-done.5.refs_0_), channel_id=1, source_target_pairs={{0,8},{8,0},{16,24},{24,16},{1,9},{9,1},{17,25},{25,17},{2,10},{10... | collective-permute-start | bytes 2752520 | tf_op jit(solution)/shard_map/ppermute | solution.py:424
  54.3 20.3 %collective-permute-start.16 = (bf16[448,1024]{1,0:T(8,128)(2,1)}, bf16[448,1024]{1,0:T(8,128)(2,1)}, u32[]{:S(2)}, u32[]{:S(2)}) collective-permute-start(bf16[448,1024]{1,0:T(8,128)(2,1)} %collective-permute-done.4.refs_0_), channel_id=1, source_target_pairs={{0,8},{8,0},{16,24},{24,16},{1,9},{9,1},{17,25},{25,17},{2,10},{10... | collective-permute-start | bytes 2752520 | tf_op jit(solution)/shard_map/ppermute | solution.py:424
  54.8 24.2 %collective-permute-start.12 = (bf16[448,1024]{1,0:T(8,128)(2,1)}, bf16[448,1024]{1,0:T(8,128)(2,1)}, u32[]{:S(2)}, u32[]{:S(2)}) collective-permute-start(bf16[448,1024]{1,0:T(8,128)(2,1)} %collective-permute-done.5.refs_0_), channel_id=1, source_target_pairs={{0,4},{1,5},{2,0},{3,1},{4,6},{5,7},{6,2},{7,3},{8,12},{9,13},{10,... | collective-permute-start | bytes 2752520 | tf_op jit(solution)/shard_map/ppermute | solution.py:421
  56.6 22.4 %collective-permute-start.13 = (bf16[448,1024]{1,0:T(8,128)(2,1)}, bf16[448,1024]{1,0:T(8,128)(2,1)}, u32[]{:S(2)}, u32[]{:S(2)}) collective-permute-start(bf16[448,1024]{1,0:T(8,128)(2,1)} %collective-permute-done.5.refs_0_), channel_id=1, source_target_pairs={{0,1},{1,0},{2,3},{3,2},{4,5},{5,4},{6,7},{7,6},{8,9},{9,8},{10,11... | collective-permute-start | bytes 2752520 | tf_op jit(solution)/shard_map/ppermute | solution.py:418
  61.9 16.8 %collective-permute-start.15 = (bf16[448,384]{1,0:T(8,128)(2,1)}, bf16[448,384]{1,0:T(8,128)(2,1)}, u32[]{:S(2)}, u32[]{:S(2)}) collective-permute-start(bf16[448,384]{1,0:T(8,128)(2,1)} %get-tuple-element.121), channel_id=1, source_target_pairs={{0,16},{8,24},{16,0},{24,8},{1,17},{9,25},{17,1},{25,9},{2,18},{10... | collective-permute-start | bytes 1032200 | tf_op jit(solution)/shard_map/ppermute | solution.py:427
  64.3 14.7 %collective-permute-start.14 = (bf16[448,384]{1,0:T(8,128)(2,1)}, bf16[448,384]{1,0:T(8,128)(2,1)}, u32[]{:S(2)}, u32[]{:S(2)}) collective-permute-start(bf16[448,384]{1,0:T(8,128)(2,1)} %get-tuple-element.117), channel_id=1, source_target_pairs={{0,16},{8,24},{16,0},{24,8},{1,17},{9,25},{17,1},{25,9},{2,18},{10... | collective-permute-start | bytes 1032200 | tf_op jit(solution)/shard_map/ppermute | solution.py:427
  65.5 2.0 %copy-start = (f32[3584,256]{1,0:T(8,128)S(1)}, f32[3584,256]{1,0:T(8,128)}, u32[]{:S(2)}) copy-start(f32[3584,256]{1,0:T(8,128)} %fusion.2.table) | copy-start | bytes 11010052
  67.5 1.0 copy-start.13
  68.5 1.0 copy-start.15
  69.5 1.3 copy-start.9
  74.6 5.0 %copy-start.5 = (bf16[512,1024]{1,0:T(8,128)(2,1)S(1)}, bf16[512,1024]{1,0:T(8,128)(2,1)}, u32[]{:S(2)}) copy-start(bf16[512,1024]{1,0:T(8,128)(2,1)} %refs_0_.3) | copy-start | bytes 3145732
  79.0 9.7 %copy-start.1 = (f32[3584,256]{1,0:T(8,128)S(1)}, f32[3584,256]{1,0:T(8,128)}, u32[]{:S(2)}) copy-start(f32[3584,256]{1,0:T(8,128)} %fusion.2.table) | copy-start | bytes 11010052
  79.0 3.9 %collective-permute-start.21 = (bf16[448,1024]{1,0:T(8,128)(2,1)}, bf16[448,1024]{1,0:T(8,128)(2,1)S(1)}, u32[]{:S(2)}, u32[]{:S(2)}) collective-permute-start(bf16[448,1024]{1,0:T(8,128)(2,1)} %collective-permute-done.12.refs_0_), channel_id=1, source_target_pairs={{0,8},{8,0},{16,24},{24,16},{1,9},{9,1},{17,25},{25,17},{2,10},{10... | collective-permute-start | bytes 2752520 | tf_op jit(solution)/shard_map/ppermute | solution.py:424
  79.1 8.1 %collective-permute-start.23 = (bf16[448,1024]{1,0:T(8,128)(2,1)}, bf16[448,1024]{1,0:T(8,128)(2,1)S(1)}, u32[]{:S(2)}, u32[]{:S(2)}) collective-permute-start(bf16[448,1024]{1,0:T(8,128)(2,1)} %collective-permute-done.13.refs_0_), channel_id=1, source_target_pairs={{0,8},{8,0},{16,24},{24,16},{1,9},{9,1},{17,25},{25,17},{2,10},{10... | collective-permute-start | bytes 2752520 | tf_op jit(solution)/shard_map/ppermute | solution.py:424
  79.6 25.1 %collective-permute-start.11 = (bf16[512,1024]{1,0:T(8,128)(2,1)S(1)}, bf16[512,1024]{1,0:T(8,128)(2,1)S(1)}, u32[]{:S(2)}, u32[]{:S(2)}) collective-permute-start(bf16[512,1024]{1,0:T(8,128)(2,1)S(1)} %copy-done.5), channel_id=1, source_target_pairs={{0,4},{1,5},{2,0},{3,1},{4,6},{5,7},{6,2},{7,3},{8,12},{9,13},{10,... | collective-permute-start | bytes 3145736 | tf_op jit(solution)/shard_map/ppermute | solution.py:421
  80.7 24.1 %collective-permute-start.18 = (bf16[448,1024]{1,0:T(8,128)(2,1)}, bf16[448,1024]{1,0:T(8,128)(2,1)S(1)}, u32[]{:S(2)}, u32[]{:S(2)}) collective-permute-start(bf16[448,1024]{1,0:T(8,128)(2,1)} %collective-permute-done.12.refs_0_), channel_id=1, source_target_pairs={{0,1},{1,0},{2,3},{3,2},{4,5},{5,4},{6,7},{7,6},{8,9},{9,8},{10,11... | collective-permute-start | bytes 2752520 | tf_op jit(solution)/shard_map/ppermute | solution.py:418
  81.4 23.3 %collective-permute-start.19 = (bf16[448,384]{1,0:T(8,128)(2,1)S(1)}, bf16[448,384]{1,0:T(8,128)(2,1)S(1)}, u32[]{:S(2)}, u32[]{:S(2)}) collective-permute-start(bf16[448,384]{1,0:T(8,128)(2,1)S(1)} %get-tuple-element.132), channel_id=1, source_target_pairs={{0,16},{8,24},{16,0},{24,8},{1,17},{9,25},{17,1},{25,9},{2,18},{10... | collective-permute-start | bytes 1032200 | tf_op jit(solution)/shard_map/ppermute | solution.py:427
  82.9 21.9 %collective-permute-start.20 = (bf16[448,384]{1,0:T(8,128)(2,1)S(1)}, bf16[448,384]{1,0:T(8,128)(2,1)S(1)}, u32[]{:S(2)}, u32[]{:S(2)}) collective-permute-start(bf16[448,384]{1,0:T(8,128)(2,1)S(1)} %get-tuple-element.134), channel_id=1, source_target_pairs={{0,16},{8,24},{16,0},{24,8},{1,17},{9,25},{17,1},{25,9},{2,18},{10... | collective-permute-start | bytes 1032200 | tf_op jit(solution)/shard_map/ppermute | solution.py:427
  87.2 3.3 %copy-start.11 = (bf16[448,384]{1,0:T(8,128)(2,1)S(1)}, bf16[448,384]{1,0:T(8,128)(2,1)}, u32[]{:S(2)}) copy-start(bf16[448,384]{1,0:T(8,128)(2,1)} %copy-done.10) | copy-start | bytes 1032196
  87.2 18.4 %collective-permute-start.22 = (bf16[448,384]{1,0:T(8,128)(2,1)S(1)}, bf16[448,384]{1,0:T(8,128)(2,1)S(1)}, u32[]{:S(2)}, u32[]{:S(2)}) collective-permute-start(bf16[448,384]{1,0:T(8,128)(2,1)S(1)} %get-tuple-element.136), channel_id=1, source_target_pairs={{0,16},{8,24},{16,0},{24,8},{1,17},{9,25},{17,1},{25,9},{2,18},{10... | collective-permute-start | bytes 1032200 | tf_op jit(solution)/shard_map/ppermute | solution.py:427
  105.6 2.9 %collective-permute-start.24 = (bf16[448,1024]{1,0:T(8,128)(2,1)S(1)}, bf16[448,1024]{1,0:T(8,128)(2,1)S(1)}, u32[]{:S(2)}, u32[]{:S(2)}) collective-permute-start(bf16[448,1024]{1,0:T(8,128)(2,1)S(1)} %collective-permute-done.18.refs_0_), channel_id=1, source_target_pairs={{0,8},{8,0},{16,24},{24,16},{1,9},{9,1},{17,25},{25,17},{2,10},{10... | collective-permute-start | bytes 2752520 | tf_op jit(solution)/shard_map/ppermute | solution.py:424
  105.6 25.9 %collective-permute-start.27 = (bf16[512,1024]{1,0:T(8,128)(2,1)S(1)}, bf16[512,1024]{1,0:T(8,128)(2,1)S(1)}, u32[]{:S(2)}, u32[]{:S(2)}) collective-permute-start(bf16[512,1024]{1,0:T(8,128)(2,1)S(1)} %collective-permute-done.11.refs_1_), channel_id=1, source_target_pairs={{0,4},{1,5},{2,0},{3,1},{4,6},{5,7},{6,2},{7,3},{8,12},{9,13},{10,... | collective-permute-start | bytes 3145736 | tf_op jit(solution)/shard_map/ppermute | solution.py:421
  107.1 10.9 %collective-permute-start.26 = (bf16[448,384]{1,0:T(8,128)(2,1)S(1)}, bf16[448,384]{1,0:T(8,128)(2,1)S(1)}, u32[]{:S(2)}, u32[]{:S(2)}) collective-permute-start(bf16[448,384]{1,0:T(8,128)(2,1)S(1)} %get-tuple-element.149), channel_id=1, source_target_pairs={{0,16},{8,24},{16,0},{24,8},{1,17},{9,25},{17,1},{25,9},{2,18},{10... | collective-permute-start | bytes 1032200 | tf_op jit(solution)/shard_map/ppermute | solution.py:427
  112.1 12.4 %collective-permute-start.25 = (bf16[448,384]{1,0:T(8,128)(2,1)S(1)}, bf16[448,384]{1,0:T(8,128)(2,1)S(1)}, u32[]{:S(2)}, u32[]{:S(2)}) collective-permute-start(bf16[448,384]{1,0:T(8,128)(2,1)S(1)} %get-tuple-element.147), channel_id=1, source_target_pairs={{0,16},{8,24},{16,0},{24,8},{1,17},{9,25},{17,1},{25,9},{2,18},{10... | collective-permute-start | bytes 1032200 | tf_op jit(solution)/shard_map/ppermute | solution.py:427
  131.6 10.7 %collective-permute-start.28 = (bf16[448,128]{1,0:T(8,128)(2,1)S(1)}, bf16[448,128]{1,0:T(8,128)(2,1)S(1)}, u32[]{:S(2)}, u32[]{:S(2)}) collective-permute-start(bf16[448,128]{1,0:T(8,128)(2,1)S(1)} %get-tuple-element.163), channel_id=1, source_target_pairs={{0,4},{1,5},{2,0},{3,1},{4,6},{5,7},{6,2},{7,3},{8,12},{9,13},{10,... | collective-permute-start | bytes 344072 | tf_op jit(solution)/shard_map/ppermute | solution.py:587
  133.4 9.3 %collective-permute-start.29 = (bf16[448,128]{1,0:T(8,128)(2,1)S(1)}, bf16[448,128]{1,0:T(8,128)(2,1)S(1)}, u32[]{:S(2)}, u32[]{:S(2)}) collective-permute-start(bf16[448,128]{1,0:T(8,128)(2,1)S(1)} %get-tuple-element.164), channel_id=1, source_target_pairs={{0,6},{1,7},{2,4},{3,5},{4,2},{5,3},{6,0},{7,1},{8,14},{9,15},{10,... | collective-permute-start | bytes 344072 | tf_op jit(solution)/shard_map/ppermute | solution.py:587
  136.2 9.2 %collective-permute-start.30 = (bf16[448,128]{1,0:T(8,128)(2,1)S(1)}, bf16[448,128]{1,0:T(8,128)(2,1)S(1)}, u32[]{:S(2)}, u32[]{:S(2)}) collective-permute-start(bf16[448,128]{1,0:T(8,128)(2,1)S(1)} %get-tuple-element.165), channel_id=1, source_target_pairs={{0,2},{1,3},{2,6},{3,7},{4,0},{5,1},{6,4},{7,5},{8,10},{9,11},{10,... | collective-permute-start | bytes 344072 | tf_op jit(solution)/shard_map/ppermute | solution.py:587
  145.5 13.0 %collective-permute-start.33 = (bf16[512,512]{1,0:T(8,128)(2,1)S(1)}, bf16[512,512]{1,0:T(8,128)(2,1)S(1)}, u32[]{:S(2)}, u32[]{:S(2)}) collective-permute-start(bf16[512,512]{1,0:T(8,128)(2,1)S(1)} %slice.22), channel_id=1, source_target_pairs={{0,4},{1,5},{2,0},{3,1},{4,6},{5,7},{6,2},{7,3},{8,12},{9,13},{10,... | collective-permute-start | bytes 1572872 | tf_op jit(solution)/shard_map/ppermute | solution.py:421
  145.7 11.6 %collective-permute-start.31 = (bf16[448,512]{1,0:T(8,128)(2,1)S(1)}, bf16[448,512]{1,0:T(8,128)(2,1)S(1)}, u32[]{:S(2)}, u32[]{:S(2)}) collective-permute-start(bf16[448,512]{1,0:T(8,128)(2,1)S(1)} %constant_dynamic-update-slice_fusion.refs_3_.refs_1_), channel_id=1, source_target_pairs={{0,16},{8,24},{16,0},{24,8},{1,17},{9,25},{17,1},{25,9},{2,18},{10... | collective-permute-start | bytes 1376264 | tf_op jit(solution)/shard_map/ppermute | solution.py:427
  147.3 10.0 %collective-permute-start.32 = (bf16[448,512]{1,0:T(8,128)(2,1)S(1)}, bf16[448,512]{1,0:T(8,128)(2,1)S(1)}, u32[]{:S(2)}, u32[]{:S(2)}) collective-permute-start(bf16[448,512]{1,0:T(8,128)(2,1)S(1)} %constant_dynamic-update-slice_fusion.refs_3_.refs_1_), channel_id=1, source_target_pairs={{0,8},{8,0},{16,24},{24,16},{1,9},{9,1},{17,25},{25,17},{2,10},{10... | collective-permute-start | bytes 1376264 | tf_op jit(solution)/shard_map/ppermute | solution.py:424
  158.5 5.0 %collective-permute-start.34 = (bf16[448,128]{1,0:T(8,128)(2,1)S(1)}, bf16[448,128]{1,0:T(8,128)(2,1)S(1)}, u32[]{:S(2)}, u32[]{:S(2)}) collective-permute-start(bf16[448,128]{1,0:T(8,128)(2,1)S(1)} %get-tuple-element.182), channel_id=1, source_target_pairs={{0,4},{1,5},{2,0},{3,1},{4,6},{5,7},{6,2},{7,3},{8,12},{9,13},{10,... | collective-permute-start | bytes 344072 | tf_op jit(solution)/shard_map/ppermute | solution.py:587
  160.1 8.2 %collective-permute-start.35 = (bf16[448,128]{1,0:T(8,128)(2,1)S(1)}, bf16[448,128]{1,0:T(8,128)(2,1)S(1)}, u32[]{:S(2)}, u32[]{:S(2)}) collective-permute-start(bf16[448,128]{1,0:T(8,128)(2,1)S(1)} %get-tuple-element.183), channel_id=1, source_target_pairs={{0,6},{1,7},{2,4},{3,5},{4,2},{5,3},{6,0},{7,1},{8,14},{9,15},{10,... | collective-permute-start | bytes 344072 | tf_op jit(solution)/shard_map/ppermute | solution.py:587
  162.2 8.8 %collective-permute-start.36 = (bf16[448,128]{1,0:T(8,128)(2,1)S(1)}, bf16[448,128]{1,0:T(8,128)(2,1)S(1)}, u32[]{:S(2)}, u32[]{:S(2)}) collective-permute-start(bf16[448,128]{1,0:T(8,128)(2,1)S(1)} %get-tuple-element.184), channel_id=1, source_target_pairs={{0,2},{1,3},{2,6},{3,7},{4,0},{5,1},{6,4},{7,5},{8,10},{9,11},{10,... | collective-permute-start | bytes 344072 | tf_op jit(solution)/shard_map/ppermute | solution.py:587
  162.2 10.8 %collective-permute-start.40 = (bf16[448,512]{1,0:T(8,128)(2,1)S(1)}, bf16[448,512]{1,0:T(8,128)(2,1)S(1)}, u32[]{:S(2)}, u32[]{:S(2)}) collective-permute-start(bf16[448,512]{1,0:T(8,128)(2,1)S(1)} %collective-permute-done.31.refs_4_.refs_2_), channel_id=1, source_target_pairs={{0,8},{8,0},{16,24},{24,16},{1,9},{9,1},{17,25},{25,17},{2,10},{10... | collective-permute-start | bytes 1376264 | tf_op jit(solution)/shard_map/ppermute | solution.py:424
  171.1 11.5 %collective-permute-start.37 = (bf16[448,512]{1,0:T(8,128)(2,1)S(1)}, bf16[448,512]{1,0:T(8,128)(2,1)S(1)}, u32[]{:S(2)}, u32[]{:S(2)}) collective-permute-start(bf16[448,512]{1,0:T(8,128)(2,1)S(1)} %constant_dynamic-update-slice_fusion.4.refs_3_.refs_1_), channel_id=1, source_target_pairs={{0,16},{8,24},{16,0},{24,8},{1,17},{9,25},{17,1},{25,9},{2,18},{10... | collective-permute-start | bytes 1376264 | tf_op jit(solution)/shard_map/ppermute | solution.py:427
  172.7 12.9 %collective-permute-start.42 = (bf16[512,512]{1,0:T(8,128)(2,1)S(1)}, bf16[512,512]{1,0:T(8,128)(2,1)S(1)}, u32[]{:S(2)}, u32[]{:S(2)}) collective-permute-start(bf16[512,512]{1,0:T(8,128)(2,1)S(1)} %slice.23), channel_id=1, source_target_pairs={{0,4},{1,5},{2,0},{3,1},{4,6},{5,7},{6,2},{7,3},{8,12},{9,13},{10,... | collective-permute-start | bytes 1572872 | tf_op jit(solution)/shard_map/ppermute | solution.py:421
  176.9 11.3 %collective-permute-start.41 = (bf16[448,512]{1,0:T(8,128)(2,1)S(1)}, bf16[448,512]{1,0:T(8,128)(2,1)S(1)}, u32[]{:S(2)}, u32[]{:S(2)}) collective-permute-start(bf16[448,512]{1,0:T(8,128)(2,1)S(1)} %project.9), channel_id=1, source_target_pairs={{0,1},{1,0},{2,3},{3,2},{4,5},{5,4},{6,7},{7,6},{8,9},{9,8},{10,11... | collective-permute-start | bytes 1376264 | tf_op jit(solution)/shard_map/ppermute | solution.py:418
  177.0 12.7 %collective-permute-start.38 = (bf16[448,512]{1,0:T(8,128)(2,1)S(1)}, bf16[448,512]{1,0:T(8,128)(2,1)S(1)}, u32[]{:S(2)}, u32[]{:S(2)}) collective-permute-start(bf16[448,512]{1,0:T(8,128)(2,1)S(1)} %constant_dynamic-update-slice_fusion.4.refs_3_.refs_1_), channel_id=1, source_target_pairs={{0,8},{8,0},{16,24},{24,16},{1,9},{9,1},{17,25},{25,17},{2,10},{10... | collective-permute-start | bytes 1376264 | tf_op jit(solution)/shard_map/ppermute | solution.py:424
  182.6 7.0 %collective-permute-start.39 = (bf16[448,512]{1,0:T(8,128)(2,1)S(1)}, bf16[448,512]{1,0:T(8,128)(2,1)S(1)}, u32[]{:S(2)}, u32[]{:S(2)}) collective-permute-start(bf16[448,512]{1,0:T(8,128)(2,1)S(1)} %collective-permute-done.37.refs_4_.refs_2_), channel_id=1, source_target_pairs={{0,8},{8,0},{16,24},{24,16},{1,9},{9,1},{17,25},{25,17},{2,10},{10... | collective-permute-start | bytes 1376264 | tf_op jit(solution)/shard_map/ppermute | solution.py:424
  189.3 10.3 %collective-permute-start.43 = (bf16[448,512]{1,0:T(8,128)(2,1)S(1)}, bf16[448,512]{1,0:T(8,128)(2,1)S(1)}, u32[]{:S(2)}, u32[]{:S(2)}) collective-permute-start(bf16[448,512]{1,0:T(8,128)(2,1)S(1)} %project.11), channel_id=1, source_target_pairs={{0,1},{1,0},{2,3},{3,2},{4,5},{5,4},{6,7},{7,6},{8,9},{9,8},{10,11... | collective-permute-start | bytes 1376264 | tf_op jit(solution)/shard_map/ppermute | solution.py:418
  194.7 5.1 %copy-start.4 = (bf16[448,1024]{1,0:T(8,128)(2,1)S(1)}, bf16[448,1024]{1,0:T(8,128)(2,1)}, u32[]{:S(2)}) copy-start(bf16[448,1024]{1,0:T(8,128)(2,1)} %tokens.1) | copy-start | bytes 2752516
  194.7 5.1 %copy-start.21 = (f32[1024]{0:T(1024)S(1)}, f32[1024]{0:T(1024)}, u32[]{:S(2)}) copy-start(f32[1024]{0:T(1024)} %param.17) | copy-start | bytes 12292
  (2 other events, 1.6 us)

commit v2 on v1

--- a/solution.py
+++ b/solution.py
@@ -15,6 +15,7 @@
 POSITIONS = 32
 MIB = 1024 * 1024
 STAT_ROWS = 16
+URGENT = 20 * 10**9
 LIGHT = 100
 
 
@@ -363,7 +364,7 @@
         out[:, start:end] = total.astype(out.dtype)
 
 
-def project(slots, first, weights, parts, earlier, kind, left=0):
+def project(slots, first, weights, parts, earlier, kind, left=0, urgent=0):
     pieces = len(weights)
     width = weights[0].shape[1]
     depth = sum(piece.shape[0] for piece in weights)
@@ -385,7 +386,7 @@
         ],
         compiler_params=pltpu.CompilerParams(vmem_limit_bytes=32 * MIB),
         cost_estimate=pl.CostEstimate(
-            flops=2 * count * depth * width,
+            flops=2 * count * depth * width + urgent,
             bytes_accessed=2 * (depth * (width + count) + 2 * count * width),
             transcendentals=0,
         ),
@@ -598,13 +599,17 @@
     others = cross(jnp.concatenate(both[:lines], axis=1))
     *both, w_left, w_last = hold(*others, *both[lines:], w_left, w_last)
     others, own_outs = both[:3], ring_out(both[3:])
-    w_right = by_z(w_last[:, left:])
     others = [*others, by_core(others[1])]
     other = project(heads, 0, w_ring, others, None, F32)
-    crossed = by_y(project(heads, lines - 1, [w_left], others, other, BF))
+    other_left = project(heads, lines - 1, [w_left], others, other, BF)
+    *own_outs, other_left, w_last = hold(*own_outs, other_left, w_last)
+    w_right = by_z(w_last[:, left:])
+    crossed = by_y(other_left)
     owns = cross(jnp.concatenate(own_outs, axis=1))
     crossed, w_right = hold(crossed, w_right)
-    crossed_right = by_y(project(heads, lines - 1, [w_right], others, other, BF, left))
+    crossed_right = by_y(
+        project(heads, lines - 1, [w_right], others, other, BF, left, URGENT)
+    )
     owns = [*owns, by_core(owns[1])]
     own = project(heads, 0, w_ring, owns, None, F32)
     own_left = project(heads, lines - 1, [w_left], owns, own, F32)

time: 202 us -> 201 us (level)
    ppermute x10, waiting for transfers between devices: 22.9 us -> 27.3 us  [by_x(): return lax.ppermute(value, 'row', x_swap)]
    ppermute x8, waiting for transfers between devices: 19.4 us -> 16.5 us  [by_z(): return lax.ppermute(value, 'col', z_next)]
    ppermute x6, waiting for transfers between devices: 11.9 us -> 9.8 us  [ring_out(): lax.ppermute(outs[i], 'col', ringed[i])]
  transfers between devices with their start and end apart: 44 -> 44, of which waited for: 21 -> 19; matrix products, arithmetic and copies ran while one was open for 6% -> 6% of each run, Pallas kernels for 33% -> 34%
where the time goes in v2:
time: 201 us
  Pallas kernels  67.4 us (34%)
  waiting for transfers between devices  64.9 us (32%)
  starting transfers between devices  40.8 us (20%)
  local copies, waits for them, and re-layouts  10.7 us (5%)
  other arithmetic  6.4 us (3%)
  blocking collectives  6.33 us (3%)
  matrix products  3.5 us (2%)
    pallas_call x8, Pallas kernels, qkv(): pl.pallas_call(functools.partial(qkv_kernel, len(owns)), out_shape=(out,...  30.5 us
    ppermute x10, waiting for transfers between devices, by_x(): return lax.ppermute(value, 'row', x_swap)  27.3 us
    ppermute x8, waiting for transfers between devices, by_z(): return lax.ppermute(value, 'col', z_next)  16.5 us
    ppermute x10, starting transfers between devices, by_x(): return lax.ppermute(value, 'row', x_swap)  12.9 us
    ppermute x8, starting transfers between devices, by_z(): return lax.ppermute(value, 'col', z_next)  11.9 us
    pallas_call x2, Pallas kernels, attend(): pl.pallas_call(functools.partial(attend_kernel, tile, windows, group), ou...  11.8 us
    pallas_call x8, Pallas kernels, turn(): pl.pallas_call(functools.partial(turn_kernel, group, block), out_shape=ja...  11.3 us
    ppermute x7, waiting for transfers between devices, by_y(): return lax.ppermute(value, 'col', y_swap)  11.3 us
  transfers between devices with their start and end apart: 44, of which 19 were waited for; matrix products, arithmetic and copies ran while one was open for 6% of the time, Pallas kernels for 34%

profile of v2, /device:TPU:0, one launch (start us, length us, event | category | flops | bytes accessed | tf_op | source)
XLA Modules:
  0.0 200.7 jit_solution(3586540546598978986)
XLA Ops:
  0.0 4.0 %collective-permute-start = (bf16[448,1024]{1,0:T(8,128)(2,1)}, bf16[448,1024]{1,0:T(8,128)(2,1)S(1)}, u32[]{:S(2)}, u32[]{:S(2)}) collective-permute-start(bf16[448,1024]{1,0:T(8,128)(2,1)} %tokens.1), channel_id=1, source_target_pairs={{0,4},{1,5},{2,0},{3,1},{4,6},{5,7},{6,2},{7,3},{8,12},{9,13},{10,... | collective-permute-start | bytes 2752520 | tf_op jit(solution)/shard_map/ppermute | solution.py:422
  4.0 1.5 collective-permute-start.1
  5.6 1.6 convert_reduce_fusion
  7.1 6.3 %psum.7 = f32[2,448]{1,0:T(2,128)S(1)} all-reduce(f32[2,448]{1,0:T(2,128)S(1)} %pad_maximum_fusion.1), channel_id=1, replica_groups=mesh['row'=4,'col'=8] {'row'}, use_global_device_ids=true, to_apply=%region_2.3 | all-reduce | flops 896 | bytes 7168 | tf_op jit(solution)/shard_map/psum | solution.py:450
  13.5 1.6 collective-permute-start.2
  15.7 1.5 constant_dynamic-slice_fusion.2
  17.2 1.4 pad_maximum_fusion
  19.3 5.3 %collective-permute-done.2.stats = bf16[16,1024]{1,0:T(8,128)(2,1)S(1)} collective-permute-done((bf16[16,1024]{1,0:T(8,128)(2,1)S(1)}, bf16[16,1024]{1,0:T(8,128)(2,1)S(1)}, u32[]{:S(2)}, u32[]{:S(2)}) %collective-permute-start.2) | collective-permute-done | bytes 32800 | tf_op jit(solution)/shard_map/ppermute | solution.py:422
  24.6 2.2 %collective-permute-done.3.stats = bf16[16,1024]{1,0:T(8,128)(2,1)S(1)} collective-permute-done((bf16[16,1024]{1,0:T(8,128)(2,1)S(1)}, bf16[16,1024]{1,0:T(8,128)(2,1)S(1)}, u32[]{:S(2)}, u32[]{:S(2)}) %collective-permute-start.3) | collective-permute-done | bytes 32800 | tf_op jit(solution)/shard_map/ppermute | solution.py:419
  27.7 1.6 norm.4.refs_0_
  29.3 1.5 collective-permute-start.4
  30.8 1.6 collective-permute-start.5
  32.4 1.6 norm.5.refs_0_
  35.4 3.5 %fusion.2.table = f32[3584,256]{1,0:T(8,128)} fusion(pred[3584,32]{0,1:T(32,128)(4,1)S(1)} %get-tuple-element.220, pred[3584,32]{0,1:T(32,128)(4,1)S(1)} %get-tuple-element.221, f32[32,256]{1,0:T(8,128)S(1)} %concatenate.31, f32[32,256]{1,0:T(8,128)S(1)} %concatenate.30), kind=kOutput, calls=%fused_computation.9 | convolution fusion | flops 704888832 | bytes 3964928 | tf_op jit(solution)/shard_map/dot_general | solution.py:499
  38.9 1.2 copy-done.7
  40.0 3.7 %qkv.8 = (bf16[448,384]{1,0:T(8,128)(2,1)S(1)}, bf16[448,384]{1,0:T(8,128)(2,1)S(1)}) custom-call(s32[4]{0:T(128)S(1)} %pad_add_fusion.heads.slots, bf16[1024,1536]{1,0:T(8,128)(2,1)S(1)} %copy-done.2, bf16[1024,768]{1,0:T(8,128)(2,1)} %collective-permute-done.6.w_peer, bf16[448,1024]{1,0:T(8,128)(2,1)S(1)} %copy-done.7, ...), custom_call_target="tpu_custom_call" | custom-call | flops 14092861 | bytes 56688 | tf_op jit(solution)/shard_map/qkv/pallas_call | solution.py:189
  43.8 1.6 collective-permute-start.8
  46.3 4.0 %qkv.9 = (bf16[448,384]{1,0:T(8,128)(2,1)S(1)}, bf16[448,384]{1,0:T(8,128)(2,1)}) custom-call(s32[4]{0:T(128)S(1)} %pad_add_fusion.heads.slots, bf16[1024,1536]{1,0:T(8,128)(2,1)S(1)} %copy-done.2, bf16[1024,768]{1,0:T(8,128)(2,1)} %collective-permute-done.6.w_peer, bf16[448,1024]{1,0:T(8,128)(2,1)} %norm.4.refs_0_, ...), custom_call_target="tpu_custom_call" | custom-call | flops 14092861 | bytes 56688 | tf_op jit(solution)/shard_map/qkv/pallas_call | solution.py:189
  50.3 2.1 %collective-permute-done.4.refs_0_ = bf16[448,1024]{1,0:T(8,128)(2,1)} collective-permute-done((bf16[448,1024]{1,0:T(8,128)(2,1)}, bf16[448,1024]{1,0:T(8,128)(2,1)}, u32[]{:S(2)}, u32[]{:S(2)}) %collective-permute-start.4) | collective-permute-done | bytes 917536 | tf_op jit(solution)/shard_map/ppermute | solution.py:419
  52.4 1.2 collective-permute-done.5.refs_0_
  54.8 1.8 collective-permute-start.12
  57.1 4.0 %qkv.10 = (bf16[448,384]{1,0:T(8,128)(2,1)S(1)}, bf16[448,384]{1,0:T(8,128)(2,1)}) custom-call(s32[4]{0:T(128)S(1)} %pad_add_fusion.heads.slots, bf16[1024,1536]{1,0:T(8,128)(2,1)S(1)} %copy-done.2, bf16[1024,768]{1,0:T(8,128)(2,1)} %collective-permute-done.6.w_peer, bf16[448,1024]{1,0:T(8,128)(2,1)} %norm.5.refs_0_, ...), custom_call_target="tpu_custom_call" | custom-call | flops 14092861 | bytes 56688 | tf_op jit(solution)/shard_map/qkv/pallas_call | solution.py:189
  61.9 1.5 collective-permute-start.15
  65.5 2.0 %copy-done = f32[3584,256]{1,0:T(8,128)S(1)} copy-done((f32[3584,256]{1,0:T(8,128)S(1)}, f32[3584,256]{1,0:T(8,128)}, u32[]{:S(2)}) %copy-start) | copy-done | bytes 3670040
  69.5 1.3 turn.8.refs_0_
  70.8 3.7 %qkv.12 = (bf16[448,384]{1,0:T(8,128)(2,1)S(1)}, bf16[448,384]{1,0:T(8,128)(2,1)S(1)}) custom-call(s32[4]{0:T(128)S(1)} %pad_add_fusion.heads.slots, bf16[1024,1536]{1,0:T(8,128)(2,1)S(1)} %copy-done.2, bf16[1024,768]{1,0:T(8,128)(2,1)} %collective-permute-done.6.w_peer, bf16[448,1024]{1,0:T(8,128)(2,1)} %collective-permute-done.5.refs_0_, ...), custom_call_target="tpu_custom_call" | custom-call | flops 14092861 | bytes 56688 | tf_op jit(solution)/shard_map/qkv/pallas_call | solution.py:189
  74.6 4.1 %qkv.11 = (bf16[448,384]{1,0:T(8,128)(2,1)S(1)}, bf16[448,384]{1,0:T(8,128)(2,1)S(1)}) custom-call(s32[4]{0:T(128)S(1)} %pad_add_fusion.heads.slots, bf16[1024,1536]{1,0:T(8,128)(2,1)S(1)} %copy-done.2, bf16[1024,768]{1,0:T(8,128)(2,1)} %collective-permute-done.6.w_peer, bf16[448,1024]{1,0:T(8,128)(2,1)} %collective-permute-done.4.refs_0_, ...), custom_call_target="tpu_custom_call" | custom-call | flops 14092861 | bytes 56688 | tf_op jit(solution)/shard_map/qkv/pallas_call | solution.py:189
  81.4 1.5 collective-permute-start.19
  83.4 3.7 %qkv.13 = (bf16[448,384]{1,0:T(8,128)(2,1)S(1)}, bf16[448,384]{1,0:T(8,128)(2,1)S(1)}) custom-call(s32[4]{0:T(128)S(1)} %pad_add_fusion.heads.slots, bf16[1024,1536]{1,0:T(8,128)(2,1)S(1)} %copy-done.2, bf16[1024,768]{1,0:T(8,128)(2,1)} %collective-permute-done.6.w_peer, bf16[448,1024]{1,0:T(8,128)(2,1)} %collective-permute-done.12.refs_0_, ...), custom_call_target="tpu_custom_call" | custom-call | flops 14092861 | bytes 56688 | tf_op jit(solution)/shard_map/qkv/pallas_call | solution.py:189
  87.2 1.6 collective-permute-start.22
  88.8 1.8 turn.9.refs_0_
  90.5 1.8 turn.10.refs_0_
  92.3 3.7 %qkv.14 = (bf16[448,384]{1,0:T(8,128)(2,1)S(1)}, bf16[448,384]{1,0:T(8,128)(2,1)S(1)}) custom-call(s32[4]{0:T(128)S(1)} %pad_add_fusion.heads.slots, bf16[1024,1536]{1,0:T(8,128)(2,1)S(1)} %copy-done.2, bf16[1024,768]{1,0:T(8,128)(2,1)} %collective-permute-done.6.w_peer, bf16[448,1024]{1,0:T(8,128)(2,1)} %collective-permute-done.13.refs_0_, ...), custom_call_target="tpu_custom_call" | custom-call | flops 14092861 | bytes 56688 | tf_op jit(solution)/shard_map/qkv/pallas_call | solution.py:189
  96.0 8.7 %collective-permute-done.11.refs_1_ = bf16[512,1024]{1,0:T(8,128)(2,1)S(1)} collective-permute-done((bf16[512,1024]{1,0:T(8,128)(2,1)S(1)}, bf16[512,1024]{1,0:T(8,128)(2,1)S(1)}, u32[]{:S(2)}, u32[]{:S(2)}) %collective-permute-start.11) | collective-permute-done | bytes 1048608 | tf_op jit(solution)/shard_map/ppermute | solution.py:422
  105.6 1.4 collective-permute-start.27
  107.1 1.5 collective-permute-start.26
  108.6 3.5 %qkv.15 = (bf16[448,384]{1,0:T(8,128)(2,1)S(1)}, bf16[448,384]{1,0:T(8,128)(2,1)S(1)}) custom-call(s32[4]{0:T(128)S(1)} %pad_add_fusion.heads.slots, bf16[1024,1536]{1,0:T(8,128)(2,1)S(1)} %copy-done.2, bf16[1024,768]{1,0:T(8,128)(2,1)} %collective-permute-done.6.w_peer, bf16[448,1024]{1,0:T(8,128)(2,1)S(1)} %collective-permute-done.18.refs_0_, ...), custom_call_target="tpu_custom_call" | custom-call | flops 14092861 | bytes 56688 | tf_op jit(solution)/shard_map/qkv/pallas_call | solution.py:189
  113.9 1.3 turn.11.refs_0_
  115.2 1.3 turn.12.refs_0_
  116.5 1.3 turn.13.refs_0_
  118.0 1.3 turn.14.refs_0_
  119.3 5.2 %collective-permute-done.25.received = bf16[448,384]{1,0:T(8,128)(2,1)S(1)} collective-permute-done((bf16[448,384]{1,0:T(8,128)(2,1)S(1)}, bf16[448,384]{1,0:T(8,128)(2,1)S(1)}, u32[]{:S(2)}, u32[]{:S(2)}) %collective-permute-start.25) | collective-permute-done | bytes 344096 | tf_op jit(solution)/shard_map/ppermute | solution.py:428
  124.5 1.3 turn.15.rows
  125.8 5.9 %attend.2 = (bf16[448,128]{1,0:T(8,128)(2,1)S(1)}, bf16[448,128]{1,0:T(8,128)(2,1)S(1)}, bf16[448,128]{1,0:T(8,128)(2,1)S(1)}, bf16[448,128]{1,0:T(8,128)(2,1)S(1)}) custom-call(s32[16]{0:T(128)S(1)} %fusion.12.places, s32[16]{0:T(128)S(1)} %get-tuple-element.117.lows, s32[16]{0:T(128)S(1)} %get-tuple-element.118.sizes, f32[16,224]{1,0:T(8,128)S(1)} %reshape.16.seg_tiles, ...), custom_call_target="tpu_custom_call" | custom-call | flops 1056964608 | bytes 11927552 | tf_op jit(solution)/shard_map/attend/pallas_call | solution.py:312
  131.8 1.6 collective-permute-start.28
  133.4 2.8 %collective-permute-start.29 = (bf16[448,128]{1,0:T(8,128)(2,1)S(1)}, bf16[448,128]{1,0:T(8,128)(2,1)S(1)}, u32[]{:S(2)}, u32[]{:S(2)}) collective-permute-start(bf16[448,128]{1,0:T(8,128)(2,1)S(1)} %get-tuple-element.170), channel_id=1, source_target_pairs={{0,6},{1,7},{2,4},{3,5},{4,2},{5,3},{6,0},{7,1},{8,14},{9,15},{10,... | collective-permute-start | bytes 344072 | tf_op jit(solution)/shard_map/ppermute | solution.py:588
  136.2 5.9 %attend.3 = (bf16[448,128]{1,0:T(8,128)(2,1)S(1)}, bf16[448,128]{1,0:T(8,128)(2,1)S(1)}, bf16[448,128]{1,0:T(8,128)(2,1)S(1)}, bf16[448,128]{1,0:T(8,128)(2,1)S(1)}) custom-call(s32[16]{0:T(128)S(1)} %fusion.12.places, s32[16]{0:T(128)S(1)} %get-tuple-element.117.lows, s32[16]{0:T(128)S(1)} %get-tuple-element.118.sizes, f32[16,224]{1,0:T(8,128)S(1)} %reshape.16.seg_tiles, ...), custom_call_target="tpu_custom_call" | custom-call | flops 1056964608 | bytes 11927552 | tf_op jit(solution)/shard_map/attend/pallas_call | solution.py:312
  142.7 2.7 %collective-permute-done.30 = bf16[448,128]{1,0:T(8,128)(2,1)S(1)} collective-permute-done((bf16[448,128]{1,0:T(8,128)(2,1)S(1)}, bf16[448,128]{1,0:T(8,128)(2,1)S(1)}, u32[]{:S(2)}, u32[]{:S(2)}) %collective-permute-start.30) | collective-permute-done | bytes 114720 | tf_op jit(solution)/shard_map/ppermute | solution.py:588
  145.7 1.6 collective-permute-start.31
  147.3 10.0 %collective-permute-done.31.refs_4_.refs_2_ = bf16[448,512]{1,0:T(8,128)(2,1)S(1)} collective-permute-done((bf16[448,512]{1,0:T(8,128)(2,1)S(1)}, bf16[448,512]{1,0:T(8,128)(2,1)S(1)}, u32[]{:S(2)}, u32[]{:S(2)}) %collective-permute-start.31) | collective-permute-done | bytes 458784 | tf_op jit(solution)/shard_map/ppermute | solution.py:428
  157.3 1.2 collective-permute-done.33.refs_0_
  158.5 1.7 collective-permute-start.34
  160.2 2.1 %collective-permute-start.35 = (bf16[448,128]{1,0:T(8,128)(2,1)S(1)}, bf16[448,128]{1,0:T(8,128)(2,1)S(1)}, u32[]{:S(2)}, u32[]{:S(2)}) collective-permute-start(bf16[448,128]{1,0:T(8,128)(2,1)S(1)} %get-tuple-element.189), channel_id=1, source_target_pairs={{0,6},{1,7},{2,4},{3,5},{4,2},{5,3},{6,0},{7,1},{8,14},{9,15},{10,... | collective-permute-start | bytes 344072 | tf_op jit(solution)/shard_map/ppermute | solution.py:588
  162.2 2.8 %project.6.refs_5_ = f32[448,1024]{1,0:T(8,128)S(1)} custom-call(s32[4]{0:T(128)S(1)} %pad_add_fusion.heads.slots, bf16[512,1024]{1,0:T(8,128)(2,1)S(1)} %copy-done.5, bf16[512,1024]{1,0:T(8,128)(2,1)S(1)} %collective-permute-done.11.refs_1_, bf16[512,1024]{1,0:T(8,128)(2,1)S(1)} %collective-permute-done.27.refs_2_, ...), custom_call_target="tpu_custom_call" | custom-call | flops 1409286144 | bytes 6356992 | tf_op jit(solution)/shard_map/project/pallas_call | solution.py:374
  165.0 1.1 project.7
  166.1 2.5 %collective-permute-done.35 = bf16[448,128]{1,0:T(8,128)(2,1)S(1)} collective-permute-done((bf16[448,128]{1,0:T(8,128)(2,1)S(1)}, bf16[448,128]{1,0:T(8,128)(2,1)S(1)}, u32[]{:S(2)}, u32[]{:S(2)}) %collective-permute-start.35) | collective-permute-done | bytes 114720 | tf_op jit(solution)/shard_map/ppermute | solution.py:588
  168.7 4.0 %collective-permute-done.36 = bf16[448,128]{1,0:T(8,128)(2,1)S(1)} collective-permute-done((bf16[448,128]{1,0:T(8,128)(2,1)S(1)}, bf16[448,128]{1,0:T(8,128)(2,1)S(1)}, u32[]{:S(2)}, u32[]{:S(2)}) %collective-permute-start.36) | collective-permute-done | bytes 114720 | tf_op jit(solution)/shard_map/ppermute | solution.py:588
  173.1 1.6 collective-permute-start.38
  175.2 10.0 %collective-permute-done.38.refs_4_.refs_2_ = bf16[448,512]{1,0:T(8,128)(2,1)S(1)} collective-permute-done((bf16[448,512]{1,0:T(8,128)(2,1)S(1)}, bf16[448,512]{1,0:T(8,128)(2,1)S(1)}, u32[]{:S(2)}, u32[]{:S(2)}) %collective-permute-start.38) | collective-permute-done | bytes 458784 | tf_op jit(solution)/shard_map/ppermute | solution.py:428
  185.1 1.2 collective-permute-done.41
  188.3 2.8 %project.8.refs_5_ = f32[448,1024]{1,0:T(8,128)S(1)} custom-call(s32[4]{0:T(128)S(1)} %pad_add_fusion.heads.slots, bf16[512,1024]{1,0:T(8,128)(2,1)S(1)} %copy-done.5, bf16[512,1024]{1,0:T(8,128)(2,1)S(1)} %collective-permute-done.11.refs_1_, bf16[512,1024]{1,0:T(8,128)(2,1)S(1)} %collective-permute-done.27.refs_2_, ...), custom_call_target="tpu_custom_call" | custom-call | flops 1409286144 | bytes 6356992 | tf_op jit(solution)/shard_map/project/pallas_call | solution.py:374
  191.1 1.1 project.9
  193.5 5.8 %collective-permute-done.43 = bf16[448,512]{1,0:T(8,128)(2,1)S(1)} collective-permute-done((bf16[448,512]{1,0:T(8,128)(2,1)S(1)}, bf16[448,512]{1,0:T(8,128)(2,1)S(1)}, u32[]{:S(2)}, u32[]{:S(2)}) %collective-permute-start.43) | collective-permute-done | bytes 458784 | tf_op jit(solution)/shard_map/ppermute | solution.py:419
  199.4 1.2 fusion.1
  (133 shorter events, 22.3 us)
Async XLA Ops:
  0.0 26.8 %collective-permute-start = (bf16[448,1024]{1,0:T(8,128)(2,1)}, bf16[448,1024]{1,0:T(8,128)(2,1)S(1)}, u32[]{:S(2)}, u32[]{:S(2)}) collective-permute-start(bf16[448,1024]{1,0:T(8,128)(2,1)} %tokens.1), channel_id=1, source_target_pairs={{0,4},{1,5},{2,0},{3,1},{4,6},{5,7},{6,2},{7,3},{8,12},{9,13},{10,... | collective-permute-start | bytes 2752520 | tf_op jit(solution)/shard_map/ppermute | solution.py:422
  4.0 22.7 %collective-permute-start.1 = (bf16[448,1024]{1,0:T(8,128)(2,1)}, bf16[448,1024]{1,0:T(8,128)(2,1)S(1)}, u32[]{:S(2)}, u32[]{:S(2)}) collective-permute-start(bf16[448,1024]{1,0:T(8,128)(2,1)} %tokens.1), channel_id=1, source_target_pairs={{0,1},{1,0},{2,3},{3,2},{4,5},{5,4},{6,7},{7,6},{8,9},{9,8},{10,11... | collective-permute-start | bytes 2752520 | tf_op jit(solution)/shard_map/ppermute | solution.py:419
  13.5 11.0 %collective-permute-start.2 = (bf16[16,1024]{1,0:T(8,128)(2,1)S(1)}, bf16[16,1024]{1,0:T(8,128)(2,1)S(1)}, u32[]{:S(2)}, u32[]{:S(2)}) collective-permute-start(bf16[16,1024]{1,0:T(8,128)(2,1)S(1)} %pack.1.stats), channel_id=1, source_target_pairs={{0,4},{1,5},{2,0},{3,1},{4,6},{5,7},{6,2},{7,3},{8,12},{9,13},{10,... | collective-permute-start | bytes 98312 | tf_op jit(solution)/shard_map/ppermute | solution.py:422
  15.2 11.6 %collective-permute-start.3 = (bf16[16,1024]{1,0:T(8,128)(2,1)S(1)}, bf16[16,1024]{1,0:T(8,128)(2,1)S(1)}, u32[]{:S(2)}, u32[]{:S(2)}) collective-permute-start(bf16[16,1024]{1,0:T(8,128)(2,1)S(1)} %pack.1.stats), channel_id=1, source_target_pairs={{0,1},{1,0},{2,3},{3,2},{4,5},{5,4},{6,7},{7,6},{8,9},{9,8},{10,11... | collective-permute-start | bytes 98312 | tf_op jit(solution)/shard_map/ppermute | solution.py:419
  17.2 1.4 copy-start.3
  17.2 1.4 copy-start.16
  17.2 1.4 copy-start.17
  19.3 14.7 %copy-start.6 = (bf16[448,1024]{1,0:T(8,128)(2,1)}, bf16[448,1024]{1,0:T(8,128)(2,1)S(1)}, u32[]{:S(2)}) copy-start(bf16[448,1024]{1,0:T(8,128)(2,1)S(1)} %norm.3.refs_0_) | copy-start | bytes 2752516
  26.8 7.3 %collective-permute-start.7 = (bf16[448,1024]{1,0:T(8,128)(2,1)S(1)}, bf16[448,1024]{1,0:T(8,128)(2,1)}, u32[]{:S(2)}, u32[]{:S(2)}) collective-permute-start(bf16[448,1024]{1,0:T(8,128)(2,1)S(1)} %norm.3.refs_0_), channel_id=1, source_target_pairs={{0,8},{8,0},{16,24},{24,16},{1,9},{9,1},{17,25},{25,17},{2,10},{10... | collective-permute-start | bytes 2752520 | tf_op jit(solution)/shard_map/ppermute | solution.py:425
  26.9 12.0 %collective-permute-start.6 = (bf16[1024,768]{1,0:T(8,128)(2,1)}, bf16[1024,768]{1,0:T(8,128)(2,1)}, u32[]{:S(2)}, u32[]{:S(2)}) collective-permute-start(bf16[1024,768]{1,0:T(8,128)(2,1)} %pad_maximum_fusion), channel_id=1, source_target_pairs={{0,8},{8,0},{16,24},{24,16},{1,9},{9,1},{17,25},{25,17},{2,10},{10... | collective-permute-start | bytes 4718600 | tf_op jit(solution)/shard_map/ppermute | solution.py:425
  27.7 6.3 %copy-start.19 = (s32[2,3584]{1,0:T(2,128)S(1)}, s32[2,3584]{1,0:T(2,128)}, u32[]{:S(2)}) copy-start(s32[2,3584]{1,0:T(2,128)} %param.20) | copy-start | bytes 86020
  27.7 6.6 %copy-start.18 = (s32[3584]{0:T(1024)S(1)}, s32[3584]{0:T(1024)}, u32[]{:S(2)}) copy-start(s32[3584]{0:T(1024)} %param.18) | copy-start | bytes 43012
  27.7 6.6 %copy-start.20 = (s32[3584]{0:T(1024)S(1)}, s32[3584]{0:T(1024)}, u32[]{:S(2)}) copy-start(s32[3584]{0:T(1024)} %param.19) | copy-start | bytes 43012
  29.3 17.0 %collective-permute-start.10 = (bf16[448,1024]{1,0:T(8,128)(2,1)}, bf16[448,1024]{1,0:T(8,128)(2,1)}, u32[]{:S(2)}, u32[]{:S(2)}) collective-permute-start(bf16[448,1024]{1,0:T(8,128)(2,1)} %norm.4.refs_0_), channel_id=1, source_target_pairs={{0,8},{8,0},{16,24},{24,16},{1,9},{9,1},{17,25},{25,17},{2,10},{10... | collective-permute-start | bytes 2752520 | tf_op jit(solution)/shard_map/ppermute | solution.py:425
  29.3 23.1 %collective-permute-start.4 = (bf16[448,1024]{1,0:T(8,128)(2,1)}, bf16[448,1024]{1,0:T(8,128)(2,1)}, u32[]{:S(2)}, u32[]{:S(2)}) collective-permute-start(bf16[448,1024]{1,0:T(8,128)(2,1)} %norm.4.refs_0_), channel_id=1, source_target_pairs={{0,1},{1,0},{2,3},{3,2},{4,5},{5,4},{6,7},{7,6},{8,9},{9,8},{10,11... | collective-permute-start | bytes 2752520 | tf_op jit(solution)/shard_map/ppermute | solution.py:419
  30.8 22.8 %collective-permute-start.5 = (bf16[448,1024]{1,0:T(8,128)(2,1)}, bf16[448,1024]{1,0:T(8,128)(2,1)}, u32[]{:S(2)}, u32[]{:S(2)}) collective-permute-start(bf16[448,1024]{1,0:T(8,128)(2,1)} %norm.4.refs_0_), channel_id=1, source_target_pairs={{0,4},{1,5},{2,0},{3,1},{4,6},{5,7},{6,2},{7,3},{8,12},{9,13},{10,... | collective-permute-start | bytes 2752520 | tf_op jit(solution)/shard_map/ppermute | solution.py:422
  34.1 16.2 %collective-permute-start.9 = (bf16[448,1024]{1,0:T(8,128)(2,1)}, bf16[448,1024]{1,0:T(8,128)(2,1)}, u32[]{:S(2)}, u32[]{:S(2)}) collective-permute-start(bf16[448,1024]{1,0:T(8,128)(2,1)} %norm.5.refs_0_), channel_id=1, source_target_pairs={{0,8},{8,0},{16,24},{24,16},{1,9},{9,1},{17,25},{25,17},{2,10},{10... | collective-permute-start | bytes 2752520 | tf_op jit(solution)/shard_map/ppermute | solution.py:425
  35.3 3.5 %copy-start.2 = (bf16[1024,1536]{1,0:T(8,128)(2,1)S(1)}, bf16[1024,1536]{1,0:T(8,128)(2,1)}, u32[]{:S(2)}) copy-start(bf16[1024,1536]{1,0:T(8,128)(2,1)} %w_own.15) | copy-start | bytes 9437188
  38.9 1.2 copy-start.7
  43.8 6.5 %copy-start.12 = (bf16[448,384]{1,0:T(8,128)(2,1)}, bf16[448,384]{1,0:T(8,128)(2,1)S(1)}, u32[]{:S(2)}) copy-start(bf16[448,384]{1,0:T(8,128)(2,1)S(1)} %get-tuple-element.128.kept) | copy-start | bytes 1032196
  43.8 10.5 %collective-permute-start.8 = (bf16[448,384]{1,0:T(8,128)(2,1)S(1)}, bf16[448,384]{1,0:T(8,128)(2,1)S(1)}, u32[]{:S(2)}, u32[]{:S(2)}) collective-permute-start(bf16[448,384]{1,0:T(8,128)(2,1)S(1)} %get-tuple-element.109), channel_id=1, source_target_pairs={{0,16},{8,24},{16,0},{24,8},{1,17},{9,25},{17,1},{25,9},{2,18},{10... | collective-permute-start | bytes 1032200 | tf_op jit(solution)/shard_map/ppermute | solution.py:428
  54.3 6.8 %copy-start.14 = (bf16[448,384]{1,0:T(8,128)(2,1)}, bf16[448,384]{1,0:T(8,128)(2,1)S(1)}, u32[]{:S(2)}) copy-start(bf16[448,384]{1,0:T(8,128)(2,1)S(1)} %collective-permute-done.8.received) | copy-start | bytes 1032196
  54.3 9.0 %collective-permute-start.17 = (bf16[448,1024]{1,0:T(8,128)(2,1)}, bf16[448,1024]{1,0:T(8,128)(2,1)S(1)}, u32[]{:S(2)}, u32[]{:S(2)}) collective-permute-start(bf16[448,1024]{1,0:T(8,128)(2,1)} %collective-permute-done.5.refs_0_), channel_id=1, source_target_pairs={{0,8},{8,0},{16,24},{24,16},{1,9},{9,1},{17,25},{25,17},{2,10},{10... | collective-permute-start | bytes 2752520 | tf_op jit(solution)/shard_map/ppermute | solution.py:425
  54.3 20.3 %collective-permute-start.16 = (bf16[448,1024]{1,0:T(8,128)(2,1)}, bf16[448,1024]{1,0:T(8,128)(2,1)}, u32[]{:S(2)}, u32[]{:S(2)}) collective-permute-start(bf16[448,1024]{1,0:T(8,128)(2,1)} %collective-permute-done.4.refs_0_), channel_id=1, source_target_pairs={{0,8},{8,0},{16,24},{24,16},{1,9},{9,1},{17,25},{25,17},{2,10},{10... | collective-permute-start | bytes 2752520 | tf_op jit(solution)/shard_map/ppermute | solution.py:425
  54.8 24.2 %collective-permute-start.12 = (bf16[448,1024]{1,0:T(8,128)(2,1)}, bf16[448,1024]{1,0:T(8,128)(2,1)}, u32[]{:S(2)}, u32[]{:S(2)}) collective-permute-start(bf16[448,1024]{1,0:T(8,128)(2,1)} %collective-permute-done.5.refs_0_), channel_id=1, source_target_pairs={{0,4},{1,5},{2,0},{3,1},{4,6},{5,7},{6,2},{7,3},{8,12},{9,13},{10,... | collective-permute-start | bytes 2752520 | tf_op jit(solution)/shard_map/ppermute | solution.py:422
  56.6 22.4 %collective-permute-start.13 = (bf16[448,1024]{1,0:T(8,128)(2,1)}, bf16[448,1024]{1,0:T(8,128)(2,1)}, u32[]{:S(2)}, u32[]{:S(2)}) collective-permute-start(bf16[448,1024]{1,0:T(8,128)(2,1)} %collective-permute-done.5.refs_0_), channel_id=1, source_target_pairs={{0,1},{1,0},{2,3},{3,2},{4,5},{5,4},{6,7},{7,6},{8,9},{9,8},{10,11... | collective-permute-start | bytes 2752520 | tf_op jit(solution)/shard_map/ppermute | solution.py:419
  61.9 16.8 %collective-permute-start.15 = (bf16[448,384]{1,0:T(8,128)(2,1)}, bf16[448,384]{1,0:T(8,128)(2,1)}, u32[]{:S(2)}, u32[]{:S(2)}) collective-permute-start(bf16[448,384]{1,0:T(8,128)(2,1)} %get-tuple-element.127), channel_id=1, source_target_pairs={{0,16},{8,24},{16,0},{24,8},{1,17},{9,25},{17,1},{25,9},{2,18},{10... | collective-permute-start | bytes 1032200 | tf_op jit(solution)/shard_map/ppermute | solution.py:428
  64.3 14.7 %collective-permute-start.14 = (bf16[448,384]{1,0:T(8,128)(2,1)}, bf16[448,384]{1,0:T(8,128)(2,1)}, u32[]{:S(2)}, u32[]{:S(2)}) collective-permute-start(bf16[448,384]{1,0:T(8,128)(2,1)} %get-tuple-element.123), channel_id=1, source_target_pairs={{0,16},{8,24},{16,0},{24,8},{1,17},{9,25},{17,1},{25,9},{2,18},{10... | collective-permute-start | bytes 1032200 | tf_op jit(solution)/shard_map/ppermute | solution.py:428
  65.5 2.0 %copy-start = (f32[3584,256]{1,0:T(8,128)S(1)}, f32[3584,256]{1,0:T(8,128)}, u32[]{:S(2)}) copy-start(f32[3584,256]{1,0:T(8,128)} %fusion.2.table) | copy-start | bytes 11010052
  67.5 1.0 copy-start.13
  68.5 1.0 copy-start.15
  69.5 1.3 copy-start.9
  74.6 5.0 %copy-start.5 = (bf16[512,1024]{1,0:T(8,128)(2,1)S(1)}, bf16[512,1024]{1,0:T(8,128)(2,1)}, u32[]{:S(2)}) copy-start(bf16[512,1024]{1,0:T(8,128)(2,1)} %refs_0_.3) | copy-start | bytes 3145732
  79.0 9.7 %copy-start.1 = (f32[3584,256]{1,0:T(8,128)S(1)}, f32[3584,256]{1,0:T(8,128)}, u32[]{:S(2)}) copy-start(f32[3584,256]{1,0:T(8,128)} %fusion.2.table) | copy-start | bytes 11010052
  79.0 3.9 %collective-permute-start.21 = (bf16[448,1024]{1,0:T(8,128)(2,1)}, bf16[448,1024]{1,0:T(8,128)(2,1)S(1)}, u32[]{:S(2)}, u32[]{:S(2)}) collective-permute-start(bf16[448,1024]{1,0:T(8,128)(2,1)} %collective-permute-done.12.refs_0_), channel_id=1, source_target_pairs={{0,8},{8,0},{16,24},{24,16},{1,9},{9,1},{17,25},{25,17},{2,10},{10... | collective-permute-start | bytes 2752520 | tf_op jit(solution)/shard_map/ppermute | solution.py:425
  79.1 8.1 %collective-permute-start.23 = (bf16[448,1024]{1,0:T(8,128)(2,1)}, bf16[448,1024]{1,0:T(8,128)(2,1)S(1)}, u32[]{:S(2)}, u32[]{:S(2)}) collective-permute-start(bf16[448,1024]{1,0:T(8,128)(2,1)} %collective-permute-done.13.refs_0_), channel_id=1, source_target_pairs={{0,8},{8,0},{16,24},{24,16},{1,9},{9,1},{17,25},{25,17},{2,10},{10... | collective-permute-start | bytes 2752520 | tf_op jit(solution)/shard_map/ppermute | solution.py:425
  79.6 25.1 %collective-permute-start.11 = (bf16[512,1024]{1,0:T(8,128)(2,1)S(1)}, bf16[512,1024]{1,0:T(8,128)(2,1)S(1)}, u32[]{:S(2)}, u32[]{:S(2)}) collective-permute-start(bf16[512,1024]{1,0:T(8,128)(2,1)S(1)} %copy-done.5), channel_id=1, source_target_pairs={{0,4},{1,5},{2,0},{3,1},{4,6},{5,7},{6,2},{7,3},{8,12},{9,13},{10,... | collective-permute-start | bytes 3145736 | tf_op jit(solution)/shard_map/ppermute | solution.py:422
  80.7 24.1 %collective-permute-start.18 = (bf16[448,1024]{1,0:T(8,128)(2,1)}, bf16[448,1024]{1,0:T(8,128)(2,1)S(1)}, u32[]{:S(2)}, u32[]{:S(2)}) collective-permute-start(bf16[448,1024]{1,0:T(8,128)(2,1)} %collective-permute-done.12.refs_0_), channel_id=1, source_target_pairs={{0,1},{1,0},{2,3},{3,2},{4,5},{5,4},{6,7},{7,6},{8,9},{9,8},{10,11... | collective-permute-start | bytes 2752520 | tf_op jit(solution)/shard_map/ppermute | solution.py:419
  81.4 23.3 %collective-permute-start.19 = (bf16[448,384]{1,0:T(8,128)(2,1)S(1)}, bf16[448,384]{1,0:T(8,128)(2,1)S(1)}, u32[]{:S(2)}, u32[]{:S(2)}) collective-permute-start(bf16[448,384]{1,0:T(8,128)(2,1)S(1)} %get-tuple-element.138), channel_id=1, source_target_pairs={{0,16},{8,24},{16,0},{24,8},{1,17},{9,25},{17,1},{25,9},{2,18},{10... | collective-permute-start | bytes 1032200 | tf_op jit(solution)/shard_map/ppermute | solution.py:428
  82.9 21.9 %collective-permute-start.20 = (bf16[448,384]{1,0:T(8,128)(2,1)S(1)}, bf16[448,384]{1,0:T(8,128)(2,1)S(1)}, u32[]{:S(2)}, u32[]{:S(2)}) collective-permute-start(bf16[448,384]{1,0:T(8,128)(2,1)S(1)} %get-tuple-element.140), channel_id=1, source_target_pairs={{0,16},{8,24},{16,0},{24,8},{1,17},{9,25},{17,1},{25,9},{2,18},{10... | collective-permute-start | bytes 1032200 | tf_op jit(solution)/shard_map/ppermute | solution.py:428
  87.2 3.3 %copy-start.11 = (bf16[448,384]{1,0:T(8,128)(2,1)S(1)}, bf16[448,384]{1,0:T(8,128)(2,1)}, u32[]{:S(2)}) copy-start(bf16[448,384]{1,0:T(8,128)(2,1)} %copy-done.10) | copy-start | bytes 1032196
  87.2 18.4 %collective-permute-start.22 = (bf16[448,384]{1,0:T(8,128)(2,1)S(1)}, bf16[448,384]{1,0:T(8,128)(2,1)S(1)}, u32[]{:S(2)}, u32[]{:S(2)}) collective-permute-start(bf16[448,384]{1,0:T(8,128)(2,1)S(1)} %get-tuple-element.142), channel_id=1, source_target_pairs={{0,16},{8,24},{16,0},{24,8},{1,17},{9,25},{17,1},{25,9},{2,18},{10... | collective-permute-start | bytes 1032200 | tf_op jit(solution)/shard_map/ppermute | solution.py:428
  105.6 2.9 %collective-permute-start.24 = (bf16[448,1024]{1,0:T(8,128)(2,1)S(1)}, bf16[448,1024]{1,0:T(8,128)(2,1)S(1)}, u32[]{:S(2)}, u32[]{:S(2)}) collective-permute-start(bf16[448,1024]{1,0:T(8,128)(2,1)S(1)} %collective-permute-done.18.refs_0_), channel_id=1, source_target_pairs={{0,8},{8,0},{16,24},{24,16},{1,9},{9,1},{17,25},{25,17},{2,10},{10... | collective-permute-start | bytes 2752520 | tf_op jit(solution)/shard_map/ppermute | solution.py:425
  105.6 26.1 %collective-permute-start.27 = (bf16[512,1024]{1,0:T(8,128)(2,1)S(1)}, bf16[512,1024]{1,0:T(8,128)(2,1)S(1)}, u32[]{:S(2)}, u32[]{:S(2)}) collective-permute-start(bf16[512,1024]{1,0:T(8,128)(2,1)S(1)} %collective-permute-done.11.refs_1_), channel_id=1, source_target_pairs={{0,4},{1,5},{2,0},{3,1},{4,6},{5,7},{6,2},{7,3},{8,12},{9,13},{10,... | collective-permute-start | bytes 3145736 | tf_op jit(solution)/shard_map/ppermute | solution.py:422
  107.1 10.9 %collective-permute-start.26 = (bf16[448,384]{1,0:T(8,128)(2,1)S(1)}, bf16[448,384]{1,0:T(8,128)(2,1)S(1)}, u32[]{:S(2)}, u32[]{:S(2)}) collective-permute-start(bf16[448,384]{1,0:T(8,128)(2,1)S(1)} %get-tuple-element.155), channel_id=1, source_target_pairs={{0,16},{8,24},{16,0},{24,8},{1,17},{9,25},{17,1},{25,9},{2,18},{10... | collective-permute-start | bytes 1032200 | tf_op jit(solution)/shard_map/ppermute | solution.py:428
  112.1 12.4 %collective-permute-start.25 = (bf16[448,384]{1,0:T(8,128)(2,1)S(1)}, bf16[448,384]{1,0:T(8,128)(2,1)S(1)}, u32[]{:S(2)}, u32[]{:S(2)}) collective-permute-start(bf16[448,384]{1,0:T(8,128)(2,1)S(1)} %get-tuple-element.153), channel_id=1, source_target_pairs={{0,16},{8,24},{16,0},{24,8},{1,17},{9,25},{17,1},{25,9},{2,18},{10... | collective-permute-start | bytes 1032200 | tf_op jit(solution)/shard_map/ppermute | solution.py:428
  131.8 10.3 %collective-permute-start.28 = (bf16[448,128]{1,0:T(8,128)(2,1)S(1)}, bf16[448,128]{1,0:T(8,128)(2,1)S(1)}, u32[]{:S(2)}, u32[]{:S(2)}) collective-permute-start(bf16[448,128]{1,0:T(8,128)(2,1)S(1)} %get-tuple-element.169), channel_id=1, source_target_pairs={{0,4},{1,5},{2,0},{3,1},{4,6},{5,7},{6,2},{7,3},{8,12},{9,13},{10,... | collective-permute-start | bytes 344072 | tf_op jit(solution)/shard_map/ppermute | solution.py:588
  133.4 9.3 %collective-permute-start.29 = (bf16[448,128]{1,0:T(8,128)(2,1)S(1)}, bf16[448,128]{1,0:T(8,128)(2,1)S(1)}, u32[]{:S(2)}, u32[]{:S(2)}) collective-permute-start(bf16[448,128]{1,0:T(8,128)(2,1)S(1)} %get-tuple-element.170), channel_id=1, source_target_pairs={{0,6},{1,7},{2,4},{3,5},{4,2},{5,3},{6,0},{7,1},{8,14},{9,15},{10,... | collective-permute-start | bytes 344072 | tf_op jit(solution)/shard_map/ppermute | solution.py:588
  136.2 9.2 %collective-permute-start.30 = (bf16[448,128]{1,0:T(8,128)(2,1)S(1)}, bf16[448,128]{1,0:T(8,128)(2,1)S(1)}, u32[]{:S(2)}, u32[]{:S(2)}) collective-permute-start(bf16[448,128]{1,0:T(8,128)(2,1)S(1)} %get-tuple-element.171), channel_id=1, source_target_pairs={{0,2},{1,3},{2,6},{3,7},{4,0},{5,1},{6,4},{7,5},{8,10},{9,11},{10,... | collective-permute-start | bytes 344072 | tf_op jit(solution)/shard_map/ppermute | solution.py:588
  145.5 13.0 %collective-permute-start.33 = (bf16[512,512]{1,0:T(8,128)(2,1)S(1)}, bf16[512,512]{1,0:T(8,128)(2,1)S(1)}, u32[]{:S(2)}, u32[]{:S(2)}) collective-permute-start(bf16[512,512]{1,0:T(8,128)(2,1)S(1)} %slice.22), channel_id=1, source_target_pairs={{0,4},{1,5},{2,0},{3,1},{4,6},{5,7},{6,2},{7,3},{8,12},{9,13},{10,... | collective-permute-start | bytes 1572872 | tf_op jit(solution)/shard_map/ppermute | solution.py:422
  145.7 11.6 %collective-permute-start.31 = (bf16[448,512]{1,0:T(8,128)(2,1)S(1)}, bf16[448,512]{1,0:T(8,128)(2,1)S(1)}, u32[]{:S(2)}, u32[]{:S(2)}) collective-permute-start(bf16[448,512]{1,0:T(8,128)(2,1)S(1)} %constant_dynamic-update-slice_fusion.refs_3_.refs_1_), channel_id=1, source_target_pairs={{0,16},{8,24},{16,0},{24,8},{1,17},{9,25},{17,1},{25,9},{2,18},{10... | collective-permute-start | bytes 1376264 | tf_op jit(solution)/shard_map/ppermute | solution.py:428
  147.3 10.0 %collective-permute-start.32 = (bf16[448,512]{1,0:T(8,128)(2,1)S(1)}, bf16[448,512]{1,0:T(8,128)(2,1)S(1)}, u32[]{:S(2)}, u32[]{:S(2)}) collective-permute-start(bf16[448,512]{1,0:T(8,128)(2,1)S(1)} %constant_dynamic-update-slice_fusion.refs_3_.refs_1_), channel_id=1, source_target_pairs={{0,8},{8,0},{16,24},{24,16},{1,9},{9,1},{17,25},{25,17},{2,10},{10... | collective-permute-start | bytes 1376264 | tf_op jit(solution)/shard_map/ppermute | solution.py:425
  158.5 3.7 %collective-permute-start.37 = (bf16[448,512]{1,0:T(8,128)(2,1)S(1)}, bf16[448,512]{1,0:T(8,128)(2,1)S(1)}, u32[]{:S(2)}, u32[]{:S(2)}) collective-permute-start(bf16[448,512]{1,0:T(8,128)(2,1)S(1)} %collective-permute-done.31.refs_4_.refs_2_), channel_id=1, source_target_pairs={{0,8},{8,0},{16,24},{24,16},{1,9},{9,1},{17,25},{25,17},{2,10},{10... | collective-permute-start | bytes 1376264 | tf_op jit(solution)/shard_map/ppermute | solution.py:425
  158.5 7.6 %collective-permute-start.34 = (bf16[448,128]{1,0:T(8,128)(2,1)S(1)}, bf16[448,128]{1,0:T(8,128)(2,1)S(1)}, u32[]{:S(2)}, u32[]{:S(2)}) collective-permute-start(bf16[448,128]{1,0:T(8,128)(2,1)S(1)} %get-tuple-element.188), channel_id=1, source_target_pairs={{0,4},{1,5},{2,0},{3,1},{4,6},{5,7},{6,2},{7,3},{8,12},{9,13},{10,... | collective-permute-start | bytes 344072 | tf_op jit(solution)/shard_map/ppermute | solution.py:588
  160.2 8.5 %collective-permute-start.35 = (bf16[448,128]{1,0:T(8,128)(2,1)S(1)}, bf16[448,128]{1,0:T(8,128)(2,1)S(1)}, u32[]{:S(2)}, u32[]{:S(2)}) collective-permute-start(bf16[448,128]{1,0:T(8,128)(2,1)S(1)} %get-tuple-element.189), channel_id=1, source_target_pairs={{0,6},{1,7},{2,4},{3,5},{4,2},{5,3},{6,0},{7,1},{8,14},{9,15},{10,... | collective-permute-start | bytes 344072 | tf_op jit(solution)/shard_map/ppermute | solution.py:588
  162.2 10.4 %collective-permute-start.36 = (bf16[448,128]{1,0:T(8,128)(2,1)S(1)}, bf16[448,128]{1,0:T(8,128)(2,1)S(1)}, u32[]{:S(2)}, u32[]{:S(2)}) collective-permute-start(bf16[448,128]{1,0:T(8,128)(2,1)S(1)} %get-tuple-element.190), channel_id=1, source_target_pairs={{0,2},{1,3},{2,6},{3,7},{4,0},{5,1},{6,4},{7,5},{8,10},{9,11},{10,... | collective-permute-start | bytes 344072 | tf_op jit(solution)/shard_map/ppermute | solution.py:588
  172.7 13.7 %collective-permute-start.42 = (bf16[512,512]{1,0:T(8,128)(2,1)S(1)}, bf16[512,512]{1,0:T(8,128)(2,1)S(1)}, u32[]{:S(2)}, u32[]{:S(2)}) collective-permute-start(bf16[512,512]{1,0:T(8,128)(2,1)S(1)} %slice.23), channel_id=1, source_target_pairs={{0,4},{1,5},{2,0},{3,1},{4,6},{5,7},{6,2},{7,3},{8,12},{9,13},{10,... | collective-permute-start | bytes 1572872 | tf_op jit(solution)/shard_map/ppermute | solution.py:422
  173.1 12.0 %collective-permute-start.38 = (bf16[448,512]{1,0:T(8,128)(2,1)S(1)}, bf16[448,512]{1,0:T(8,128)(2,1)S(1)}, u32[]{:S(2)}, u32[]{:S(2)}) collective-permute-start(bf16[448,512]{1,0:T(8,128)(2,1)S(1)} %constant_dynamic-update-slice_fusion.4.refs_3_.refs_1_), channel_id=1, source_target_pairs={{0,16},{8,24},{16,0},{24,8},{1,17},{9,25},{17,1},{25,9},{2,18},{10... | collective-permute-start | bytes 1376264 | tf_op jit(solution)/shard_map/ppermute | solution.py:428
  174.7 11.7 %collective-permute-start.41 = (bf16[448,512]{1,0:T(8,128)(2,1)S(1)}, bf16[448,512]{1,0:T(8,128)(2,1)S(1)}, u32[]{:S(2)}, u32[]{:S(2)}) collective-permute-start(bf16[448,512]{1,0:T(8,128)(2,1)S(1)} %project.7), channel_id=1, source_target_pairs={{0,1},{1,0},{2,3},{3,2},{4,5},{5,4},{6,7},{7,6},{8,9},{9,8},{10,11... | collective-permute-start | bytes 1376264 | tf_op jit(solution)/shard_map/ppermute | solution.py:419
  175.2 13.1 %collective-permute-start.39 = (bf16[448,512]{1,0:T(8,128)(2,1)S(1)}, bf16[448,512]{1,0:T(8,128)(2,1)S(1)}, u32[]{:S(2)}, u32[]{:S(2)}) collective-permute-start(bf16[448,512]{1,0:T(8,128)(2,1)S(1)} %constant_dynamic-update-slice_fusion.4.refs_3_.refs_1_), channel_id=1, source_target_pairs={{0,8},{8,0},{16,24},{24,16},{1,9},{9,1},{17,25},{25,17},{2,10},{10... | collective-permute-start | bytes 1376264 | tf_op jit(solution)/shard_map/ppermute | solution.py:425
  185.1 3.2 %collective-permute-start.40 = (bf16[448,512]{1,0:T(8,128)(2,1)S(1)}, bf16[448,512]{1,0:T(8,128)(2,1)S(1)}, u32[]{:S(2)}, u32[]{:S(2)}) collective-permute-start(bf16[448,512]{1,0:T(8,128)(2,1)S(1)} %collective-permute-done.38.refs_4_.refs_2_), channel_id=1, source_target_pairs={{0,8},{8,0},{16,24},{24,16},{1,9},{9,1},{17,25},{25,17},{2,10},{10... | collective-permute-start | bytes 1376264 | tf_op jit(solution)/shard_map/ppermute | solution.py:425
  187.5 11.8 %collective-permute-start.43 = (bf16[448,512]{1,0:T(8,128)(2,1)S(1)}, bf16[448,512]{1,0:T(8,128)(2,1)S(1)}, u32[]{:S(2)}, u32[]{:S(2)}) collective-permute-start(bf16[448,512]{1,0:T(8,128)(2,1)S(1)} %project.11), channel_id=1, source_target_pairs={{0,1},{1,0},{2,3},{3,2},{4,5},{5,4},{6,7},{7,6},{8,9},{9,8},{10,11... | collective-permute-start | bytes 1376264 | tf_op jit(solution)/shard_map/ppermute | solution.py:419
  193.3 6.1 %copy-start.4 = (bf16[448,1024]{1,0:T(8,128)(2,1)S(1)}, bf16[448,1024]{1,0:T(8,128)(2,1)}, u32[]{:S(2)}) copy-start(bf16[448,1024]{1,0:T(8,128)(2,1)} %tokens.1) | copy-start | bytes 2752516
  193.3 6.1 %copy-start.21 = (f32[1024]{0:T(1024)S(1)}, f32[1024]{0:T(1024)}, u32[]{:S(2)}) copy-start(f32[1024]{0:T(1024)} %param.17) | copy-start | bytes 12292
  (2 other events, 1.6 us)

commit v3 on v2

--- a/solution.py
+++ b/solution.py
@@ -160,7 +160,7 @@
         out_specs=whole(),
         compiler_params=pltpu.CompilerParams(vmem_limit_bytes=16 * MIB),
         cost_estimate=pl.CostEstimate(
-            flops=4 * rows * width, bytes_accessed=4 * rows * width, transcendentals=0
+            flops=rows, bytes_accessed=rows, transcendentals=0
         ),
         name="norm",
     )(tokens, stats, gain[None, :], shift[None, :])
@@ -258,7 +258,7 @@
         ],
         compiler_params=pltpu.CompilerParams(vmem_limit_bytes=16 * MIB),
         cost_estimate=pl.CostEstimate(
-            flops=8 * rows * HD, bytes_accessed=26 * rows * HD, transcendentals=0
+            flops=rows, bytes_accessed=rows, transcendentals=0
         ),
         name="turn",
     )(*operands)

time: 201 us -> 201 us (level)
  transfers between devices with their start and end apart: 44 -> 44, of which waited for: 19 -> 19; matrix products, arithmetic and copies ran while one was open for 6% -> 6% of each run, Pallas kernels for 34% -> 33%
where the time goes in v3:
time: 201 us
  Pallas kernels  67.1 us (33%)
  waiting for transfers between devices  65 us (32%)
  starting transfers between devices  41 us (20%)
  local copies, waits for them, and re-layouts  10.7 us (5%)
  other arithmetic  6.4 us (3%)
  blocking collectives  6.33 us (3%)
  matrix products  3.5 us (2%)
    pallas_call x8, Pallas kernels, qkv(): pl.pallas_call(functools.partial(qkv_kernel, len(owns)), out_shape=(out,...  30.5 us
    ppermute x10, waiting for transfers between devices, by_x(): return lax.ppermute(value, 'row', x_swap)  27.3 us
    ppermute x8, waiting for transfers between devices, by_z(): return lax.ppermute(value, 'col', z_next)  16.5 us
    ppermute x10, starting transfers between devices, by_x(): return lax.ppermute(value, 'row', x_swap)  12.9 us
    ppermute x8, starting transfers between devices, by_z(): return lax.ppermute(value, 'col', z_next)  11.9 us
    pallas_call x2, Pallas kernels, attend(): pl.pallas_call(functools.partial(attend_kernel, tile, windows, group), ou...  11.5 us
    pallas_call x8, Pallas kernels, turn(): pl.pallas_call(functools.partial(turn_kernel, group, block), out_shape=ja...  11.3 us
    ppermute x7, waiting for transfers between devices, by_y(): return lax.ppermute(value, 'col', y_swap)  11.3 us
  transfers between devices with their start and end apart: 44, of which 19 were waited for; matrix products, arithmetic and copies ran while one was open for 6% of the time, Pallas kernels for 33%

profile of v3, /device:TPU:0, one launch (start us, length us, event | category | flops | bytes accessed | tf_op | source)
XLA Modules:
  0.0 200.7 jit_solution(3586540546598978986)
XLA Ops:
  0.0 4.0 %collective-permute-start = (bf16[448,1024]{1,0:T(8,128)(2,1)}, bf16[448,1024]{1,0:T(8,128)(2,1)S(1)}, u32[]{:S(2)}, u32[]{:S(2)}) collective-permute-start(bf16[448,1024]{1,0:T(8,128)(2,1)} %tokens.1), channel_id=1, source_target_pairs={{0,4},{1,5},{2,0},{3,1},{4,6},{5,7},{6,2},{7,3},{8,12},{9,13},{10,... | collective-permute-start | bytes 2752520 | tf_op jit(solution)/shard_map/ppermute | solution.py:422
  4.0 1.5 collective-permute-start.1
  5.6 1.6 convert_reduce_fusion
  7.1 6.3 %psum.7 = f32[2,448]{1,0:T(2,128)S(1)} all-reduce(f32[2,448]{1,0:T(2,128)S(1)} %pad_maximum_fusion.1), channel_id=1, replica_groups=mesh['row'=4,'col'=8] {'row'}, use_global_device_ids=true, to_apply=%region_2.3 | all-reduce | flops 896 | bytes 7168 | tf_op jit(solution)/shard_map/psum | solution.py:450
  13.5 1.6 collective-permute-start.2
  15.7 1.5 constant_dynamic-slice_fusion.2
  17.2 1.4 pad_maximum_fusion
  19.3 5.3 %collective-permute-done.2.stats = bf16[16,1024]{1,0:T(8,128)(2,1)S(1)} collective-permute-done((bf16[16,1024]{1,0:T(8,128)(2,1)S(1)}, bf16[16,1024]{1,0:T(8,128)(2,1)S(1)}, u32[]{:S(2)}, u32[]{:S(2)}) %collective-permute-start.2) | collective-permute-done | bytes 32800 | tf_op jit(solution)/shard_map/ppermute | solution.py:422
  24.6 2.2 %collective-permute-done.3.stats = bf16[16,1024]{1,0:T(8,128)(2,1)S(1)} collective-permute-done((bf16[16,1024]{1,0:T(8,128)(2,1)S(1)}, bf16[16,1024]{1,0:T(8,128)(2,1)S(1)}, u32[]{:S(2)}, u32[]{:S(2)}) %collective-permute-start.3) | collective-permute-done | bytes 32800 | tf_op jit(solution)/shard_map/ppermute | solution.py:419
  27.7 1.6 norm.4.refs_0_
  29.3 1.5 collective-permute-start.4
  30.8 1.6 collective-permute-start.5
  32.4 1.6 norm.5.refs_0_
  35.4 3.5 %fusion.2.table = f32[3584,256]{1,0:T(8,128)} fusion(pred[3584,32]{0,1:T(32,128)(4,1)S(1)} %get-tuple-element.220, pred[3584,32]{0,1:T(32,128)(4,1)S(1)} %get-tuple-element.221, f32[32,256]{1,0:T(8,128)S(1)} %concatenate.31, f32[32,256]{1,0:T(8,128)S(1)} %concatenate.30), kind=kOutput, calls=%fused_computation.9 | convolution fusion | flops 704888832 | bytes 3964928 | tf_op jit(solution)/shard_map/dot_general | solution.py:499
  38.9 1.2 copy-done.7
  40.0 3.7 %qkv.8 = (bf16[448,384]{1,0:T(8,128)(2,1)S(1)}, bf16[448,384]{1,0:T(8,128)(2,1)S(1)}) custom-call(s32[4]{0:T(128)S(1)} %pad_add_fusion.heads.slots, bf16[1024,1536]{1,0:T(8,128)(2,1)S(1)} %copy-done.2, bf16[1024,768]{1,0:T(8,128)(2,1)} %collective-permute-done.6.w_peer, bf16[448,1024]{1,0:T(8,128)(2,1)S(1)} %copy-done.7, ...), custom_call_target="tpu_custom_call" | custom-call | flops 14092861 | bytes 56688 | tf_op jit(solution)/shard_map/qkv/pallas_call | solution.py:189
  43.8 1.6 collective-permute-start.8
  46.3 4.0 %qkv.9 = (bf16[448,384]{1,0:T(8,128)(2,1)S(1)}, bf16[448,384]{1,0:T(8,128)(2,1)}) custom-call(s32[4]{0:T(128)S(1)} %pad_add_fusion.heads.slots, bf16[1024,1536]{1,0:T(8,128)(2,1)S(1)} %copy-done.2, bf16[1024,768]{1,0:T(8,128)(2,1)} %collective-permute-done.6.w_peer, bf16[448,1024]{1,0:T(8,128)(2,1)} %norm.4.refs_0_, ...), custom_call_target="tpu_custom_call" | custom-call | flops 14092861 | bytes 56688 | tf_op jit(solution)/shard_map/qkv/pallas_call | solution.py:189
  50.3 2.1 %collective-permute-done.4.refs_0_ = bf16[448,1024]{1,0:T(8,128)(2,1)} collective-permute-done((bf16[448,1024]{1,0:T(8,128)(2,1)}, bf16[448,1024]{1,0:T(8,128)(2,1)}, u32[]{:S(2)}, u32[]{:S(2)}) %collective-permute-start.4) | collective-permute-done | bytes 917536 | tf_op jit(solution)/shard_map/ppermute | solution.py:419
  52.4 1.2 collective-permute-done.5.refs_0_
  54.8 1.8 collective-permute-start.12
  57.1 4.0 %qkv.10 = (bf16[448,384]{1,0:T(8,128)(2,1)S(1)}, bf16[448,384]{1,0:T(8,128)(2,1)}) custom-call(s32[4]{0:T(128)S(1)} %pad_add_fusion.heads.slots, bf16[1024,1536]{1,0:T(8,128)(2,1)S(1)} %copy-done.2, bf16[1024,768]{1,0:T(8,128)(2,1)} %collective-permute-done.6.w_peer, bf16[448,1024]{1,0:T(8,128)(2,1)} %norm.5.refs_0_, ...), custom_call_target="tpu_custom_call" | custom-call | flops 14092861 | bytes 56688 | tf_op jit(solution)/shard_map/qkv/pallas_call | solution.py:189
  61.9 1.5 collective-permute-start.15
  65.5 2.0 %copy-done = f32[3584,256]{1,0:T(8,128)S(1)} copy-done((f32[3584,256]{1,0:T(8,128)S(1)}, f32[3584,256]{1,0:T(8,128)}, u32[]{:S(2)}) %copy-start) | copy-done | bytes 3670040
  69.5 1.3 turn.8.refs_0_
  70.8 3.7 %qkv.12 = (bf16[448,384]{1,0:T(8,128)(2,1)S(1)}, bf16[448,384]{1,0:T(8,128)(2,1)S(1)}) custom-call(s32[4]{0:T(128)S(1)} %pad_add_fusion.heads.slots, bf16[1024,1536]{1,0:T(8,128)(2,1)S(1)} %copy-done.2, bf16[1024,768]{1,0:T(8,128)(2,1)} %collective-permute-done.6.w_peer, bf16[448,1024]{1,0:T(8,128)(2,1)} %collective-permute-done.5.refs_0_, ...), custom_call_target="tpu_custom_call" | custom-call | flops 14092861 | bytes 56688 | tf_op jit(solution)/shard_map/qkv/pallas_call | solution.py:189
  74.6 4.1 %qkv.11 = (bf16[448,384]{1,0:T(8,128)(2,1)S(1)}, bf16[448,384]{1,0:T(8,128)(2,1)S(1)}) custom-call(s32[4]{0:T(128)S(1)} %pad_add_fusion.heads.slots, bf16[1024,1536]{1,0:T(8,128)(2,1)S(1)} %copy-done.2, bf16[1024,768]{1,0:T(8,128)(2,1)} %collective-permute-done.6.w_peer, bf16[448,1024]{1,0:T(8,128)(2,1)} %collective-permute-done.4.refs_0_, ...), custom_call_target="tpu_custom_call" | custom-call | flops 14092861 | bytes 56688 | tf_op jit(solution)/shard_map/qkv/pallas_call | solution.py:189
  81.4 1.5 collective-permute-start.19
  83.4 3.7 %qkv.13 = (bf16[448,384]{1,0:T(8,128)(2,1)S(1)}, bf16[448,384]{1,0:T(8,128)(2,1)S(1)}) custom-call(s32[4]{0:T(128)S(1)} %pad_add_fusion.heads.slots, bf16[1024,1536]{1,0:T(8,128)(2,1)S(1)} %copy-done.2, bf16[1024,768]{1,0:T(8,128)(2,1)} %collective-permute-done.6.w_peer, bf16[448,1024]{1,0:T(8,128)(2,1)} %collective-permute-done.12.refs_0_, ...), custom_call_target="tpu_custom_call" | custom-call | flops 14092861 | bytes 56688 | tf_op jit(solution)/shard_map/qkv/pallas_call | solution.py:189
  87.2 1.6 collective-permute-start.22
  88.8 1.8 turn.9.refs_0_
  90.5 1.8 turn.10.refs_0_
  92.3 3.7 %qkv.14 = (bf16[448,384]{1,0:T(8,128)(2,1)S(1)}, bf16[448,384]{1,0:T(8,128)(2,1)S(1)}) custom-call(s32[4]{0:T(128)S(1)} %pad_add_fusion.heads.slots, bf16[1024,1536]{1,0:T(8,128)(2,1)S(1)} %copy-done.2, bf16[1024,768]{1,0:T(8,128)(2,1)} %collective-permute-done.6.w_peer, bf16[448,1024]{1,0:T(8,128)(2,1)} %collective-permute-done.13.refs_0_, ...), custom_call_target="tpu_custom_call" | custom-call | flops 14092861 | bytes 56688 | tf_op jit(solution)/shard_map/qkv/pallas_call | solution.py:189
  96.0 8.7 %collective-permute-done.11.refs_1_ = bf16[512,1024]{1,0:T(8,128)(2,1)S(1)} collective-permute-done((bf16[512,1024]{1,0:T(8,128)(2,1)S(1)}, bf16[512,1024]{1,0:T(8,128)(2,1)S(1)}, u32[]{:S(2)}, u32[]{:S(2)}) %collective-permute-start.11) | collective-permute-done | bytes 1048608 | tf_op jit(solution)/shard_map/ppermute | solution.py:422
  105.6 1.4 collective-permute-start.27
  107.1 1.5 collective-permute-start.26
  108.6 3.5 %qkv.15 = (bf16[448,384]{1,0:T(8,128)(2,1)S(1)}, bf16[448,384]{1,0:T(8,128)(2,1)S(1)}) custom-call(s32[4]{0:T(128)S(1)} %pad_add_fusion.heads.slots, bf16[1024,1536]{1,0:T(8,128)(2,1)S(1)} %copy-done.2, bf16[1024,768]{1,0:T(8,128)(2,1)} %collective-permute-done.6.w_peer, bf16[448,1024]{1,0:T(8,128)(2,1)S(1)} %collective-permute-done.18.refs_0_, ...), custom_call_target="tpu_custom_call" | custom-call | flops 14092861 | bytes 56688 | tf_op jit(solution)/shard_map/qkv/pallas_call | solution.py:189
  113.9 1.3 turn.11.refs_0_
  115.2 1.3 turn.12.refs_0_
  116.5 1.3 turn.13.refs_0_
  118.0 1.3 turn.14.refs_0_
  119.3 5.2 %collective-permute-done.25.received = bf16[448,384]{1,0:T(8,128)(2,1)S(1)} collective-permute-done((bf16[448,384]{1,0:T(8,128)(2,1)S(1)}, bf16[448,384]{1,0:T(8,128)(2,1)S(1)}, u32[]{:S(2)}, u32[]{:S(2)}) %collective-permute-start.25) | collective-permute-done | bytes 344096 | tf_op jit(solution)/shard_map/ppermute | solution.py:428
  124.5 1.3 turn.15.rows
  125.8 5.7 %attend.2 = (bf16[448,128]{1,0:T(8,128)(2,1)S(1)}, bf16[448,128]{1,0:T(8,128)(2,1)S(1)}, bf16[448,128]{1,0:T(8,128)(2,1)S(1)}, bf16[448,128]{1,0:T(8,128)(2,1)S(1)}) custom-call(s32[16]{0:T(128)S(1)} %fusion.12.places, s32[16]{0:T(128)S(1)} %get-tuple-element.117.lows, s32[16]{0:T(128)S(1)} %get-tuple-element.118.sizes, f32[16,224]{1,0:T(8,128)S(1)} %reshape.16.seg_tiles, ...), custom_call_target="tpu_custom_call" | custom-call | flops 1056964608 | bytes 11927552 | tf_op jit(solution)/shard_map/attend/pallas_call | solution.py:312
  131.6 1.8 collective-permute-start.28
  133.4 2.8 %collective-permute-start.29 = (bf16[448,128]{1,0:T(8,128)(2,1)S(1)}, bf16[448,128]{1,0:T(8,128)(2,1)S(1)}, u32[]{:S(2)}, u32[]{:S(2)}) collective-permute-start(bf16[448,128]{1,0:T(8,128)(2,1)S(1)} %get-tuple-element.170), channel_id=1, source_target_pairs={{0,6},{1,7},{2,4},{3,5},{4,2},{5,3},{6,0},{7,1},{8,14},{9,15},{10,... | collective-permute-start | bytes 344072 | tf_op jit(solution)/shard_map/ppermute | solution.py:588
  136.2 5.8 %attend.3 = (bf16[448,128]{1,0:T(8,128)(2,1)S(1)}, bf16[448,128]{1,0:T(8,128)(2,1)S(1)}, bf16[448,128]{1,0:T(8,128)(2,1)S(1)}, bf16[448,128]{1,0:T(8,128)(2,1)S(1)}) custom-call(s32[16]{0:T(128)S(1)} %fusion.12.places, s32[16]{0:T(128)S(1)} %get-tuple-element.117.lows, s32[16]{0:T(128)S(1)} %get-tuple-element.118.sizes, f32[16,224]{1,0:T(8,128)S(1)} %reshape.16.seg_tiles, ...), custom_call_target="tpu_custom_call" | custom-call | flops 1056964608 | bytes 11927552 | tf_op jit(solution)/shard_map/attend/pallas_call | solution.py:312
  142.7 2.7 %collective-permute-done.30 = bf16[448,128]{1,0:T(8,128)(2,1)S(1)} collective-permute-done((bf16[448,128]{1,0:T(8,128)(2,1)S(1)}, bf16[448,128]{1,0:T(8,128)(2,1)S(1)}, u32[]{:S(2)}, u32[]{:S(2)}) %collective-permute-start.30) | collective-permute-done | bytes 114720 | tf_op jit(solution)/shard_map/ppermute | solution.py:588
  145.7 1.6 collective-permute-start.31
  147.3 10.0 %collective-permute-done.31.refs_4_.refs_2_ = bf16[448,512]{1,0:T(8,128)(2,1)S(1)} collective-permute-done((bf16[448,512]{1,0:T(8,128)(2,1)S(1)}, bf16[448,512]{1,0:T(8,128)(2,1)S(1)}, u32[]{:S(2)}, u32[]{:S(2)}) %collective-permute-start.31) | collective-permute-done | bytes 458784 | tf_op jit(solution)/shard_map/ppermute | solution.py:428
  157.3 1.2 collective-permute-done.33.refs_0_
  158.5 1.7 collective-permute-start.34
  160.2 2.1 %collective-permute-start.35 = (bf16[448,128]{1,0:T(8,128)(2,1)S(1)}, bf16[448,128]{1,0:T(8,128)(2,1)S(1)}, u32[]{:S(2)}, u32[]{:S(2)}) collective-permute-start(bf16[448,128]{1,0:T(8,128)(2,1)S(1)} %get-tuple-element.189), channel_id=1, source_target_pairs={{0,6},{1,7},{2,4},{3,5},{4,2},{5,3},{6,0},{7,1},{8,14},{9,15},{10,... | collective-permute-start | bytes 344072 | tf_op jit(solution)/shard_map/ppermute | solution.py:588
  162.2 2.8 %project.6.refs_5_ = f32[448,1024]{1,0:T(8,128)S(1)} custom-call(s32[4]{0:T(128)S(1)} %pad_add_fusion.heads.slots, bf16[512,1024]{1,0:T(8,128)(2,1)S(1)} %copy-done.5, bf16[512,1024]{1,0:T(8,128)(2,1)S(1)} %collective-permute-done.11.refs_1_, bf16[512,1024]{1,0:T(8,128)(2,1)S(1)} %collective-permute-done.27.refs_2_, ...), custom_call_target="tpu_custom_call" | custom-call | flops 1409286144 | bytes 6356992 | tf_op jit(solution)/shard_map/project/pallas_call | solution.py:374
  165.0 1.1 project.7
  166.1 2.5 %collective-permute-done.35 = bf16[448,128]{1,0:T(8,128)(2,1)S(1)} collective-permute-done((bf16[448,128]{1,0:T(8,128)(2,1)S(1)}, bf16[448,128]{1,0:T(8,128)(2,1)S(1)}, u32[]{:S(2)}, u32[]{:S(2)}) %collective-permute-start.35) | collective-permute-done | bytes 114720 | tf_op jit(solution)/shard_map/ppermute | solution.py:588
  168.7 4.0 %collective-permute-done.36 = bf16[448,128]{1,0:T(8,128)(2,1)S(1)} collective-permute-done((bf16[448,128]{1,0:T(8,128)(2,1)S(1)}, bf16[448,128]{1,0:T(8,128)(2,1)S(1)}, u32[]{:S(2)}, u32[]{:S(2)}) %collective-permute-start.36) | collective-permute-done | bytes 114720 | tf_op jit(solution)/shard_map/ppermute | solution.py:588
  173.1 1.6 collective-permute-start.38
  175.2 10.0 %collective-permute-done.38.refs_4_.refs_2_ = bf16[448,512]{1,0:T(8,128)(2,1)S(1)} collective-permute-done((bf16[448,512]{1,0:T(8,128)(2,1)S(1)}, bf16[448,512]{1,0:T(8,128)(2,1)S(1)}, u32[]{:S(2)}, u32[]{:S(2)}) %collective-permute-start.38) | collective-permute-done | bytes 458784 | tf_op jit(solution)/shard_map/ppermute | solution.py:428
  185.1 1.2 collective-permute-done.41
  188.3 2.8 %project.8.refs_5_ = f32[448,1024]{1,0:T(8,128)S(1)} custom-call(s32[4]{0:T(128)S(1)} %pad_add_fusion.heads.slots, bf16[512,1024]{1,0:T(8,128)(2,1)S(1)} %copy-done.5, bf16[512,1024]{1,0:T(8,128)(2,1)S(1)} %collective-permute-done.11.refs_1_, bf16[512,1024]{1,0:T(8,128)(2,1)S(1)} %collective-permute-done.27.refs_2_, ...), custom_call_target="tpu_custom_call" | custom-call | flops 1409286144 | bytes 6356992 | tf_op jit(solution)/shard_map/project/pallas_call | solution.py:374
  191.1 1.1 project.9
  193.5 5.8 %collective-permute-done.43 = bf16[448,512]{1,0:T(8,128)(2,1)S(1)} collective-permute-done((bf16[448,512]{1,0:T(8,128)(2,1)S(1)}, bf16[448,512]{1,0:T(8,128)(2,1)S(1)}, u32[]{:S(2)}, u32[]{:S(2)}) %collective-permute-start.43) | collective-permute-done | bytes 458784 | tf_op jit(solution)/shard_map/ppermute | solution.py:419
  199.4 1.2 fusion.1
  (133 shorter events, 22.4 us)
Async XLA Ops:
  0.0 26.8 %collective-permute-start = (bf16[448,1024]{1,0:T(8,128)(2,1)}, bf16[448,1024]{1,0:T(8,128)(2,1)S(1)}, u32[]{:S(2)}, u32[]{:S(2)}) collective-permute-start(bf16[448,1024]{1,0:T(8,128)(2,1)} %tokens.1), channel_id=1, source_target_pairs={{0,4},{1,5},{2,0},{3,1},{4,6},{5,7},{6,2},{7,3},{8,12},{9,13},{10,... | collective-permute-start | bytes 2752520 | tf_op jit(solution)/shard_map/ppermute | solution.py:422
  4.0 22.7 %collective-permute-start.1 = (bf16[448,1024]{1,0:T(8,128)(2,1)}, bf16[448,1024]{1,0:T(8,128)(2,1)S(1)}, u32[]{:S(2)}, u32[]{:S(2)}) collective-permute-start(bf16[448,1024]{1,0:T(8,128)(2,1)} %tokens.1), channel_id=1, source_target_pairs={{0,1},{1,0},{2,3},{3,2},{4,5},{5,4},{6,7},{7,6},{8,9},{9,8},{10,11... | collective-permute-start | bytes 2752520 | tf_op jit(solution)/shard_map/ppermute | solution.py:419
  13.5 11.0 %collective-permute-start.2 = (bf16[16,1024]{1,0:T(8,128)(2,1)S(1)}, bf16[16,1024]{1,0:T(8,128)(2,1)S(1)}, u32[]{:S(2)}, u32[]{:S(2)}) collective-permute-start(bf16[16,1024]{1,0:T(8,128)(2,1)S(1)} %pack.1.stats), channel_id=1, source_target_pairs={{0,4},{1,5},{2,0},{3,1},{4,6},{5,7},{6,2},{7,3},{8,12},{9,13},{10,... | collective-permute-start | bytes 98312 | tf_op jit(solution)/shard_map/ppermute | solution.py:422
  15.2 11.6 %collective-permute-start.3 = (bf16[16,1024]{1,0:T(8,128)(2,1)S(1)}, bf16[16,1024]{1,0:T(8,128)(2,1)S(1)}, u32[]{:S(2)}, u32[]{:S(2)}) collective-permute-start(bf16[16,1024]{1,0:T(8,128)(2,1)S(1)} %pack.1.stats), channel_id=1, source_target_pairs={{0,1},{1,0},{2,3},{3,2},{4,5},{5,4},{6,7},{7,6},{8,9},{9,8},{10,11... | collective-permute-start | bytes 98312 | tf_op jit(solution)/shard_map/ppermute | solution.py:419
  17.2 1.4 copy-start.3
  17.2 1.4 copy-start.16
  17.2 1.4 copy-start.17
  19.3 14.7 %copy-start.6 = (bf16[448,1024]{1,0:T(8,128)(2,1)}, bf16[448,1024]{1,0:T(8,128)(2,1)S(1)}, u32[]{:S(2)}) copy-start(bf16[448,1024]{1,0:T(8,128)(2,1)S(1)} %norm.3.refs_0_) | copy-start | bytes 2752516
  26.8 7.3 %collective-permute-start.7 = (bf16[448,1024]{1,0:T(8,128)(2,1)S(1)}, bf16[448,1024]{1,0:T(8,128)(2,1)}, u32[]{:S(2)}, u32[]{:S(2)}) collective-permute-start(bf16[448,1024]{1,0:T(8,128)(2,1)S(1)} %norm.3.refs_0_), channel_id=1, source_target_pairs={{0,8},{8,0},{16,24},{24,16},{1,9},{9,1},{17,25},{25,17},{2,10},{10... | collective-permute-start | bytes 2752520 | tf_op jit(solution)/shard_map/ppermute | solution.py:425
  26.9 12.0 %collective-permute-start.6 = (bf16[1024,768]{1,0:T(8,128)(2,1)}, bf16[1024,768]{1,0:T(8,128)(2,1)}, u32[]{:S(2)}, u32[]{:S(2)}) collective-permute-start(bf16[1024,768]{1,0:T(8,128)(2,1)} %pad_maximum_fusion), channel_id=1, source_target_pairs={{0,8},{8,0},{16,24},{24,16},{1,9},{9,1},{17,25},{25,17},{2,10},{10... | collective-permute-start | bytes 4718600 | tf_op jit(solution)/shard_map/ppermute | solution.py:425
  27.7 6.3 %copy-start.19 = (s32[2,3584]{1,0:T(2,128)S(1)}, s32[2,3584]{1,0:T(2,128)}, u32[]{:S(2)}) copy-start(s32[2,3584]{1,0:T(2,128)} %param.20) | copy-start | bytes 86020
  27.7 6.6 %copy-start.18 = (s32[3584]{0:T(1024)S(1)}, s32[3584]{0:T(1024)}, u32[]{:S(2)}) copy-start(s32[3584]{0:T(1024)} %param.18) | copy-start | bytes 43012
  27.7 6.6 %copy-start.20 = (s32[3584]{0:T(1024)S(1)}, s32[3584]{0:T(1024)}, u32[]{:S(2)}) copy-start(s32[3584]{0:T(1024)} %param.19) | copy-start | bytes 43012
  29.3 17.0 %collective-permute-start.10 = (bf16[448,1024]{1,0:T(8,128)(2,1)}, bf16[448,1024]{1,0:T(8,128)(2,1)}, u32[]{:S(2)}, u32[]{:S(2)}) collective-permute-start(bf16[448,1024]{1,0:T(8,128)(2,1)} %norm.4.refs_0_), channel_id=1, source_target_pairs={{0,8},{8,0},{16,24},{24,16},{1,9},{9,1},{17,25},{25,17},{2,10},{10... | collective-permute-start | bytes 2752520 | tf_op jit(solution)/shard_map/ppermute | solution.py:425
  29.3 23.1 %collective-permute-start.4 = (bf16[448,1024]{1,0:T(8,128)(2,1)}, bf16[448,1024]{1,0:T(8,128)(2,1)}, u32[]{:S(2)}, u32[]{:S(2)}) collective-permute-start(bf16[448,1024]{1,0:T(8,128)(2,1)} %norm.4.refs_0_), channel_id=1, source_target_pairs={{0,1},{1,0},{2,3},{3,2},{4,5},{5,4},{6,7},{7,6},{8,9},{9,8},{10,11... | collective-permute-start | bytes 2752520 | tf_op jit(solution)/shard_map/ppermute | solution.py:419
  30.8 22.8 %collective-permute-start.5 = (bf16[448,1024]{1,0:T(8,128)(2,1)}, bf16[448,1024]{1,0:T(8,128)(2,1)}, u32[]{:S(2)}, u32[]{:S(2)}) collective-permute-start(bf16[448,1024]{1,0:T(8,128)(2,1)} %norm.4.refs_0_), channel_id=1, source_target_pairs={{0,4},{1,5},{2,0},{3,1},{4,6},{5,7},{6,2},{7,3},{8,12},{9,13},{10,... | collective-permute-start | bytes 2752520 | tf_op jit(solution)/shard_map/ppermute | solution.py:422
  34.1 16.2 %collective-permute-start.9 = (bf16[448,1024]{1,0:T(8,128)(2,1)}, bf16[448,1024]{1,0:T(8,128)(2,1)}, u32[]{:S(2)}, u32[]{:S(2)}) collective-permute-start(bf16[448,1024]{1,0:T(8,128)(2,1)} %norm.5.refs_0_), channel_id=1, source_target_pairs={{0,8},{8,0},{16,24},{24,16},{1,9},{9,1},{17,25},{25,17},{2,10},{10... | collective-permute-start | bytes 2752520 | tf_op jit(solution)/shard_map/ppermute | solution.py:425
  35.3 3.5 %copy-start.2 = (bf16[1024,1536]{1,0:T(8,128)(2,1)S(1)}, bf16[1024,1536]{1,0:T(8,128)(2,1)}, u32[]{:S(2)}) copy-start(bf16[1024,1536]{1,0:T(8,128)(2,1)} %w_own.15) | copy-start | bytes 9437188
  38.9 1.2 copy-start.7
  43.8 6.5 %copy-start.12 = (bf16[448,384]{1,0:T(8,128)(2,1)}, bf16[448,384]{1,0:T(8,128)(2,1)S(1)}, u32[]{:S(2)}) copy-start(bf16[448,384]{1,0:T(8,128)(2,1)S(1)} %get-tuple-element.128.kept) | copy-start | bytes 1032196
  43.8 10.5 %collective-permute-start.8 = (bf16[448,384]{1,0:T(8,128)(2,1)S(1)}, bf16[448,384]{1,0:T(8,128)(2,1)S(1)}, u32[]{:S(2)}, u32[]{:S(2)}) collective-permute-start(bf16[448,384]{1,0:T(8,128)(2,1)S(1)} %get-tuple-element.109), channel_id=1, source_target_pairs={{0,16},{8,24},{16,0},{24,8},{1,17},{9,25},{17,1},{25,9},{2,18},{10... | collective-permute-start | bytes 1032200 | tf_op jit(solution)/shard_map/ppermute | solution.py:428
  54.3 6.8 %copy-start.14 = (bf16[448,384]{1,0:T(8,128)(2,1)}, bf16[448,384]{1,0:T(8,128)(2,1)S(1)}, u32[]{:S(2)}) copy-start(bf16[448,384]{1,0:T(8,128)(2,1)S(1)} %collective-permute-done.8.received) | copy-start | bytes 1032196
  54.3 9.0 %collective-permute-start.17 = (bf16[448,1024]{1,0:T(8,128)(2,1)}, bf16[448,1024]{1,0:T(8,128)(2,1)S(1)}, u32[]{:S(2)}, u32[]{:S(2)}) collective-permute-start(bf16[448,1024]{1,0:T(8,128)(2,1)} %collective-permute-done.5.refs_0_), channel_id=1, source_target_pairs={{0,8},{8,0},{16,24},{24,16},{1,9},{9,1},{17,25},{25,17},{2,10},{10... | collective-permute-start | bytes 2752520 | tf_op jit(solution)/shard_map/ppermute | solution.py:425
  54.3 20.3 %collective-permute-start.16 = (bf16[448,1024]{1,0:T(8,128)(2,1)}, bf16[448,1024]{1,0:T(8,128)(2,1)}, u32[]{:S(2)}, u32[]{:S(2)}) collective-permute-start(bf16[448,1024]{1,0:T(8,128)(2,1)} %collective-permute-done.4.refs_0_), channel_id=1, source_target_pairs={{0,8},{8,0},{16,24},{24,16},{1,9},{9,1},{17,25},{25,17},{2,10},{10... | collective-permute-start | bytes 2752520 | tf_op jit(solution)/shard_map/ppermute | solution.py:425
  54.8 24.2 %collective-permute-start.12 = (bf16[448,1024]{1,0:T(8,128)(2,1)}, bf16[448,1024]{1,0:T(8,128)(2,1)}, u32[]{:S(2)}, u32[]{:S(2)}) collective-permute-start(bf16[448,1024]{1,0:T(8,128)(2,1)} %collective-permute-done.5.refs_0_), channel_id=1, source_target_pairs={{0,4},{1,5},{2,0},{3,1},{4,6},{5,7},{6,2},{7,3},{8,12},{9,13},{10,... | collective-permute-start | bytes 2752520 | tf_op jit(solution)/shard_map/ppermute | solution.py:422
  56.6 22.4 %collective-permute-start.13 = (bf16[448,1024]{1,0:T(8,128)(2,1)}, bf16[448,1024]{1,0:T(8,128)(2,1)}, u32[]{:S(2)}, u32[]{:S(2)}) collective-permute-start(bf16[448,1024]{1,0:T(8,128)(2,1)} %collective-permute-done.5.refs_0_), channel_id=1, source_target_pairs={{0,1},{1,0},{2,3},{3,2},{4,5},{5,4},{6,7},{7,6},{8,9},{9,8},{10,11... | collective-permute-start | bytes 2752520 | tf_op jit(solution)/shard_map/ppermute | solution.py:419
  61.9 16.8 %collective-permute-start.15 = (bf16[448,384]{1,0:T(8,128)(2,1)}, bf16[448,384]{1,0:T(8,128)(2,1)}, u32[]{:S(2)}, u32[]{:S(2)}) collective-permute-start(bf16[448,384]{1,0:T(8,128)(2,1)} %get-tuple-element.127), channel_id=1, source_target_pairs={{0,16},{8,24},{16,0},{24,8},{1,17},{9,25},{17,1},{25,9},{2,18},{10... | collective-permute-start | bytes 1032200 | tf_op jit(solution)/shard_map/ppermute | solution.py:428
  64.3 14.7 %collective-permute-start.14 = (bf16[448,384]{1,0:T(8,128)(2,1)}, bf16[448,384]{1,0:T(8,128)(2,1)}, u32[]{:S(2)}, u32[]{:S(2)}) collective-permute-start(bf16[448,384]{1,0:T(8,128)(2,1)} %get-tuple-element.123), channel_id=1, source_target_pairs={{0,16},{8,24},{16,0},{24,8},{1,17},{9,25},{17,1},{25,9},{2,18},{10... | collective-permute-start | bytes 1032200 | tf_op jit(solution)/shard_map/ppermute | solution.py:428
  65.5 2.0 %copy-start = (f32[3584,256]{1,0:T(8,128)S(1)}, f32[3584,256]{1,0:T(8,128)}, u32[]{:S(2)}) copy-start(f32[3584,256]{1,0:T(8,128)} %fusion.2.table) | copy-start | bytes 11010052
  67.5 1.0 copy-start.13
  68.5 1.0 copy-start.15
  69.5 1.3 copy-start.9
  74.6 5.0 %copy-start.5 = (bf16[512,1024]{1,0:T(8,128)(2,1)S(1)}, bf16[512,1024]{1,0:T(8,128)(2,1)}, u32[]{:S(2)}) copy-start(bf16[512,1024]{1,0:T(8,128)(2,1)} %refs_0_.3) | copy-start | bytes 3145732
  79.0 9.7 %copy-start.1 = (f32[3584,256]{1,0:T(8,128)S(1)}, f32[3584,256]{1,0:T(8,128)}, u32[]{:S(2)}) copy-start(f32[3584,256]{1,0:T(8,128)} %fusion.2.table) | copy-start | bytes 11010052
  79.0 3.9 %collective-permute-start.21 = (bf16[448,1024]{1,0:T(8,128)(2,1)}, bf16[448,1024]{1,0:T(8,128)(2,1)S(1)}, u32[]{:S(2)}, u32[]{:S(2)}) collective-permute-start(bf16[448,1024]{1,0:T(8,128)(2,1)} %collective-permute-done.12.refs_0_), channel_id=1, source_target_pairs={{0,8},{8,0},{16,24},{24,16},{1,9},{9,1},{17,25},{25,17},{2,10},{10... | collective-permute-start | bytes 2752520 | tf_op jit(solution)/shard_map/ppermute | solution.py:425
  79.1 8.1 %collective-permute-start.23 = (bf16[448,1024]{1,0:T(8,128)(2,1)}, bf16[448,1024]{1,0:T(8,128)(2,1)S(1)}, u32[]{:S(2)}, u32[]{:S(2)}) collective-permute-start(bf16[448,1024]{1,0:T(8,128)(2,1)} %collective-permute-done.13.refs_0_), channel_id=1, source_target_pairs={{0,8},{8,0},{16,24},{24,16},{1,9},{9,1},{17,25},{25,17},{2,10},{10... | collective-permute-start | bytes 2752520 | tf_op jit(solution)/shard_map/ppermute | solution.py:425
  79.6 25.1 %collective-permute-start.11 = (bf16[512,1024]{1,0:T(8,128)(2,1)S(1)}, bf16[512,1024]{1,0:T(8,128)(2,1)S(1)}, u32[]{:S(2)}, u32[]{:S(2)}) collective-permute-start(bf16[512,1024]{1,0:T(8,128)(2,1)S(1)} %copy-done.5), channel_id=1, source_target_pairs={{0,4},{1,5},{2,0},{3,1},{4,6},{5,7},{6,2},{7,3},{8,12},{9,13},{10,... | collective-permute-start | bytes 3145736 | tf_op jit(solution)/shard_map/ppermute | solution.py:422
  80.7 24.1 %collective-permute-start.18 = (bf16[448,1024]{1,0:T(8,128)(2,1)}, bf16[448,1024]{1,0:T(8,128)(2,1)S(1)}, u32[]{:S(2)}, u32[]{:S(2)}) collective-permute-start(bf16[448,1024]{1,0:T(8,128)(2,1)} %collective-permute-done.12.refs_0_), channel_id=1, source_target_pairs={{0,1},{1,0},{2,3},{3,2},{4,5},{5,4},{6,7},{7,6},{8,9},{9,8},{10,11... | collective-permute-start | bytes 2752520 | tf_op jit(solution)/shard_map/ppermute | solution.py:419
  81.4 23.3 %collective-permute-start.19 = (bf16[448,384]{1,0:T(8,128)(2,1)S(1)}, bf16[448,384]{1,0:T(8,128)(2,1)S(1)}, u32[]{:S(2)}, u32[]{:S(2)}) collective-permute-start(bf16[448,384]{1,0:T(8,128)(2,1)S(1)} %get-tuple-element.138), channel_id=1, source_target_pairs={{0,16},{8,24},{16,0},{24,8},{1,17},{9,25},{17,1},{25,9},{2,18},{10... | collective-permute-start | bytes 1032200 | tf_op jit(solution)/shard_map/ppermute | solution.py:428
  82.9 21.9 %collective-permute-start.20 = (bf16[448,384]{1,0:T(8,128)(2,1)S(1)}, bf16[448,384]{1,0:T(8,128)(2,1)S(1)}, u32[]{:S(2)}, u32[]{:S(2)}) collective-permute-start(bf16[448,384]{1,0:T(8,128)(2,1)S(1)} %get-tuple-element.140), channel_id=1, source_target_pairs={{0,16},{8,24},{16,0},{24,8},{1,17},{9,25},{17,1},{25,9},{2,18},{10... | collective-permute-start | bytes 1032200 | tf_op jit(solution)/shard_map/ppermute | solution.py:428
  87.2 3.3 %copy-start.11 = (bf16[448,384]{1,0:T(8,128)(2,1)S(1)}, bf16[448,384]{1,0:T(8,128)(2,1)}, u32[]{:S(2)}) copy-start(bf16[448,384]{1,0:T(8,128)(2,1)} %copy-done.10) | copy-start | bytes 1032196
  87.2 18.4 %collective-permute-start.22 = (bf16[448,384]{1,0:T(8,128)(2,1)S(1)}, bf16[448,384]{1,0:T(8,128)(2,1)S(1)}, u32[]{:S(2)}, u32[]{:S(2)}) collective-permute-start(bf16[448,384]{1,0:T(8,128)(2,1)S(1)} %get-tuple-element.142), channel_id=1, source_target_pairs={{0,16},{8,24},{16,0},{24,8},{1,17},{9,25},{17,1},{25,9},{2,18},{10... | collective-permute-start | bytes 1032200 | tf_op jit(solution)/shard_map/ppermute | solution.py:428
  105.6 2.9 %collective-permute-start.24 = (bf16[448,1024]{1,0:T(8,128)(2,1)S(1)}, bf16[448,1024]{1,0:T(8,128)(2,1)S(1)}, u32[]{:S(2)}, u32[]{:S(2)}) collective-permute-start(bf16[448,1024]{1,0:T(8,128)(2,1)S(1)} %collective-permute-done.18.refs_0_), channel_id=1, source_target_pairs={{0,8},{8,0},{16,24},{24,16},{1,9},{9,1},{17,25},{25,17},{2,10},{10... | collective-permute-start | bytes 2752520 | tf_op jit(solution)/shard_map/ppermute | solution.py:425
  105.6 25.9 %collective-permute-start.27 = (bf16[512,1024]{1,0:T(8,128)(2,1)S(1)}, bf16[512,1024]{1,0:T(8,128)(2,1)S(1)}, u32[]{:S(2)}, u32[]{:S(2)}) collective-permute-start(bf16[512,1024]{1,0:T(8,128)(2,1)S(1)} %collective-permute-done.11.refs_1_), channel_id=1, source_target_pairs={{0,4},{1,5},{2,0},{3,1},{4,6},{5,7},{6,2},{7,3},{8,12},{9,13},{10,... | collective-permute-start | bytes 3145736 | tf_op jit(solution)/shard_map/ppermute | solution.py:422
  107.1 10.9 %collective-permute-start.26 = (bf16[448,384]{1,0:T(8,128)(2,1)S(1)}, bf16[448,384]{1,0:T(8,128)(2,1)S(1)}, u32[]{:S(2)}, u32[]{:S(2)}) collective-permute-start(bf16[448,384]{1,0:T(8,128)(2,1)S(1)} %get-tuple-element.155), channel_id=1, source_target_pairs={{0,16},{8,24},{16,0},{24,8},{1,17},{9,25},{17,1},{25,9},{2,18},{10... | collective-permute-start | bytes 1032200 | tf_op jit(solution)/shard_map/ppermute | solution.py:428
  112.1 12.4 %collective-permute-start.25 = (bf16[448,384]{1,0:T(8,128)(2,1)S(1)}, bf16[448,384]{1,0:T(8,128)(2,1)S(1)}, u32[]{:S(2)}, u32[]{:S(2)}) collective-permute-start(bf16[448,384]{1,0:T(8,128)(2,1)S(1)} %get-tuple-element.153), channel_id=1, source_target_pairs={{0,16},{8,24},{16,0},{24,8},{1,17},{9,25},{17,1},{25,9},{2,18},{10... | collective-permute-start | bytes 1032200 | tf_op jit(solution)/shard_map/ppermute | solution.py:428
  131.6 10.4 %collective-permute-start.28 = (bf16[448,128]{1,0:T(8,128)(2,1)S(1)}, bf16[448,128]{1,0:T(8,128)(2,1)S(1)}, u32[]{:S(2)}, u32[]{:S(2)}) collective-permute-start(bf16[448,128]{1,0:T(8,128)(2,1)S(1)} %get-tuple-element.169), channel_id=1, source_target_pairs={{0,4},{1,5},{2,0},{3,1},{4,6},{5,7},{6,2},{7,3},{8,12},{9,13},{10,... | collective-permute-start | bytes 344072 | tf_op jit(solution)/shard_map/ppermute | solution.py:588
  133.4 9.3 %collective-permute-start.29 = (bf16[448,128]{1,0:T(8,128)(2,1)S(1)}, bf16[448,128]{1,0:T(8,128)(2,1)S(1)}, u32[]{:S(2)}, u32[]{:S(2)}) collective-permute-start(bf16[448,128]{1,0:T(8,128)(2,1)S(1)} %get-tuple-element.170), channel_id=1, source_target_pairs={{0,6},{1,7},{2,4},{3,5},{4,2},{5,3},{6,0},{7,1},{8,14},{9,15},{10,... | collective-permute-start | bytes 344072 | tf_op jit(solution)/shard_map/ppermute | solution.py:588
  136.2 9.2 %collective-permute-start.30 = (bf16[448,128]{1,0:T(8,128)(2,1)S(1)}, bf16[448,128]{1,0:T(8,128)(2,1)S(1)}, u32[]{:S(2)}, u32[]{:S(2)}) collective-permute-start(bf16[448,128]{1,0:T(8,128)(2,1)S(1)} %get-tuple-element.171), channel_id=1, source_target_pairs={{0,2},{1,3},{2,6},{3,7},{4,0},{5,1},{6,4},{7,5},{8,10},{9,11},{10,... | collective-permute-start | bytes 344072 | tf_op jit(solution)/shard_map/ppermute | solution.py:588
  145.5 13.0 %collective-permute-start.33 = (bf16[512,512]{1,0:T(8,128)(2,1)S(1)}, bf16[512,512]{1,0:T(8,128)(2,1)S(1)}, u32[]{:S(2)}, u32[]{:S(2)}) collective-permute-start(bf16[512,512]{1,0:T(8,128)(2,1)S(1)} %slice.22), channel_id=1, source_target_pairs={{0,4},{1,5},{2,0},{3,1},{4,6},{5,7},{6,2},{7,3},{8,12},{9,13},{10,... | collective-permute-start | bytes 1572872 | tf_op jit(solution)/shard_map/ppermute | solution.py:422
  145.7 11.6 %collective-permute-start.31 = (bf16[448,512]{1,0:T(8,128)(2,1)S(1)}, bf16[448,512]{1,0:T(8,128)(2,1)S(1)}, u32[]{:S(2)}, u32[]{:S(2)}) collective-permute-start(bf16[448,512]{1,0:T(8,128)(2,1)S(1)} %constant_dynamic-update-slice_fusion.refs_3_.refs_1_), channel_id=1, source_target_pairs={{0,16},{8,24},{16,0},{24,8},{1,17},{9,25},{17,1},{25,9},{2,18},{10... | collective-permute-start | bytes 1376264 | tf_op jit(solution)/shard_map/ppermute | solution.py:428
  147.3 10.0 %collective-permute-start.32 = (bf16[448,512]{1,0:T(8,128)(2,1)S(1)}, bf16[448,512]{1,0:T(8,128)(2,1)S(1)}, u32[]{:S(2)}, u32[]{:S(2)}) collective-permute-start(bf16[448,512]{1,0:T(8,128)(2,1)S(1)} %constant_dynamic-update-slice_fusion.refs_3_.refs_1_), channel_id=1, source_target_pairs={{0,8},{8,0},{16,24},{24,16},{1,9},{9,1},{17,25},{25,17},{2,10},{10... | collective-permute-start | bytes 1376264 | tf_op jit(solution)/shard_map/ppermute | solution.py:425
  158.5 3.7 %collective-permute-start.37 = (bf16[448,512]{1,0:T(8,128)(2,1)S(1)}, bf16[448,512]{1,0:T(8,128)(2,1)S(1)}, u32[]{:S(2)}, u32[]{:S(2)}) collective-permute-start(bf16[448,512]{1,0:T(8,128)(2,1)S(1)} %collective-permute-done.31.refs_4_.refs_2_), channel_id=1, source_target_pairs={{0,8},{8,0},{16,24},{24,16},{1,9},{9,1},{17,25},{25,17},{2,10},{10... | collective-permute-start | bytes 1376264 | tf_op jit(solution)/shard_map/ppermute | solution.py:425
  158.5 7.6 %collective-permute-start.34 = (bf16[448,128]{1,0:T(8,128)(2,1)S(1)}, bf16[448,128]{1,0:T(8,128)(2,1)S(1)}, u32[]{:S(2)}, u32[]{:S(2)}) collective-permute-start(bf16[448,128]{1,0:T(8,128)(2,1)S(1)} %get-tuple-element.188), channel_id=1, source_target_pairs={{0,4},{1,5},{2,0},{3,1},{4,6},{5,7},{6,2},{7,3},{8,12},{9,13},{10,... | collective-permute-start | bytes 344072 | tf_op jit(solution)/shard_map/ppermute | solution.py:588
  160.2 8.5 %collective-permute-start.35 = (bf16[448,128]{1,0:T(8,128)(2,1)S(1)}, bf16[448,128]{1,0:T(8,128)(2,1)S(1)}, u32[]{:S(2)}, u32[]{:S(2)}) collective-permute-start(bf16[448,128]{1,0:T(8,128)(2,1)S(1)} %get-tuple-element.189), channel_id=1, source_target_pairs={{0,6},{1,7},{2,4},{3,5},{4,2},{5,3},{6,0},{7,1},{8,14},{9,15},{10,... | collective-permute-start | bytes 344072 | tf_op jit(solution)/shard_map/ppermute | solution.py:588
  162.2 10.4 %collective-permute-start.36 = (bf16[448,128]{1,0:T(8,128)(2,1)S(1)}, bf16[448,128]{1,0:T(8,128)(2,1)S(1)}, u32[]{:S(2)}, u32[]{:S(2)}) collective-permute-start(bf16[448,128]{1,0:T(8,128)(2,1)S(1)} %get-tuple-element.190), channel_id=1, source_target_pairs={{0,2},{1,3},{2,6},{3,7},{4,0},{5,1},{6,4},{7,5},{8,10},{9,11},{10,... | collective-permute-start | bytes 344072 | tf_op jit(solution)/shard_map/ppermute | solution.py:588
  172.7 13.7 %collective-permute-start.42 = (bf16[512,512]{1,0:T(8,128)(2,1)S(1)}, bf16[512,512]{1,0:T(8,128)(2,1)S(1)}, u32[]{:S(2)}, u32[]{:S(2)}) collective-permute-start(bf16[512,512]{1,0:T(8,128)(2,1)S(1)} %slice.23), channel_id=1, source_target_pairs={{0,4},{1,5},{2,0},{3,1},{4,6},{5,7},{6,2},{7,3},{8,12},{9,13},{10,... | collective-permute-start | bytes 1572872 | tf_op jit(solution)/shard_map/ppermute | solution.py:422
  173.1 12.0 %collective-permute-start.38 = (bf16[448,512]{1,0:T(8,128)(2,1)S(1)}, bf16[448,512]{1,0:T(8,128)(2,1)S(1)}, u32[]{:S(2)}, u32[]{:S(2)}) collective-permute-start(bf16[448,512]{1,0:T(8,128)(2,1)S(1)} %constant_dynamic-update-slice_fusion.4.refs_3_.refs_1_), channel_id=1, source_target_pairs={{0,16},{8,24},{16,0},{24,8},{1,17},{9,25},{17,1},{25,9},{2,18},{10... | collective-permute-start | bytes 1376264 | tf_op jit(solution)/shard_map/ppermute | solution.py:428
  174.7 11.7 %collective-permute-start.41 = (bf16[448,512]{1,0:T(8,128)(2,1)S(1)}, bf16[448,512]{1,0:T(8,128)(2,1)S(1)}, u32[]{:S(2)}, u32[]{:S(2)}) collective-permute-start(bf16[448,512]{1,0:T(8,128)(2,1)S(1)} %project.7), channel_id=1, source_target_pairs={{0,1},{1,0},{2,3},{3,2},{4,5},{5,4},{6,7},{7,6},{8,9},{9,8},{10,11... | collective-permute-start | bytes 1376264 | tf_op jit(solution)/shard_map/ppermute | solution.py:419
  175.2 13.1 %collective-permute-start.39 = (bf16[448,512]{1,0:T(8,128)(2,1)S(1)}, bf16[448,512]{1,0:T(8,128)(2,1)S(1)}, u32[]{:S(2)}, u32[]{:S(2)}) collective-permute-start(bf16[448,512]{1,0:T(8,128)(2,1)S(1)} %constant_dynamic-update-slice_fusion.4.refs_3_.refs_1_), channel_id=1, source_target_pairs={{0,8},{8,0},{16,24},{24,16},{1,9},{9,1},{17,25},{25,17},{2,10},{10... | collective-permute-start | bytes 1376264 | tf_op jit(solution)/shard_map/ppermute | solution.py:425
  185.1 3.2 %collective-permute-start.40 = (bf16[448,512]{1,0:T(8,128)(2,1)S(1)}, bf16[448,512]{1,0:T(8,128)(2,1)S(1)}, u32[]{:S(2)}, u32[]{:S(2)}) collective-permute-start(bf16[448,512]{1,0:T(8,128)(2,1)S(1)} %collective-permute-done.38.refs_4_.refs_2_), channel_id=1, source_target_pairs={{0,8},{8,0},{16,24},{24,16},{1,9},{9,1},{17,25},{25,17},{2,10},{10... | collective-permute-start | bytes 1376264 | tf_op jit(solution)/shard_map/ppermute | solution.py:425
  187.5 11.8 %collective-permute-start.43 = (bf16[448,512]{1,0:T(8,128)(2,1)S(1)}, bf16[448,512]{1,0:T(8,128)(2,1)S(1)}, u32[]{:S(2)}, u32[]{:S(2)}) collective-permute-start(bf16[448,512]{1,0:T(8,128)(2,1)S(1)} %project.11), channel_id=1, source_target_pairs={{0,1},{1,0},{2,3},{3,2},{4,5},{5,4},{6,7},{7,6},{8,9},{9,8},{10,11... | collective-permute-start | bytes 1376264 | tf_op jit(solution)/shard_map/ppermute | solution.py:419
  193.3 6.1 %copy-start.4 = (bf16[448,1024]{1,0:T(8,128)(2,1)S(1)}, bf16[448,1024]{1,0:T(8,128)(2,1)}, u32[]{:S(2)}) copy-start(bf16[448,1024]{1,0:T(8,128)(2,1)} %tokens.1) | copy-start | bytes 2752516
  193.3 6.1 %copy-start.21 = (f32[1024]{0:T(1024)S(1)}, f32[1024]{0:T(1024)}, u32[]{:S(2)}) copy-start(f32[1024]{0:T(1024)} %param.17) | copy-start | bytes 12292
  (2 other events, 1.6 us)
